TPU v7x, 256 devices: a whole 4x4x8 slice. The times are simulated.
256 devices in a mesh: blk: 128 (over x_hi, z, y, core), rep: 2 (over x_lo).
Axes of the slice: x: 4 (x_hi: 2, x_lo: 2; x = x_hi * 2 + x_lo), y: 4, z: 8, core: 2. Of those that a mesh axis runs over, the one named last changes fastest.
Arguments:
- activations: bfloat16 [256, 8192], P(('blk', 'rep')), may hold values from -6 to 6
- out_cotangent: bfloat16 [256, 8192], P(('blk', 'rep')), may hold values from -6 to 6
- gate_blocks: bfloat16 [256, 72, 4096], P('blk'), may hold values from -0.09375 to 0.09375
- up_blocks: bfloat16 [256, 72, 4096], P('blk'), may hold values from -0.09375 to 0.09375
- down_blocks: bfloat16 [256, 72, 4096], P('blk'), may hold values from -0.0625 to 0.0625
- block_index: int32 [3, 256, 72], P(None, 'blk'), may hold values from 0 to 127, as said below
- block_counts: int32 [3, 256], P(None, 'blk'), may hold values from 56 to 72, as said below
Outputs:
- layer_out: bfloat16 [256, 8192], P(('blk', 'rep'))
- input_grad: bfloat16 [256, 8192], P(('blk', 'rep'))
- gate_grad: float32 [256, 72, 4096], P('blk', 'rep')
- up_grad: float32 [256, 72, 4096], P('blk', 'rep')
- down_grad: float32 [256, 72, 4096], P('blk', 'rep')
Inputs may be any that keep to these rules, and one draw needn't show every extreme that they name: `block_index`: for each list the first block_counts entries are distinct model-width block numbers and the remaining entries are 0. `block_counts`: each of the three matrices has a list with exactly 72 live entries, at a hidden block drawn from the seed.
All inputs are finite; a program needn't handle non-finite values.
Results may differ from a plain program's by a relative error of at most 0.01.
Values may be sent and summed in bfloat16 or wider, within the bound.
No kernel may reach another device: no remote copies, remote signals or barrier semaphores. Data moves between devices by JAX's collectives and lax.ppermute only.
A program may use at most 128 MiB of HBM per device.

v0:
```python
import math

import jax
import jax.numpy as jnp
from jax import lax
from jax.sharding import PartitionSpec as P


def densify_inputs(blocks, select_half):
    col_count, list_length, square = blocks.shape
    block_side = math.isqrt(square)
    block_count = select_half.shape[2]
    squares = blocks.reshape(col_count, list_length, block_side, block_side)
    dense = jnp.einsum("fbn,fbij->nifj", select_half, squares, preferred_element_type=jnp.bfloat16)
    return dense.reshape(block_count * block_side, col_count * block_side)


def densify_outputs(blocks, select_half):
    col_count, list_length, square = blocks.shape
    block_side = math.isqrt(square)
    block_count = select_half.shape[2]
    squares = blocks.reshape(col_count, list_length, block_side, block_side)
    dense = jnp.einsum("fbn,fbjk->fjnk", select_half, squares, preferred_element_type=jnp.bfloat16)
    return dense.reshape(col_count * block_side, block_count * block_side)


def over_tokens(left, right):
    return lax.dot_general(
        left, right, (((0,), (0,)), ((), ())), preferred_element_type=jnp.float32
    )


def over_width(left, right):
    return lax.dot_general(
        left, right, (((1,), (1,)), ((), ())), preferred_element_type=jnp.float32
    )


def pick_blocks(dense_tiles, lists, live_float):
    picked = jnp.take_along_axis(dense_tiles, lists[:, :, None, None], axis=1)
    return picked * live_float[:, :, None, None]


def per_device(
    activations, out_cotangent, gate_blocks, up_blocks, down_blocks, block_index, block_counts
):
    col_count, list_length, square = gate_blocks.shape
    block_side = math.isqrt(square)
    model_width = activations.shape[1]
    block_count = model_width // block_side
    live_mask = jnp.arange(list_length)[None, None, :] < block_counts[:, :, None]
    live_float = live_mask.astype(jnp.float32)
    select_half = (
        (block_index[:, :, :, None] == jnp.arange(block_count)[None, None, None, :])
        & live_mask[:, :, :, None]
    ).astype(jnp.bfloat16)
    w_gate = densify_inputs(gate_blocks, select_half[0])
    w_up = densify_inputs(up_blocks, select_half[1])
    w_down = densify_outputs(down_blocks, select_half[2])
    inputs_all = lax.all_gather(activations, "blk", axis=0, tiled=True)
    gate = jnp.dot(inputs_all, w_gate, preferred_element_type=jnp.float32)
    upper = jnp.dot(inputs_all, w_up, preferred_element_type=jnp.float32)
    sigmoid_gate = jax.nn.sigmoid(gate)
    activation = gate * sigmoid_gate
    hidden = (activation * upper).astype(jnp.bfloat16)
    layer_out = lax.psum_scatter(
        jnp.dot(hidden, w_down, preferred_element_type=jnp.float32),
        "blk",
        scatter_dimension=0,
        tiled=True,
    ).astype(jnp.bfloat16)
    cot_all = lax.all_gather(out_cotangent, "blk", axis=0, tiled=True)
    hidden_grad = over_width(cot_all, w_down)
    gate_cot = (hidden_grad * upper * sigmoid_gate * (1.0 + gate * (1.0 - sigmoid_gate))).astype(
        jnp.bfloat16
    )
    up_cot = (hidden_grad * activation).astype(jnp.bfloat16)
    down_dense = over_tokens(hidden, cot_all).reshape(
        col_count, block_side, block_count, block_side
    )
    down_dense = jnp.transpose(down_dense, (0, 2, 1, 3))
    down_grad = pick_blocks(down_dense, block_index[2], live_float[2]).reshape(
        col_count, list_length, square
    )
    gate_dense = over_tokens(inputs_all, gate_cot).reshape(
        block_count, block_side, col_count, block_side
    )
    gate_dense = jnp.transpose(gate_dense, (2, 0, 1, 3))
    gate_grad = pick_blocks(gate_dense, block_index[0], live_float[0]).reshape(
        col_count, list_length, square
    )
    up_dense = over_tokens(inputs_all, up_cot).reshape(
        block_count, block_side, col_count, block_side
    )
    up_dense = jnp.transpose(up_dense, (2, 0, 1, 3))
    up_grad = pick_blocks(up_dense, block_index[1], live_float[1]).reshape(
        col_count, list_length, square
    )
    gate_grad, up_grad, down_grad = (
        lax.psum_scatter(
            gate_grad.astype(jnp.bfloat16), "rep", scatter_dimension=1, tiled=True
        ).astype(jnp.float32),
        lax.psum_scatter(
            up_grad.astype(jnp.bfloat16), "rep", scatter_dimension=1, tiled=True
        ).astype(jnp.float32),
        lax.psum_scatter(
            down_grad.astype(jnp.bfloat16), "rep", scatter_dimension=1, tiled=True
        ).astype(jnp.float32),
    )
    input_grad = lax.psum_scatter(
        over_width(gate_cot, w_gate) + over_width(up_cot, w_up),
        "blk",
        scatter_dimension=0,
        tiled=True,
    ).astype(jnp.bfloat16)
    return (layer_out, input_grad, gate_grad, up_grad, down_grad)


def solution(mesh):
    placed = (
        P(("blk", "rep"), None),
        P(("blk", "rep"), None),
        P("blk", None, None),
        P("blk", None, None),
        P("blk", None, None),
        P(None, "blk", None),
        P(None, "blk"),
    )
    return jax.shard_map(
        per_device,
        mesh=mesh,
        in_specs=placed,
        out_specs=(
            P(("blk", "rep"), None),
            P(("blk", "rep"), None),
            P("blk", "rep", None),
            P("blk", "rep", None),
            P("blk", "rep", None),
        ),
        check_vma=False,
    )
```

profile of v0, /device:TPU:2, one launch (start us, length us, event | category | flops | bytes accessed | tf_op | source)
XLA Modules:
  0.0 1133.2 jit_solution(1677589372176548421)
XLA Ops:
  11.4 4.0 copy.40
  15.4 6.7 reshape.70
  23.0 4.0 copy.42
  27.0 6.7 reshape.72
  34.7 3.3 copy.44
  38.0 7.2 reshape.74
  47.3 86.2 %all-gather.5.cloned.1.call-done = bf16[128,1,8192]{2,1,0:T(2,128)(2,1)} async-done(((bf16[1,1,8192]{2,1,0:T(2,128)(2,1)}), bf16[128,1,8192]{2,1,0:T(2,128)(2,1)}) %all-gather.5.cloned.1.call-update) | async-done | bytes 2097168 | tf_op jit(solution)/shard_map/all_gather | solution.py:60
  133.5 4.6 copy.54
  140.4 113.2 %all-gather.7.cloned.1.call-done = bf16[128,1,8192]{2,1,0:T(2,128)(2,1)} async-done(((bf16[1,1,8192]{2,1,0:T(2,128)(2,1)}), bf16[128,1,8192]{2,1,0:T(2,128)(2,1)}) %all-gather.7.cloned.1.call-update) | async-done | bytes 2097168 | tf_op jit(solution)/shard_map/all_gather | solution.py:72
  253.7 5.6 multiply_convert_fusion
  260.0 2.7 convolution_bitcast_fusion.1
  262.7 2.7 fusion.30
  265.4 2.8 convolution_bitcast_fusion
  268.2 2.7 convolution_add_fusion
  270.9 7.9 reshape.75
  278.9 9.2 copy.45
  288.0 7.3 gather_fusion
  295.4 2.7 fusion.2
  298.1 2.8 convert_element_type.53
  300.9 3.5 copy.46
  304.4 6.9 fusion.3
  311.3 8.0 reshape.77
  319.4 11.5 %copy.67 = f32[2,64,128,64]{3,1,2,0:T(8,128)} copy(f32[2,64,128,64]{3,2,1,0:T(8,128)} %reshape.77) | data formatting | bytes 8388608 | tf_op jit(solution)/shard_map/reshape | solution.py:78
  330.9 7.9 reshape.76
  338.8 9.0 copy.47
  347.8 7.3 gather_fusion.2
  355.2 7.3 gather_fusion.1
  362.5 5.4 fusion
  367.9 3.6 convert_element_type.56
  378.1 739.3 %all-reduce.11 = (bf16[128,8192]{1,0:T(8,128)(2,1)S(1)}, bf16[128,8192]{1,0:T(8,128)(2,1)}) all-reduce(f32[128,8192]{1,0:T(8,128)} %fusion.30, f32[128,8192]{1,0:T(8,128)} %convolution_add_fusion), channel_id=2, replica_groups=mesh['blk'=128,'rep'=2] {'blk'}, use_global_device_ids=true, to_apply=%region_0.0.clone | all-reduce | flops 2097152 | bytes 12582912
  1119.7 2.7 dynamic-slice_convert_fusion.2
  1122.4 2.6 dynamic-slice_convert_fusion.1
  (55 shorter events, 21.0 us)
Async XLA Ops:
  7.2 3.3 copy-start
  7.2 126.3 %all-gather.5.cloned.1.call-start = ((), (), s32[]{:S(2)}) async-start(), calls=%async_computation | async-start | bytes 4227072 | tf_op jit(solution)/shard_map/all_gather | solution.py:60
  7.9 245.7 %all-gather.7.cloned.1.call-start = ((), (), s32[]{:S(2)}) async-start(), calls=%async_computation.1 | async-start | bytes 4227072 | tf_op jit(solution)/shard_map/all_gather | solution.py:72
  8.7 1111.0 %all-reduce.10.cloned.1.call-start = ((), (), s32[]{:S(2)}) async-start(), calls=%async_computation.2 | async-start | bytes 7077888
  15.4 6.7 copy-start.7
  27.0 6.7 copy-start.8
  38.0 7.2 copy-start.10
  38.0 7.4 copy-start.12
  38.0 8.1 copy-start.11
  133.5 4.6 copy-start.4
  138.1 1.6 copy-start.2
  253.7 5.6 copy-start.5
  260.0 2.7 copy-start.6
  265.4 2.8 copy-start.3
  1119.7 5.3 copy-start.9
  1119.7 6.8 copy-start.1
Sparse Core Ops, SparseCore 0:
  11.6 121.8 all-gather.4
  137.1 116.5 all-gather.6
  378.2 103.2 all-reduce.9
where the time goes:
time: 1140 us; the launch traced here: 1130 us
  blocking collectives  739 us (65%)
  waiting for transfers between devices  201 us (18%)
  local copies, waits for them, and re-layouts  134 us (12%)
  matrix products  28.4 us (2%)
  other arithmetic  15.8 us (1%)
  between operations  14.9 us (1%)
    unnamed x1, blocking collectives  739 us
    all_gather x1, waiting for transfers between devices, per_device(): cot_all = lax.all_gather(out_cotangent, 'blk', axis=0, tiled=True)  113 us
    all_gather x1, waiting for transfers between devices, per_device(): inputs_all = lax.all_gather(activations, 'blk', axis=0, tiled=True)  86.2 us
  transfers between devices with their start and end apart: 3, of which 2 were waited for; matrix products, arithmetic and copies ran while one was open for 4% of the time, Pallas kernels for 0%

commit v1 on v0

v1 whole, which is shorter than its diff:
```python
import functools

import jax
import jax.numpy as jnp
from jax import lax
from jax.experimental import pallas as pl
from jax.experimental.pallas import tpu as pltpu
from jax.sharding import Mesh
from jax.sharding import PartitionSpec as P

SIDE = 64
LANES = 128
WIDTH = SIDE * LANES
UNITS = 2 * SIDE
HALF = 36
PADDED = 40
ROWS = 16
FAR = 16
SHIFTS = (2, 1, 3)
VMEM_BYTES = 44 * 1024 * 1024
BF16 = jnp.bfloat16
F32 = jnp.float32
NT = (((1,), (1,)), ((), ()))


def call(kernel, outs, scratch, micros, *operands):
    return pl.pallas_call(
        kernel,
        out_shape=outs,
        in_specs=[pl.BlockSpec(memory_space=pltpu.VMEM)] * len(operands),
        out_specs=[pl.BlockSpec(memory_space=pltpu.VMEM)] * len(outs),
        scratch_shapes=scratch,
        compiler_params=pltpu.CompilerParams(vmem_limit_bytes=VMEM_BYTES),
        cost_estimate=pl.CostEstimate(
            flops=0, bytes_accessed=int(micros * 3_000_000), transcendentals=0
        ),
    )(*operands)


def span(step, width):
    return pl.ds(pl.multiple_of(step * width, width), width)


def densify_kernel(pick_ref, gate_ref, up_ref, down_ref, wide_ref, down_dense_ref, strip_ref):
    for matrix, blocks_ref in enumerate((gate_ref, up_ref)):

        def spread(step, carry, matrix=matrix, blocks_ref=blocks_ref):
            cols = span(step, 8 * SIDE)
            first, second = (
                jnp.dot(
                    pick_ref[2 * matrix + unit],
                    blocks_ref[unit, :, cols],
                    preferred_element_type=F32,
                )
                for unit in range(2)
            )
            for inner in range(8):
                part = slice(inner * SIDE, (inner + 1) * SIDE)
                tile = jnp.concatenate([first[:, part], second[:, part]], axis=1)
                wide_ref[
                    span(step * 8 + inner, LANES), matrix * UNITS : (matrix + 1) * UNITS
                ] = tile.astype(BF16)
            return carry

        lax.fori_loop(0, 8, spread, 0)
    for unit in range(2):

        def turn(step, carry, unit=unit):
            dense = jnp.dot(
                pick_ref[4 + unit],
                down_ref[unit, :, span(step, 256)],
                preferred_element_type=F32,
            )
            strip_ref[span(step, 256), :] = dense.T
            return carry

        lax.fori_loop(0, 16, turn, 0)
        for inner in range(SIDE):
            rows = strip_ref[pl.ds(inner, SIDE, SIDE), :]
            down_dense_ref[
                unit * SIDE : (unit + 1) * SIDE, inner * LANES : (inner + 1) * LANES
            ] = rows.astype(BF16)


def joined(pieces, which, cols):
    return jnp.concatenate([piece[which, :, cols] for piece in pieces], axis=0)


def middle_kernel(*refs):
    pieces = refs[:8]
    wide_ref, down_ref, near_ref, away_ref, hidden_ref, cots_ref, back_ref = refs[8:]

    def forward(step, total):
        cols = span(step, 1024)
        return total + jnp.dot(
            joined(pieces, 0, cols), wide_ref[cols, :], preferred_element_type=F32
        )

    both = lax.fori_loop(0, 8, forward, jnp.zeros((LANES, 2 * UNITS), F32))

    def backward(step, total):
        cols = span(step, 1024)
        return total + lax.dot_general(
            joined(pieces, 1, cols), down_ref[:, cols], NT, preferred_element_type=F32
        )

    hidden_grad = lax.fori_loop(0, 8, backward, jnp.zeros((LANES, UNITS), F32))
    gate, upper = both[:, :UNITS], both[:, UNITS:]
    sigmoid_gate = jax.nn.sigmoid(gate)
    activation = gate * sigmoid_gate
    hidden = activation * upper
    gate_cot = hidden_grad * upper * sigmoid_gate * (1.0 + gate * (1.0 - sigmoid_gate))
    up_cot = hidden_grad * activation
    hidden_ref[...] = hidden.T.astype(BF16)
    cots_ref[:UNITS, :] = gate_cot.T.astype(BF16)
    cots_ref[UNITS:, :] = up_cot.T.astype(BF16)
    hidden = hidden.astype(BF16)
    back_ref[:, :UNITS] = gate_cot.astype(BF16)
    back_ref[:, UNITS:] = up_cot.astype(BF16)

    def put(which, cols, values):
        values = values.astype(BF16)
        for slot in range(4):
            near_ref[slot, which, :, cols] = values[slot * ROWS : (slot + 1) * ROWS]
            away_ref[slot, which, :, cols] = values[(slot + 4) * ROWS : (slot + 5) * ROWS]

    def outward(step, carry):
        cols = span(step, 512)
        put(0, cols, jnp.dot(hidden, down_ref[:, cols], preferred_element_type=F32))
        put(
            1,
            cols,
            lax.dot_general(back_ref[...], wide_ref[cols, :], NT, preferred_element_type=F32),
        )
        return carry

    lax.fori_loop(0, 16, outward, 0)


def listed(select_ref, rows, cols, keep_ref, send_ref):
    values = lax.dot_general(select_ref[...], rows, NT, preferred_element_type=F32)
    keep_ref[:, cols] = values[: 2 * PADDED]
    send_ref[:, cols] = values[2 * PADDED :].astype(BF16)


def down_grad_kernel(*refs):
    pieces = refs[:8]
    hidden_ref, select_ref, keep_ref, send_ref, strip_ref = refs[8:]

    def dense(step, carry):
        values = jnp.dot(
            hidden_ref[...], joined(pieces, 1, span(step, 512)), preferred_element_type=F32
        )
        for part in range(4):
            for unit in range(2):
                strip_ref[unit, pl.ds(step * 4 + part, SIDE, SIDE), :] = values[
                    unit * SIDE : (unit + 1) * SIDE, part * LANES : (part + 1) * LANES
                ]
        return carry

    lax.fori_loop(0, 16, dense, 0)

    def pick(step, carry):
        cols = span(step, 256)
        rows = jnp.concatenate([strip_ref[0, cols, :], strip_ref[1, cols, :]], axis=1)
        listed(select_ref, rows.astype(BF16), cols, keep_ref, send_ref)
        return carry

    lax.fori_loop(0, 16, pick, 0)


def wide_grad_kernel(*refs):
    pieces = refs[:8]
    cots_ref, select_ref, keep_gate, send_gate, keep_up, send_up = refs[8:]

    def step_of(step, carry):
        values = jnp.dot(
            cots_ref[...], joined(pieces, 0, span(step, 512)), preferred_element_type=F32
        ).astype(BF16)
        for matrix, keep_ref, send_ref in ((0, keep_gate, send_gate), (1, keep_up, send_up)):
            rows = jnp.concatenate(
                [
                    jnp.concatenate(
                        [
                            values[
                                matrix * UNITS + unit * SIDE : matrix * UNITS + (unit + 1) * SIDE,
                                part * LANES : (part + 1) * LANES,
                            ]
                            for unit in range(2)
                        ],
                        axis=1,
                    )
                    for part in range(4)
                ],
                axis=0,
            )
            listed(select_ref.at[matrix], rows, span(step, 256), keep_ref, send_ref)
        return carry

    lax.fori_loop(0, 16, step_of, 0)


def ring(size, shift):
    return [(place, (place + shift) % size) for place in range(size)]


def per_device(
    activations, out_cotangent, gate_blocks, up_blocks, down_blocks, block_index, block_counts
):
    length = gate_blocks.shape[1]
    live = jnp.arange(length)[None, None, :] < block_counts[:, :, None]
    places = jnp.where(live, block_index, -1)
    pick = (places[:, :, None, :] == jnp.arange(LANES)[None, None, :, None]).astype(BF16)
    pick = pick.reshape(6, LANES, length)
    halves = jnp.pad(
        places.reshape(3, 2, 2, HALF), ((0, 0), (0, 0), (0, 0), (0, PADDED - HALF)), constant_values=-1
    )
    halves = jnp.where(lax.axis_index("rep") == 0, halves, halves[:, :, ::-1])
    halves = jnp.transpose(halves, (0, 2, 1, 3))
    goal = jnp.where(halves >= 0, halves + LANES * jnp.arange(2)[None, None, :, None], -1)
    select = (goal.reshape(3, 4 * PADDED)[:, :, None] == jnp.arange(2 * LANES)).astype(BF16)

    wide, down = call(
        densify_kernel,
        [
            jax.ShapeDtypeStruct((WIDTH, 2 * UNITS), BF16),
            jax.ShapeDtypeStruct((UNITS, WIDTH), BF16),
        ],
        [pltpu.VMEM((SIDE * SIDE, LANES), F32)],
        8,
        pick,
        gate_blocks,
        up_blocks,
        down_blocks,
    )

    rows = jnp.stack([activations, out_cotangent], axis=1).reshape(1, 2, LANES, SIDE)
    rows = jnp.swapaxes(rows, 2, 3)
    rows = lax.all_to_all(
        jnp.broadcast_to(rows, (FAR, 2, SIDE, LANES)), ("xh", "z"), 0, 0, tiled=True
    )
    first = jnp.swapaxes(rows.reshape(FAR, 2, WIDTH), 0, 1)
    here = [first] + [lax.ppermute(first, "y", ring(4, shift)) for shift in SHIFTS]
    there = [lax.ppermute(piece, "c", ring(2, 1)) for piece in here]
    pieces = here + there

    sums = jax.ShapeDtypeStruct((4, 2, ROWS, WIDTH), BF16)
    near, away, hidden, cots = call(
        middle_kernel,
        [
            sums,
            sums,
            jax.ShapeDtypeStruct((UNITS, LANES), BF16),
            jax.ShapeDtypeStruct((2 * UNITS, LANES), BF16),
        ],
        [pltpu.VMEM((LANES, 2 * UNITS), BF16)],
        8,
        *pieces,
        wide,
        down,
    )
    kept = jax.ShapeDtypeStruct((2 * PADDED, SIDE * SIDE), F32)
    sent = jax.ShapeDtypeStruct((2 * PADDED, SIDE * SIDE), BF16)

    away = lax.ppermute(away, "c", ring(2, 1))
    keep_down, send_down = call(
        down_grad_kernel,
        [kept, sent],
        [pltpu.VMEM((2, SIDE * SIDE, LANES), F32)],
        5,
        *pieces,
        hidden,
        select[2],
    )
    keep_gate, send_gate, keep_up, send_up = call(
        wide_grad_kernel, [kept, sent, kept, sent], [], 5, *pieces, cots, select[:2]
    )

    total = near.astype(F32) + away.astype(F32)
    moved = [
        lax.ppermute(total[slot + 1].astype(BF16), "y", ring(4, -shift))
        for slot, shift in enumerate(SHIFTS)
    ]
    total = total[0] + sum(part.astype(F32) for part in moved)
    total = jnp.swapaxes(total.astype(BF16), 0, 1).reshape(FAR, 2, SIDE, LANES)
    total = lax.all_to_all(total, ("xh", "z"), 0, 0, tiled=True)
    total = jnp.sum(total.astype(F32), axis=0)
    total = jnp.swapaxes(total, 1, 2).reshape(2, 1, WIDTH).astype(BF16)

    def settle(keep, send):
        other = lax.ppermute(send, "rep", ring(2, 1))
        keep, other = (
            part.reshape(2, PADDED, SIDE * SIDE)[:, :HALF] for part in (keep, other)
        )
        return keep + other.astype(F32)

    return (
        total[0],
        total[1],
        settle(keep_gate, send_gate),
        settle(keep_up, send_up),
        settle(keep_down, send_down),
    )


def solution(mesh):
    fine = Mesh(mesh.devices.reshape(2, 8, 4, 2, 2), ("xh", "z", "y", "c", "rep"))
    blk = ("xh", "z", "y", "c")
    placed = (
        P((*blk, "rep"), None),
        P((*blk, "rep"), None),
        P(blk, None, None),
        P(blk, None, None),
        P(blk, None, None),
        P(None, blk, None),
        P(None, blk),
    )
    return jax.shard_map(
        per_device,
        mesh=fine,
        in_specs=placed,
        out_specs=(
            P((*blk, "rep"), None),
            P((*blk, "rep"), None),
            P(blk, "rep", None),
            P(blk, "rep", None),
            P(blk, "rep", None),
        ),
        check_vma=False,
    )
```

time: 1140 us -> 170 us (0.15)
  blocking collectives: 739 us -> 27.1 us
  waiting for transfers between devices: 201 us -> 48.2 us
  local copies, waits for them, and re-layouts: 134 us -> 12.3 us
  Pallas kernels: 0 us -> 45.8 us
  matrix products: 28.4 us -> 0 us
  starting transfers between devices: 0.11 us -> 21.4 us
  between operations: 14.9 us -> 0.87 us
    unnamed x1 -> x0, blocking collectives: 739 us -> none
    all_gather x2 -> x0, waiting for transfers between devices: 199 us -> none  [the longest x1 113 us: per_device(): cot_all = lax.all_gather(out_cotangent, 'blk', axis=0, tiled=True)]
    reshape x9 -> x4, local copies, waits for them, and re-layouts: 74.1 us -> 1.35 us  [the longest x1 0.85 us: per_device(): total = jnp.swapaxes(total.astype(BF16), 0, 1).reshape(FAR, 2, SIDE, LANES)]
    pallas_call x0 -> x4, Pallas kernels: none -> 45.8 us  [call(): pl.pallas_call(kernel, out_shape=outs, in_specs=[pl.BlockSpec(memory_spac...]
    ppermute x0 -> x14, waiting for transfers between devices: none -> 37.1 us  [the longest x3 19 us: per_device(): lax.ppermute(total[slot + 1].astype(BF16), 'y', ring(4, -shift))]
    all_to_all x0 -> x1, blocking collectives: none -> 27.1 us  [per_device(): lax.all_to_all(jnp.broadcast_to(rows, (FAR, 2, SIDE, LANES)), ('xh', 'z')...]
    dot_general x9 -> x0, matrix products: 25.6 us -> none  [the longest x3 12.5 us: over_tokens(): lax.dot_general(left, right, (((0,), (0,)), ((), ())), preferred_element_...]
    gather x6 -> x0, local copies, waits for them, and re-layouts: 22.3 us -> none  [pick_blocks(): picked = jnp.take_along_axis(dense_tiles, lists[:, :, None, None], axis=1)]
  transfers between devices with their start and end apart: 3 -> 15, of which waited for: 2 -> 6; matrix products, arithmetic and copies ran while one was open for 4% -> 7% of each run, Pallas kernels for 0% -> 20%
where the time goes in v1:
time: 170 us; the launch traced here: 167 us
  waiting for transfers between devices  48.2 us (28%)
  Pallas kernels  45.8 us (27%)
  blocking collectives  27.1 us (16%)
  starting transfers between devices  21.4 us (13%)
  local copies, waits for them, and re-layouts  12.3 us (7%)
  other arithmetic  11.3 us (7%)
    pallas_call x4, Pallas kernels, call(): pl.pallas_call(kernel, out_shape=outs, in_specs=[pl.BlockSpec(memory_spac...  45.8 us
    all_to_all x1, blocking collectives, per_device(): lax.all_to_all(jnp.broadcast_to(rows, (FAR, 2, SIDE, LANES)), ('xh', 'z')...  27.1 us
    ppermute x3, waiting for transfers between devices, per_device(): lax.ppermute(total[slot + 1].astype(BF16), 'y', ring(4, -shift))  19 us
    ppermute x3, waiting for transfers between devices, per_device(): lax.ppermute(first, 'y', ring(4, shift))  18.1 us
    all_to_all x1, waiting for transfers between devices, per_device(): total = lax.all_to_all(total, ('xh', 'z'), 0, 0, tiled=True)  11.1 us
    unnamed x28, local copies, waits for them, and re-layouts  8.67 us
    add x3, other arithmetic, settle(): return keep + other.astype(F32)  6.7 us
    ppermute x3, starting transfers between devices, per_device(): lax.ppermute(first, 'y', ring(4, shift))  6.52 us
  transfers between devices with their start and end apart: 15, of which 6 were waited for; matrix products, arithmetic and copies ran while one was open for 7% of the time, Pallas kernels for 20%

profile of v1, /device:TPU:2, one launch (start us, length us, event | category | flops | bytes accessed | tf_op | source)
XLA Modules:
  0.0 167.0 jit_solution(17707786883832060040)
XLA Ops:
  0.6 0.8 reduce.2
  1.6 0.8 reduce.1
  2.7 27.1 %all_to_all.10 = bf16[16,2,64,128]{3,2,1,0:T(8,128)(2,1)S(1)} all-to-all(bf16[16,2,64,128]{3,2,1,0:T(8,128)(2,1)S(1)} %broadcast_in_dim.22), channel_id=1, replica_groups=mesh['xh'=2,'z'=8,'y'=4,'c'=2,'rep'=2] {'xh','z'}, dimensions={0} | all-to-all | bytes 1048576 | tf_op jit(solution)/shard_map/all_to_all | solution.py:239
  30.3 3.3 %collective-permute-start = (bf16[2,16,8192]{2,1,0:T(8,128)(2,1)S(1)}, bf16[2,16,8192]{2,1,0:T(8,128)(2,1)S(1)}, u32[]{:S(2)}, u32[]{:S(2)}) collective-permute-start(bf16[2,16,8192]{2,1,0:T(8,128)(2,1)S(1)} %bitcast.45), channel_id=1, source_target_pairs={{0,8},{4,12},{8,0},{12,4},{1,9},{5,13},{9,1},{13,5},{2,10},{6,14},... | collective-permute-start | bytes 1572872 | tf_op jit(solution)/shard_map/ppermute | solution.py:243
  34.3 2.6 %collective-permute-start.2 = (bf16[2,16,8192]{2,1,0:T(8,128)(2,1)S(1)}, bf16[2,16,8192]{2,1,0:T(8,128)(2,1)S(1)}, u32[]{:S(2)}, u32[]{:S(2)}) collective-permute-start(bf16[2,16,8192]{2,1,0:T(8,128)(2,1)S(1)} %bitcast.47), channel_id=1, source_target_pairs={{0,12},{4,0},{8,4},{12,8},{1,13},{5,1},{9,5},{13,9},{2,14},{6,2},{... | collective-permute-start | bytes 1572872 | tf_op jit(solution)/shard_map/ppermute | solution.py:243
  36.8 10.0 %collective-permute-done.refs_1_ = bf16[2,16,8192]{2,1,0:T(8,128)(2,1)S(1)} collective-permute-done((bf16[2,16,8192]{2,1,0:T(8,128)(2,1)S(1)}, bf16[2,16,8192]{2,1,0:T(8,128)(2,1)S(1)}, u32[]{:S(2)}, u32[]{:S(2)}) %collective-permute-start) | collective-permute-done | bytes 524320 | tf_op jit(solution)/shard_map/ppermute | solution.py:243
  46.8 7.8 %collective-permute-done.1.refs_2_ = bf16[2,16,8192]{2,1,0:T(8,128)(2,1)S(1)} collective-permute-done((bf16[2,16,8192]{2,1,0:T(8,128)(2,1)S(1)}, bf16[2,16,8192]{2,1,0:T(8,128)(2,1)S(1)}, u32[]{:S(2)}, u32[]{:S(2)}) %collective-permute-start.1) | collective-permute-done | bytes 524320 | tf_op jit(solution)/shard_map/ppermute | solution.py:243
  55.3 1.3 copy-done.8
  56.6 1.3 copy-done.9
  57.9 1.3 copy-done.10
  59.1 14.7 %shard_map.110 = (bf16[8192,256]{1,0:T(8,128)(2,1)S(1)}, bf16[128,8192]{1,0:T(8,128)(2,1)S(1)}) custom-call(bf16[6,128,72]{2,1,0:T(8,128)(2,1)S(1)} %fusion.3.pick_ref, bf16[2,72,4096]{2,1,0:T(8,128)(2,1)S(1)} %copy-done.8, bf16[2,72,4096]{2,1,0:T(8,128)(2,1)S(1)} %copy-done.9, bf16[2,72,4096]{2,1,0:T(8,128)(2,1)S(1)} %copy-done.10), custom_call_target="tpu_custom_call" | custom-call | bytes 24000000 | tf_op jit(solution)/shard_map/pallas_call | solution.py:27
  73.9 1.9 %copy-done = bf16[8192,256]{1,0:T(8,128)(2,1)} copy-done((bf16[8192,256]{1,0:T(8,128)(2,1)}, bf16[8192,256]{1,0:T(8,128)(2,1)S(1)}, u32[]{:S(2)}) %copy-start) | copy-done | bytes 4194328
  75.8 1.4 copy-done.3
  77.2 12.6 %shard_map.111 = (bf16[4,2,16,8192]{3,2,1,0:T(8,128)(2,1)S(1)}, bf16[4,2,16,8192]{3,2,1,0:T(8,128)(2,1)}, bf16[128,128]{1,0:T(8,128)(2,1)S(1)}, bf16[256,128]{1,0:T(8,128)(2,1)S(1)}) custom-call(bf16[2,16,8192]{2,1,0:T(8,128)(2,1)S(1)} %bitcast.49, bf16[2,16,8192]{2,1,0:T(8,128)(2,1)S(1)} %collective-permute-done.refs_1_, ...), custom_call_target="tpu_custom_call" | custom-call | bytes 24000000 | tf_op jit(solution)/shard_map/pallas_call | solution.py:27
  89.8 1.3 copy-done.1
  92.0 9.3 %shard_map.113 = (f32[80,4096]{1,0:T(8,128)S(1)}, bf16[80,4096]{1,0:T(8,128)(2,1)S(1)}) custom-call(bf16[2,16,8192]{2,1,0:T(8,128)(2,1)S(1)} %bitcast.50, bf16[2,16,8192]{2,1,0:T(8,128)(2,1)S(1)} %collective-permute-done.refs_1_, bf16[2,16,8192]{2,1,0:T(8,128)(2,1)S(1)} %collective-permute-done.1.refs_2_, ...), custom_call_target="tpu_custom_call" | custom-call | bytes 15000000 | tf_op jit(solution)/shard_map/pallas_call | solution.py:27
  101.3 1.5 collective-permute-start.13
  102.8 9.2 %shard_map.112 = (f32[80,4096]{1,0:T(8,128)S(1)}, bf16[80,4096]{1,0:T(8,128)(2,1)}, f32[80,4096]{1,0:T(8,128)S(1)}, bf16[80,4096]{1,0:T(8,128)(2,1)}) custom-call(bf16[2,16,8192]{2,1,0:T(8,128)(2,1)S(1)} %bitcast.51, bf16[2,16,8192]{2,1,0:T(8,128)(2,1)S(1)} %collective-permute-done.refs_1_, bf16[2,16,8192]{2,1,0:T(8,128)(2,1)S(1)} %collective-permute-done.1.refs_2_, ...), custom_call_target="tpu_custom_call" | custom-call | bytes 15000000 | tf_op jit(solution)/shard_map/pallas_call | solution.py:27
  112.6 1.4 collective-permute-start.11
  114.0 2.2 %fusion.5 = (bf16[4,2,16,8192]{3,2,1,0:T(8,128)(2,1)S(1)}, f32[4,2,16,8192]{3,2,1,0:T(8,128)S(1)}) fusion(bf16[4,2,16,8192]{3,2,1,0:T(8,128)(2,1)} %collective-permute-done.7, bf16[4,2,16,8192]{3,2,1,0:T(8,128)(2,1)S(1)} %copy-done.2), kind=kLoop, calls=%fused_computation.21 | loop fusion | flops 4194304 | bytes 10485760 | tf_op jit(solution)/shard_map/convert.3
  116.4 1.4 collective-permute-start.10
  117.8 2.7 %collective-permute-start.8 = (bf16[2,16,8192]{2,1,0:T(8,128)(2,1)S(1)}, bf16[2,16,8192]{2,1,0:T(8,128)(2,1)S(1)}, u32[]{:S(2)}, u32[]{:S(2)}) collective-permute-start(bf16[2,16,8192]{2,1,0:T(8,128)(2,1)S(1)} %get-tuple-element.31), channel_id=1, source_target_pairs={{0,8},{4,12},{8,0},{12,4},{1,9},{5,13},{9,1},{13,5},{2,10},{6,14},... | collective-permute-start | bytes 1572872 | tf_op jit(solution)/shard_map/ppermute | solution.py:281
  120.6 1.0 collective-permute-start.9
  121.6 2.2 %copy_add_fusion = f32[2,36,4096]{2,0,1:T(2,128)} fusion(f32[2,36,4096]{2,1,0:T(8,128)S(1)} %bitcast.54, bf16[2,36,4096]{2,1,0:T(8,128)(2,1)S(1)} %bitcast.59), kind=kLoop, calls=%fused_computation.1 | loop fusion | flops 589824 | bytes 2949120 | tf_op jit(solution)/shard_map/add | solution.py:295
  123.8 8.1 %collective-permute-done.10 = bf16[2,16,8192]{2,1,0:T(8,128)(2,1)S(1)} collective-permute-done((bf16[2,16,8192]{2,1,0:T(8,128)(2,1)S(1)}, bf16[2,16,8192]{2,1,0:T(8,128)(2,1)S(1)}, u32[]{:S(2)}, u32[]{:S(2)}) %collective-permute-start.10) | collective-permute-done | bytes 524320 | tf_op jit(solution)/shard_map/ppermute | solution.py:281
  131.9 10.9 %collective-permute-done.8 = bf16[2,16,8192]{2,1,0:T(8,128)(2,1)S(1)} collective-permute-done((bf16[2,16,8192]{2,1,0:T(8,128)(2,1)S(1)}, bf16[2,16,8192]{2,1,0:T(8,128)(2,1)S(1)}, u32[]{:S(2)}, u32[]{:S(2)}) %collective-permute-start.8) | collective-permute-done | bytes 524320 | tf_op jit(solution)/shard_map/ppermute | solution.py:281
  143.2 0.9 copy.33
  144.0 5.6 %all-to-all-start.1 = ((bf16[16,2,64,128]{3,2,1,0:T(8,128)(2,1)}), bf16[16,2,64,128]{3,2,1,0:T(8,128)(2,1)S(1)}, u32[]{:S(2)}, u32[]{:S(2)}) async-start(bf16[16,2,64,128]{3,2,1,0:T(8,128)(2,1)} %copy.33), calls=%async_computation.1 | async-start | bytes 1048576 | tf_op jit(solution)/shard_map/all_to_all | solution.py:286
  149.7 2.2 %copy_add_fusion.1 = f32[2,36,4096]{2,0,1:T(2,128)} fusion(f32[2,36,4096]{2,1,0:T(8,128)S(1)} %bitcast.53, bf16[2,36,4096]{2,1,0:T(8,128)(2,1)S(1)} %bitcast.58), kind=kLoop, calls=%fused_computation.2 | loop fusion | flops 589824 | bytes 2949120 | tf_op jit(solution)/shard_map/add | solution.py:295
  151.9 2.2 %copy_add_fusion.2 = f32[2,36,4096]{2,0,1:T(2,128)} fusion(f32[2,36,4096]{2,1,0:T(8,128)S(1)} %bitcast.52, bf16[2,36,4096]{2,1,0:T(8,128)(2,1)S(1)} %bitcast.57), kind=kLoop, calls=%fused_computation.3 | loop fusion | flops 589824 | bytes 2949120 | tf_op jit(solution)/shard_map/add | solution.py:295
  154.2 11.1 %all-to-all-done.1 = bf16[16,2,64,128]{3,2,1,0:T(8,128)(2,1)S(1)} async-done(((bf16[16,2,64,128]{3,2,1,0:T(8,128)(2,1)}), bf16[16,2,64,128]{3,2,1,0:T(8,128)(2,1)S(1)}, u32[]{:S(2)}, u32[]{:S(2)}) %all-to-all-start.1) | async-done | bytes 524320 | tf_op jit(solution)/shard_map/all_to_all | solution.py:286
  165.5 0.7 squeeze.16
  (66 shorter events, 5.2 us)
Async XLA Ops:
  29.9 25.2 %copy-start.12 = (s32[3,2]{0,1:T(2,128)S(1)}, s32[3,2]{0,1:T(2,128)}, u32[]{:S(2)}) copy-start(s32[3,2]{0,1:T(2,128)} %param.13) | copy-start | bytes 76
  29.9 25.3 %copy-start.11 = (s32[3,2,72]{2,1,0:T(2,128)S(1)}, s32[3,2,72]{2,1,0:T(2,128)}, u32[]{:S(2)}) copy-start(s32[3,2,72]{2,1,0:T(2,128)} %param.12) | copy-start | bytes 5188
  30.3 16.5 %collective-permute-start = (bf16[2,16,8192]{2,1,0:T(8,128)(2,1)S(1)}, bf16[2,16,8192]{2,1,0:T(8,128)(2,1)S(1)}, u32[]{:S(2)}, u32[]{:S(2)}) collective-permute-start(bf16[2,16,8192]{2,1,0:T(8,128)(2,1)S(1)} %bitcast.45), channel_id=1, source_target_pairs={{0,8},{4,12},{8,0},{12,4},{1,9},{5,13},{9,1},{13,5},{2,10},{6,14},... | collective-permute-start | bytes 1572872 | tf_op jit(solution)/shard_map/ppermute | solution.py:243
  33.6 21.0 %collective-permute-start.1 = (bf16[2,16,8192]{2,1,0:T(8,128)(2,1)S(1)}, bf16[2,16,8192]{2,1,0:T(8,128)(2,1)S(1)}, u32[]{:S(2)}, u32[]{:S(2)}) collective-permute-start(bf16[2,16,8192]{2,1,0:T(8,128)(2,1)S(1)} %bitcast.46), channel_id=1, source_target_pairs={{0,4},{4,8},{8,12},{12,0},{1,5},{5,9},{9,13},{13,1},{2,6},{6,10},{... | collective-permute-start | bytes 1572872 | tf_op jit(solution)/shard_map/ppermute | solution.py:243
  34.3 20.7 %collective-permute-start.2 = (bf16[2,16,8192]{2,1,0:T(8,128)(2,1)S(1)}, bf16[2,16,8192]{2,1,0:T(8,128)(2,1)S(1)}, u32[]{:S(2)}, u32[]{:S(2)}) collective-permute-start(bf16[2,16,8192]{2,1,0:T(8,128)(2,1)S(1)} %bitcast.47), channel_id=1, source_target_pairs={{0,12},{4,0},{8,4},{12,8},{1,13},{5,1},{9,5},{13,9},{2,14},{6,2},{... | collective-permute-start | bytes 1572872 | tf_op jit(solution)/shard_map/ppermute | solution.py:243
  36.8 40.4 %collective-permute-start.3 = (bf16[2,16,8192]{2,1,0:T(8,128)(2,1)S(1)}, bf16[2,16,8192]{2,1,0:T(8,128)(2,1)S(1)}, u32[]{:S(2)}, u32[]{:S(2)}) collective-permute-start(bf16[2,16,8192]{2,1,0:T(8,128)(2,1)S(1)} %bitcast.48), channel_id=1, source_target_pairs={{0,2},{2,0},{1,3},{3,1},{4,6},{6,4},{5,7},{7,5},{8,10},{10,8},{9,1... | collective-permute-start | bytes 1572872 | tf_op jit(solution)/shard_map/ppermute | solution.py:244
  46.8 30.4 %collective-permute-start.4 = (bf16[2,16,8192]{2,1,0:T(8,128)(2,1)S(1)}, bf16[2,16,8192]{2,1,0:T(8,128)(2,1)S(1)}, u32[]{:S(2)}, u32[]{:S(2)}) collective-permute-start(bf16[2,16,8192]{2,1,0:T(8,128)(2,1)S(1)} %collective-permute-done.refs_1_), channel_id=1, source_target_pairs={{0,2},{2,0},{1,3},{3,1},{4,6},{6,4},{5,7},{7,5},{8,10},{10,8},{9,1... | collective-permute-start | bytes 1572872 | tf_op jit(solution)/shard_map/ppermute | solution.py:244
  54.6 22.7 %collective-permute-start.5 = (bf16[2,16,8192]{2,1,0:T(8,128)(2,1)S(1)}, bf16[2,16,8192]{2,1,0:T(8,128)(2,1)}, u32[]{:S(2)}, u32[]{:S(2)}) collective-permute-start(bf16[2,16,8192]{2,1,0:T(8,128)(2,1)S(1)} %collective-permute-done.1.refs_2_), channel_id=1, source_target_pairs={{0,2},{2,0},{1,3},{3,1},{4,6},{6,4},{5,7},{7,5},{8,10},{10,8},{9,1... | collective-permute-start | bytes 1572872 | tf_op jit(solution)/shard_map/ppermute | solution.py:244
  55.0 22.3 %collective-permute-start.6 = (bf16[2,16,8192]{2,1,0:T(8,128)(2,1)S(1)}, bf16[2,16,8192]{2,1,0:T(8,128)(2,1)}, u32[]{:S(2)}, u32[]{:S(2)}) collective-permute-start(bf16[2,16,8192]{2,1,0:T(8,128)(2,1)S(1)} %collective-permute-done.2.refs_3_), channel_id=1, source_target_pairs={{0,2},{2,0},{1,3},{3,1},{4,6},{6,4},{5,7},{7,5},{8,10},{10,8},{9,1... | collective-permute-start | bytes 1572872 | tf_op jit(solution)/shard_map/ppermute | solution.py:244
  55.3 1.3 copy-start.8
  56.6 1.3 copy-start.9
  57.9 1.3 copy-start.10
  73.9 2.0 %copy-start = (bf16[8192,256]{1,0:T(8,128)(2,1)}, bf16[8192,256]{1,0:T(8,128)(2,1)S(1)}, u32[]{:S(2)}) copy-start(bf16[8192,256]{1,0:T(8,128)(2,1)S(1)} %get-tuple-element.17.refs_8_) | copy-start | bytes 12582916
  75.8 1.4 copy-start.3
  89.8 1.3 copy-start.1
  91.1 22.9 %collective-permute-start.7 = (bf16[4,2,16,8192]{3,2,1,0:T(8,128)(2,1)}, bf16[4,2,16,8192]{3,2,1,0:T(8,128)(2,1)}, u32[]{:S(2)}, u32[]{:S(2)}) collective-permute-start(bf16[4,2,16,8192]{3,2,1,0:T(8,128)(2,1)} %get-tuple-element.20), channel_id=1, source_target_pairs={{0,2},{2,0},{1,3},{3,1},{4,6},{6,4},{5,7},{7,5},{8,10},{10,8},{9,1... | collective-permute-start | bytes 6291464 | tf_op jit(solution)/shard_map/ppermute | solution.py:265
  101.3 19.3 %collective-permute-start.13 = (bf16[80,4096]{1,0:T(8,128)(2,1)S(1)}, bf16[80,4096]{1,0:T(8,128)(2,1)S(1)}, u32[]{:S(2)}, u32[]{:S(2)}) collective-permute-start(bf16[80,4096]{1,0:T(8,128)(2,1)S(1)} %get-tuple-element.28), channel_id=1, source_target_pairs={{0,1},{1,0},{2,3},{3,2},{4,5},{5,4},{6,7},{7,6},{8,9},{9,8},{10,11... | collective-permute-start | bytes 1966088 | tf_op jit(solution)/shard_map/ppermute | solution.py:291
  102.8 11.2 %copy-start.2 = (bf16[4,2,16,8192]{3,2,1,0:T(8,128)(2,1)S(1)}, bf16[4,2,16,8192]{3,2,1,0:T(8,128)(2,1)}, u32[]{:S(2)}) copy-start(bf16[4,2,16,8192]{3,2,1,0:T(8,128)(2,1)} %copy-done.1) | copy-start | bytes 6291460
  112.0 4.3 %copy-start.4 = (f32[80,4096]{1,0:T(8,128)}, f32[80,4096]{1,0:T(8,128)S(1)}, u32[]{:S(2)}) copy-start(f32[80,4096]{1,0:T(8,128)S(1)} %get-tuple-element.22) | copy-start | bytes 3932164
  112.0 4.3 %copy-start.6 = (f32[80,4096]{1,0:T(8,128)}, f32[80,4096]{1,0:T(8,128)S(1)}, u32[]{:S(2)}) copy-start(f32[80,4096]{1,0:T(8,128)S(1)} %get-tuple-element.24) | copy-start | bytes 3932164
  112.0 37.7 %collective-permute-start.12 = (bf16[80,4096]{1,0:T(8,128)(2,1)}, bf16[80,4096]{1,0:T(8,128)(2,1)S(1)}, u32[]{:S(2)}, u32[]{:S(2)}) collective-permute-start(bf16[80,4096]{1,0:T(8,128)(2,1)} %get-tuple-element.25), channel_id=1, source_target_pairs={{0,1},{1,0},{2,3},{3,2},{4,5},{5,4},{6,7},{7,6},{8,9},{9,8},{10,11... | collective-permute-start | bytes 1966088 | tf_op jit(solution)/shard_map/ppermute | solution.py:291
  112.6 39.3 %collective-permute-start.11 = (bf16[80,4096]{1,0:T(8,128)(2,1)}, bf16[80,4096]{1,0:T(8,128)(2,1)S(1)}, u32[]{:S(2)}, u32[]{:S(2)}) collective-permute-start(bf16[80,4096]{1,0:T(8,128)(2,1)} %get-tuple-element.23), channel_id=1, source_target_pairs={{0,1},{1,0},{2,3},{3,2},{4,5},{5,4},{6,7},{7,6},{8,9},{9,8},{10,11... | collective-permute-start | bytes 1966088 | tf_op jit(solution)/shard_map/ppermute | solution.py:291
  116.4 15.5 %collective-permute-start.10 = (bf16[2,16,8192]{2,1,0:T(8,128)(2,1)S(1)}, bf16[2,16,8192]{2,1,0:T(8,128)(2,1)S(1)}, u32[]{:S(2)}, u32[]{:S(2)}) collective-permute-start(bf16[2,16,8192]{2,1,0:T(8,128)(2,1)S(1)} %get-tuple-element.32), channel_id=1, source_target_pairs={{0,4},{4,8},{8,12},{12,0},{1,5},{5,9},{9,13},{13,1},{2,6},{6,10},{... | collective-permute-start | bytes 1572872 | tf_op jit(solution)/shard_map/ppermute | solution.py:281
  117.8 24.9 %collective-permute-start.8 = (bf16[2,16,8192]{2,1,0:T(8,128)(2,1)S(1)}, bf16[2,16,8192]{2,1,0:T(8,128)(2,1)S(1)}, u32[]{:S(2)}, u32[]{:S(2)}) collective-permute-start(bf16[2,16,8192]{2,1,0:T(8,128)(2,1)S(1)} %get-tuple-element.31), channel_id=1, source_target_pairs={{0,8},{4,12},{8,0},{12,4},{1,9},{5,13},{9,1},{13,5},{2,10},{6,14},... | collective-permute-start | bytes 1572872 | tf_op jit(solution)/shard_map/ppermute | solution.py:281
  120.6 22.2 %collective-permute-start.9 = (bf16[2,16,8192]{2,1,0:T(8,128)(2,1)S(1)}, bf16[2,16,8192]{2,1,0:T(8,128)(2,1)S(1)}, u32[]{:S(2)}, u32[]{:S(2)}) collective-permute-start(bf16[2,16,8192]{2,1,0:T(8,128)(2,1)S(1)} %get-tuple-element.33), channel_id=1, source_target_pairs={{0,12},{4,0},{8,4},{12,8},{1,13},{5,1},{9,5},{13,9},{2,14},{6,2},{... | collective-permute-start | bytes 1572872 | tf_op jit(solution)/shard_map/ppermute | solution.py:281
  143.2 6.5 %copy-start.7 = (f32[80,4096]{1,0:T(8,128)S(1)}, f32[80,4096]{1,0:T(8,128)}, u32[]{:S(2)}) copy-start(f32[80,4096]{1,0:T(8,128)} %copy-done.6) | copy-start | bytes 3932164
  144.0 21.2 %all-to-all-start.1 = ((bf16[16,2,64,128]{3,2,1,0:T(8,128)(2,1)}), bf16[16,2,64,128]{3,2,1,0:T(8,128)(2,1)S(1)}, u32[]{:S(2)}, u32[]{:S(2)}) async-start(bf16[16,2,64,128]{3,2,1,0:T(8,128)(2,1)} %copy.33), calls=%async_computation.1 | async-start | bytes 1048576 | tf_op jit(solution)/shard_map/all_to_all | solution.py:286
  149.7 2.2 %copy-start.5 = (f32[80,4096]{1,0:T(8,128)S(1)}, f32[80,4096]{1,0:T(8,128)}, u32[]{:S(2)}) copy-start(f32[80,4096]{1,0:T(8,128)} %copy-done.4) | copy-start | bytes 3932164

commit v2 on v1

v2 whole, which is shorter than its diff:
```python
import functools

import jax
import jax.numpy as jnp
from jax import lax
from jax.experimental import pallas as pl
from jax.experimental.pallas import tpu as pltpu
from jax.sharding import Mesh
from jax.sharding import PartitionSpec as P

SIDE = 64
LANES = 128
WIDTH = SIDE * LANES
UNITS = 2 * SIDE
TRIPLE = 3 * UNITS
HALF = 36
KEPT = 2 * HALF
ROWS = 16
TOKENS = 4 * ROWS
FAR = 16
SHIFTS = (2, 1, 3)
VMEM_BYTES = 14 * 1024 * 1024
COST_BYTES = 30_000
BF16 = jnp.bfloat16
F32 = jnp.float32
NT = (((1,), (1,)), ((), ()))


def call(kernel, outs, scratch, micros, *operands, space=pltpu.VMEM):
    return pl.pallas_call(
        kernel,
        out_shape=outs,
        in_specs=[pl.BlockSpec(memory_space=pltpu.VMEM)] * len(operands),
        out_specs=[pl.BlockSpec(memory_space=space)] * len(outs),
        scratch_shapes=scratch,
        compiler_params=pltpu.CompilerParams(vmem_limit_bytes=VMEM_BYTES),
        cost_estimate=pl.CostEstimate(
            flops=0, bytes_accessed=int(micros * COST_BYTES), transcendentals=0
        ),
    )(*operands)


def span(step, width):
    return pl.ds(pl.multiple_of(step * width, width), width)


def densify_wide_kernel(pick_ref, gate_ref, up_ref, wide_ref):
    def spread(step, carry):
        cols = span(step, 4 * SIDE)
        for matrix, blocks_ref in enumerate((gate_ref, up_ref)):
            first, second = (
                jnp.dot(
                    pick_ref[2 * matrix + unit],
                    blocks_ref[unit, :, cols],
                    preferred_element_type=F32,
                ).astype(BF16)
                for unit in range(2)
            )
            for inner in range(4):
                part = slice(inner * SIDE, (inner + 1) * SIDE)
                wide_ref[
                    span(step * 4 + inner, LANES), matrix * UNITS : (matrix + 1) * UNITS
                ] = jnp.concatenate([first[:, part], second[:, part]], axis=1)
        return carry

    lax.fori_loop(0, 16, spread, 0, unroll=2)


def densify_down_kernel(pick_ref, down_ref, dense_ref, strip_ref):
    for unit in range(2):

        def turn(step, carry, unit=unit):
            dense = jnp.dot(
                pick_ref[4 + unit],
                down_ref[unit, :, span(step, 256)],
                preferred_element_type=F32,
            )
            strip_ref[unit, span(step, 256), :] = dense.T
            return carry

        lax.fori_loop(0, 16, turn, 0, unroll=2)

    def gather(inner, carry):
        dense_ref[:, span(inner, LANES)] = jnp.concatenate(
            [strip_ref[unit, pl.ds(inner, SIDE, SIDE), :] for unit in range(2)], axis=0
        ).astype(BF16)
        return carry

    lax.fori_loop(0, SIDE, gather, 0, unroll=8)


def joined(pieces, cols):
    return jnp.concatenate([piece[:, cols] for piece in pieces], axis=0)


def put(first_ref, moved, cols, values):
    first_ref[:, cols] = values[:ROWS]
    for slot, ref in enumerate(moved):
        ref[:, cols] = values[(slot + 1) * ROWS : (slot + 2) * ROWS].astype(BF16)


def forward_kernel(*refs):
    pieces = refs[:4]
    wides, downs = refs[4:6], refs[6:8]
    both_ref, hidden_ref, low_ref, high_ref, first_ref, *moved = refs[8:]

    def project(step, totals):
        cols = span(step, 1024)
        rows = joined(pieces, cols)
        return tuple(
            total + jnp.dot(rows, wide_ref[cols, :], preferred_element_type=F32)
            for total, wide_ref in zip(totals, wides)
        )

    zeros = jnp.zeros((TOKENS, 2 * UNITS), F32)
    totals = lax.fori_loop(0, 8, project, (zeros, zeros), unroll=2)
    hidden = []
    for core, both in enumerate(totals):
        both_ref[core] = both
        gate, upper = both[:, :UNITS], both[:, UNITS:]
        hidden.append((gate * jax.nn.sigmoid(gate) * upper).astype(BF16))
    hidden = jnp.concatenate(hidden, axis=1)
    hidden_ref[...] = hidden

    def outward(step, carry):
        cols = span(step, 512)
        weights = jnp.concatenate([down_ref[:, cols] for down_ref in downs], axis=0)
        put(first_ref, moved, cols, jnp.dot(hidden, weights, preferred_element_type=F32))
        low_ref[:, cols] = joined(pieces[:2], cols)
        high_ref[:, cols] = joined(pieces[2:], cols)
        return carry

    lax.fori_loop(0, 16, outward, 0, unroll=2)


def backward_kernel(*refs):
    pieces = refs[:4]
    wides, downs = refs[4:6], refs[6:8]
    both_ref, hidden_ref, near_ref, away_ref, first_ref, *moved, back_ref = refs[8:]

    def project(step, total):
        cols = span(step, 1024)
        weights = jnp.concatenate([down_ref[:, cols] for down_ref in downs], axis=0)
        return total + lax.dot_general(
            joined(pieces, cols), weights, NT, preferred_element_type=F32
        )

    hidden_grads = lax.fori_loop(0, 8, project, jnp.zeros((TOKENS, 2 * UNITS), F32), unroll=2)
    for core, (small_ref, start) in enumerate(((near_ref, 0), (away_ref, WIDTH))):
        hidden_grad = hidden_grads[:, core * UNITS : (core + 1) * UNITS]
        gate, upper = both_ref[core, :, :UNITS], both_ref[core, :, UNITS:]
        sigmoid_gate = jax.nn.sigmoid(gate)
        gate_cot = hidden_grad * upper * sigmoid_gate * (1.0 + gate * (1.0 - sigmoid_gate))
        up_cot = hidden_grad * (gate * sigmoid_gate)
        cots = jnp.concatenate([gate_cot, up_cot], axis=1).astype(BF16)
        back_ref[core] = cots
        small_ref[:, start : start + UNITS] = hidden_ref[:, core * UNITS : (core + 1) * UNITS]
        small_ref[:, start + UNITS : start + TRIPLE] = cots

    def outward(step, carry):
        cols = span(step, 512)
        values = sum(
            lax.dot_general(back_ref[core], wide_ref[cols, :], NT, preferred_element_type=F32)
            for core, wide_ref in enumerate(wides)
        )
        put(first_ref, moved, cols, values)
        away_ref[:, cols] = joined(pieces, cols)
        return carry

    lax.fori_loop(0, 16, outward, 0, unroll=2)


def turned(values):
    return jnp.concatenate(values, axis=0).astype(F32).T.astype(BF16)


def down_grad_kernel(*refs):
    pieces = (*refs[:4], refs[5])
    near_ref, away_ref, select_ref, keep_ref, send_ref, strip_ref = refs[4:]
    hidden = turned([near_ref[:, :UNITS], away_ref[:, WIDTH : WIDTH + UNITS]])

    def dense(step, carry):
        values = jnp.dot(
            hidden, joined(pieces, span(step, 512)), preferred_element_type=F32
        )
        for part in range(4):
            for unit in range(2):
                strip_ref[unit, pl.ds(step * 4 + part, SIDE, SIDE), :] = values[
                    unit * SIDE : (unit + 1) * SIDE, part * LANES : (part + 1) * LANES
                ]
        return carry

    lax.fori_loop(0, 16, dense, 0, unroll=2)

    def pick(step, carry):
        cols = span(step, 256)
        rows = jnp.concatenate([strip_ref[0, cols, :], strip_ref[1, cols, :]], axis=1)
        values = lax.dot_general(
            select_ref[...], rows.astype(BF16), NT, preferred_element_type=F32
        ).astype(BF16)
        keep_ref[:, cols] = values[:KEPT]
        send_ref[:, cols] = values[KEPT:]
        return carry

    lax.fori_loop(0, 16, pick, 0, unroll=2)


def paired(total_ref, cols, values):
    for entry in range(HALF):
        total_ref[entry, :, cols] = values[2 * entry : 2 * entry + 2]


def wide_grad_kernel(*refs):
    pieces = refs[:8]
    here_ref, far_ref, select_ref, gate_ref, up_ref, total_ref, done = refs[8:]
    cots = turned([here_ref[:, UNITS:], far_ref[:, UNITS:]])

    def step_of(step, carry):
        values = jnp.dot(
            cots, joined(pieces, span(step, 512)), preferred_element_type=F32
        ).astype(BF16)
        for matrix in range(2):
            rows = jnp.concatenate(
                [
                    jnp.concatenate(
                        [
                            values[
                                matrix * UNITS + unit * SIDE : matrix * UNITS + (unit + 1) * SIDE,
                                part * LANES : (part + 1) * LANES,
                            ]
                            for unit in range(2)
                        ],
                        axis=1,
                    )
                    for part in range(4)
                ],
                axis=0,
            )
            picked = lax.dot_general(select_ref[matrix], rows, NT, preferred_element_type=F32)
            paired(total_ref.at[matrix], span(step, 256), picked)
        return carry

    lax.fori_loop(0, 16, step_of, 0, unroll=2)
    copies = [
        pltpu.make_async_copy(total_ref.at[place], out_ref, done.at[place])
        for place, out_ref in enumerate((gate_ref, up_ref))
    ]
    for copy in copies:
        copy.start()
    for copy in copies:
        copy.wait()


def settle_kernel(keep_ref, send_ref, out_ref, total_ref, done):
    def settle(step, carry):
        cols = span(step, 512)
        paired(total_ref, cols, keep_ref[:, cols].astype(F32) + send_ref[:, cols].astype(F32))
        return carry

    lax.fori_loop(0, 8, settle, 0)
    copy = pltpu.make_async_copy(total_ref, out_ref, done)
    copy.start()
    copy.wait()


def ring(size, shift):
    return [(place, (place + shift) % size) for place in range(size)]


def per_device(
    activations, out_cotangent, gate_blocks, up_blocks, down_blocks, block_index, block_counts
):
    length = gate_blocks.shape[1]
    def shaped(dims, kind=BF16):
        return jax.ShapeDtypeStruct(dims, kind)

    def along(first):
        return [first] + [lax.ppermute(first, "y", ring(4, shift)) for shift in SHIFTS]

    def over(piece):
        return lax.ppermute(piece, "c", ring(2, 1))

    def swap(piece):
        return lax.ppermute(piece, "rep", ring(2, 1))

    def back(moved):
        return [
            lax.ppermute(part, "y", ring(4, -shift)) for part, shift in zip(moved, SHIFTS)
        ]

    def collect(first, moved):
        return (first + sum(part.astype(F32) for part in moved)).astype(BF16)

    tie = lax.optimization_barrier
    rows = jnp.stack([activations, out_cotangent], axis=1).reshape(1, 2, LANES, SIDE)
    rows = jnp.broadcast_to(jnp.swapaxes(rows, 2, 3), (FAR, 2, SIDE, LANES))
    rows = lax.all_to_all(rows, ("xh", "z"), 0, 0, tiled=True).reshape(FAR, 2, WIDTH)
    act_first, cot_first = rows[:, 0], rows[:, 1]

    live = jnp.arange(length)[None, None, :] < block_counts[:, :, None]
    places = jnp.where(live, block_index, -1)
    pick = (places[:, :, None, :] == jnp.arange(LANES)[None, None, :, None]).astype(BF16)
    pick = pick.reshape(6, LANES, length)
    wide = call(
        densify_wide_kernel,
        [shaped((WIDTH, 2 * UNITS))],
        [],
        3,
        pick[:4],
        gate_blocks,
        up_blocks,
    )[0]
    down = call(
        densify_down_kernel,
        [shaped((UNITS, WIDTH))],
        [pltpu.VMEM((2, SIDE * SIDE, LANES), F32)],
        8,
        pick,
        down_blocks,
    )[0]
    act_first, cot_first, wide, down, places = tie((act_first, cot_first, wide, down, places))

    acts = along(act_first)
    wides, downs = (wide, over(wide)), (down, over(down))
    halves = places.reshape(3, 2, 2, HALF)
    halves = jnp.where(lax.axis_index("rep") == 0, halves, halves[:, :, ::-1])
    halves = jnp.transpose(halves, (0, 2, 3, 1))
    goal = jnp.where(halves >= 0, halves + LANES * jnp.arange(2), -1)
    select = (goal.reshape(3, 2 * KEPT)[:, :, None] == jnp.arange(2 * LANES)).astype(BF16)
    acts, wides, downs, cot_first, select = tie((acts, wides, downs, cot_first, select))

    cot_pieces = along(cot_first)
    first, moved = shaped((ROWS, WIDTH), F32), [shaped((ROWS, WIDTH))] * 3
    lump = shaped((2 * ROWS, WIDTH))
    both, hidden, low, high, out_first, *out_moved = call(
        forward_kernel,
        [
            shaped((2, TOKENS, 2 * UNITS), F32),
            shaped((TOKENS, 2 * UNITS)),
            lump,
            lump,
            first,
            *moved,
        ],
        [],
        4,
        *acts,
        *wides,
        *downs,
    )
    cot_pieces, both, hidden, low, high, out_moved = tie(
        (cot_pieces, both, hidden, low, high, out_moved)
    )

    out_moved = back(out_moved)
    far_low = swap(low)
    over_low = over(low)
    near, away, grad_first, *grad_moved = call(
        backward_kernel,
        [shaped((TOKENS, TRIPLE)), shaped((TOKENS, WIDTH + TRIPLE)), first, *moved],
        [pltpu.VMEM((2, TOKENS, 2 * UNITS), BF16)],
        4,
        *cot_pieces,
        *wides,
        *downs,
        both,
        hidden,
    )
    out_moved, far_low, over_low, near, away, grad_moved, high = tie(
        (out_moved, far_low, over_low, near, away, grad_moved, high)
    )

    grad_moved = back(grad_moved)
    far_high = swap(high)
    away = over(away)
    here = jnp.concatenate([near, away[:, WIDTH:]], axis=0)
    far = swap(here)
    kept = sent = shaped((KEPT, SIDE * SIDE))
    keep_down, send_down = call(
        down_grad_kernel,
        [kept, sent],
        [pltpu.VMEM((2, SIDE * SIDE, LANES), F32)],
        7,
        *cot_pieces,
        near,
        away,
        select[2],
    )
    send_down, grad_moved, here, far, far_high = tie(
        (send_down, grad_moved, here, far, far_high)
    )

    come_down = swap(send_down)
    acts = [low, high, over_low, over(high), far_low, far_high, over(far_low), over(far_high)]
    total = jnp.stack([collect(out_first, out_moved), collect(grad_first, grad_moved)], axis=1)
    total = lax.all_to_all(
        total.reshape(FAR, 2, SIDE, LANES), ("xh", "z"), 0, 0, tiled=True
    )
    grad = shaped((HALF, 2, SIDE * SIDE), F32)
    gate_grad, up_grad = call(
        wide_grad_kernel,
        [grad, grad],
        [pltpu.VMEM((2, HALF, 2, SIDE * SIDE), F32), pltpu.SemaphoreType.DMA((2,))],
        7,
        *acts,
        here,
        far,
        select[:2, :KEPT],
        space=pltpu.HBM,
    )
    down_grad = call(
        settle_kernel,
        [grad],
        [pltpu.VMEM((HALF, 2, SIDE * SIDE), F32), pltpu.SemaphoreType.DMA],
        1.5,
        keep_down,
        come_down,
        space=pltpu.HBM,
    )[0]
    gate_grad, up_grad, down_grad = (
        jnp.swapaxes(grad, 0, 1) for grad in (gate_grad, up_grad, down_grad)
    )
    total = jnp.sum(total.astype(F32), axis=0)
    total = jnp.swapaxes(total, 1, 2).reshape(2, 1, WIDTH).astype(BF16)
    return (total[0], total[1], gate_grad, up_grad, down_grad)


def solution(mesh):
    fine = Mesh(mesh.devices.reshape(2, 8, 4, 2, 2), ("xh", "z", "y", "c", "rep"))
    blk = ("xh", "z", "y", "c")
    placed = (
        P((*blk, "rep"), None),
        P((*blk, "rep"), None),
        P(blk, None, None),
        P(blk, None, None),
        P(blk, None, None),
        P(None, blk, None),
        P(None, blk),
    )
    return jax.shard_map(
        per_device,
        mesh=fine,
        in_specs=placed,
        out_specs=(
            P((*blk, "rep"), None),
            P((*blk, "rep"), None),
            P(blk, "rep", None),
            P(blk, "rep", None),
            P(blk, "rep", None),
        ),
        check_vma=False,
    )
```

time: 170 us -> 135 us (0.79)
  blocking collectives: 27.1 us -> 0 us
  starting transfers between devices: 21.4 us -> 37.6 us
  waiting for transfers between devices: 48.2 us -> 33.3 us
  Pallas kernels: 45.8 us -> 39.4 us
  other arithmetic: 11.3 us -> 5.06 us
  local copies, waits for them, and re-layouts: 12.3 us -> 17.1 us
    all_to_all x1 -> x0, blocking collectives: 27.1 us -> none  [per_device(): lax.all_to_all(jnp.broadcast_to(rows, (FAR, 2, SIDE, LANES)), ('xh', 'z')...]
    all_to_all x1 -> x2, starting transfers between devices: 5.62 us -> 15.6 us  [the longest x1 10.2 us: per_device(): lax.all_to_all(rows, ('xh', 'z'), 0, 0, tiled=True).reshape(FAR, 2, WIDTH)]
    ppermute x14 -> x23, waiting for transfers between devices: 37.1 us -> 29.1 us  [the longest x6 12.2 us: along(): lax.ppermute(first, 'y', ring(4, shift))]
    all_to_all x1 -> x2, waiting for transfers between devices: 11.1 us -> 4.17 us  [the longest x1 4.17 us: per_device(): lax.all_to_all(rows, ('xh', 'z'), 0, 0, tiled=True).reshape(FAR, 2, WIDTH)]
    add x3 -> x0, other arithmetic: 6.7 us -> none  [settle(): return keep + other.astype(F32)]
    pallas_call x4 -> x7, Pallas kernels: 45.8 us -> 39.4 us  [call(): pl.pallas_call(kernel, out_shape=outs, in_specs=[pl.BlockSpec(memory_spac...]
    ppermute x14 -> x23, starting transfers between devices: 15.8 us -> 22 us  [the longest x6 8.25 us: back(): lax.ppermute(part, 'y', ring(4, -shift))]
    slice x4 -> x7, local copies, waits for them, and re-layouts: 0.24 us -> 2.24 us  [the longest x1 1.1 us: per_device(): act_first, cot_first = (rows[:, 0], rows[:, 1])]
  transfers between devices with their start and end apart: 15 -> 25, of which waited for: 6 -> 12; matrix products, arithmetic and copies ran while one was open for 7% -> 3% of each run, Pallas kernels for 20% -> 30%
where the time goes in v2:
time: 135 us; the launch traced here: 133 us
  Pallas kernels  39.4 us (29%)
  starting transfers between devices  37.6 us (28%)
  waiting for transfers between devices  33.3 us (25%)
  local copies, waits for them, and re-layouts  17.1 us (13%)
  other arithmetic  5.06 us (4%)
    pallas_call x7, Pallas kernels, call(): pl.pallas_call(kernel, out_shape=outs, in_specs=[pl.BlockSpec(memory_spac...  39.4 us
    ppermute x6, waiting for transfers between devices, along(): lax.ppermute(first, 'y', ring(4, shift))  12.2 us
    all_to_all x1, starting transfers between devices, per_device(): lax.all_to_all(rows, ('xh', 'z'), 0, 0, tiled=True).reshape(FAR, 2, WIDTH)  10.2 us
    unnamed x45, local copies, waits for them, and re-layouts  9.22 us
    ppermute x6, starting transfers between devices, back(): lax.ppermute(part, 'y', ring(4, -shift))  8.25 us
    ppermute x4, waiting for transfers between devices, swap(): return lax.ppermute(piece, 'rep', ring(2, 1))  7.58 us
    ppermute x6, starting transfers between devices, along(): lax.ppermute(first, 'y', ring(4, shift))  7.25 us
    ppermute x6, waiting for transfers between devices, back(): lax.ppermute(part, 'y', ring(4, -shift))  7.17 us
  transfers between devices with their start and end apart: 25, of which 12 were waited for; matrix products, arithmetic and copies ran while one was open for 3% of the time, Pallas kernels for 30%

profile of v2, /device:TPU:2, one launch (start us, length us, event | category | flops | bytes accessed | tf_op | source)
XLA Modules:
  0.0 133.5 jit_solution(10224416190910648654)
XLA Ops:
  3.7 10.2 %all-to-all-start = ((bf16[16,2,64,128]{3,2,1,0:T(8,128)(2,1)}), bf16[16,2,64,128]{3,2,1,0:T(8,128)(2,1)}, u32[]{:S(2)}, u32[]{:S(2)}) async-start(bf16[16,2,64,128]{3,2,1,0:T(8,128)(2,1)} %broadcast_in_dim.22), calls=%async_computation | async-start | bytes 1048576 | tf_op jit(solution)/shard_map/all_to_all | solution.py:297
  14.1 7.8 %shard_map.111.refs_6_ = bf16[128,8192]{1,0:T(8,128)(2,1)S(1)} custom-call(bf16[6,128,72]{2,1,0:T(8,128)(2,1)S(1)} %fusion.1.pick_ref, bf16[2,72,4096]{2,1,0:T(8,128)(2,1)S(1)} %copy-done.4), custom_call_target="tpu_custom_call" | custom-call | bytes 240000 | tf_op jit(solution)/shard_map/pallas_call | solution.py:30
  22.0 3.0 %shard_map.110.refs_4_ = bf16[8192,256]{1,0:T(8,128)(2,1)S(1)} custom-call(bf16[4,128,72]{2,1,0:T(8,128)(2,1)S(1)} %bitcast.33, bf16[2,72,4096]{2,1,0:T(8,128)(2,1)S(1)} %copy-done.2, bf16[2,72,4096]{2,1,0:T(8,128)(2,1)S(1)} %copy-done.3), custom_call_target="tpu_custom_call" | custom-call | bytes 90000 | tf_op jit(solution)/shard_map/pallas_call | solution.py:30
  25.0 1.9 %copy-done = bf16[8192,256]{1,0:T(8,128)(2,1)} copy-done((bf16[8192,256]{1,0:T(8,128)(2,1)}, bf16[8192,256]{1,0:T(8,128)(2,1)S(1)}, u32[]{:S(2)}) %copy-start) | copy-done | bytes 4194328
  26.9 4.2 %all-to-all-done = bf16[16,2,64,128]{3,2,1,0:T(8,128)(2,1)} async-done(((bf16[16,2,64,128]{3,2,1,0:T(8,128)(2,1)}), bf16[16,2,64,128]{3,2,1,0:T(8,128)(2,1)}, u32[]{:S(2)}, u32[]{:S(2)}) %all-to-all-start) | async-done | bytes 524320 | tf_op jit(solution)/shard_map/all_to_all | solution.py:297
  31.1 1.2 reshape.58
  34.6 3.0 %collective-permute-start.2 = (bf16[16,8192]{1,0:T(8,128)(2,1)S(1)}, bf16[16,8192]{1,0:T(8,128)(2,1)S(1)}, u32[]{:S(2)}, u32[]{:S(2)}) collective-permute-start(bf16[16,8192]{1,0:T(8,128)(2,1)S(1)} %get-tuple-element.72.refs_0_), channel_id=1, source_target_pairs={{0,12},{4,0},{8,4},{12,8},{1,13},{5,1},{9,5},{13,9},{2,14},{6,2},{... | collective-permute-start | bytes 786440 | tf_op jit(solution)/shard_map/ppermute | solution.py:278
  37.6 2.2 %collective-permute-start = (bf16[16,8192]{1,0:T(8,128)(2,1)S(1)}, bf16[16,8192]{1,0:T(8,128)(2,1)S(1)}, u32[]{:S(2)}, u32[]{:S(2)}) collective-permute-start(bf16[16,8192]{1,0:T(8,128)(2,1)S(1)} %get-tuple-element.72.refs_0_), channel_id=1, source_target_pairs={{0,8},{4,12},{8,0},{12,4},{1,9},{5,13},{9,1},{13,5},{2,10},{6,14},... | collective-permute-start | bytes 786440 | tf_op jit(solution)/shard_map/ppermute | solution.py:278
  41.9 7.2 %collective-permute-done.2.refs_3_ = bf16[16,8192]{1,0:T(8,128)(2,1)S(1)} collective-permute-done((bf16[16,8192]{1,0:T(8,128)(2,1)S(1)}, bf16[16,8192]{1,0:T(8,128)(2,1)S(1)}, u32[]{:S(2)}, u32[]{:S(2)}) %collective-permute-start.2) | collective-permute-done | bytes 262176 | tf_op jit(solution)/shard_map/ppermute | solution.py:278
  49.0 3.4 %collective-permute-done.1.refs_2_ = bf16[16,8192]{1,0:T(8,128)(2,1)S(1)} collective-permute-done((bf16[16,8192]{1,0:T(8,128)(2,1)S(1)}, bf16[16,8192]{1,0:T(8,128)(2,1)S(1)}, u32[]{:S(2)}, u32[]{:S(2)}) %collective-permute-start.1) | collective-permute-done | bytes 262176 | tf_op jit(solution)/shard_map/ppermute | solution.py:278
  54.2 1.7 %collective-permute-start.6 = (bf16[16,8192]{1,0:T(8,128)(2,1)S(1)}, bf16[16,8192]{1,0:T(8,128)(2,1)S(1)}, u32[]{:S(2)}, u32[]{:S(2)}) collective-permute-start(bf16[16,8192]{1,0:T(8,128)(2,1)S(1)} %get-tuple-element.93.refs_0_), channel_id=1, source_target_pairs={{0,4},{4,8},{8,12},{12,0},{1,5},{5,9},{9,13},{13,1},{2,6},{6,10},{... | collective-permute-start | bytes 786440 | tf_op jit(solution)/shard_map/ppermute | solution.py:278
  55.9 2.2 %copy-done.1 = bf16[8192,256]{1,0:T(8,128)(2,1)S(1)} copy-done((bf16[8192,256]{1,0:T(8,128)(2,1)S(1)}, bf16[8192,256]{1,0:T(8,128)(2,1)}, u32[]{:S(2)}) %copy-start.1) | copy-done | bytes 4194328
  60.0 6.5 %shard_map.112 = (f32[2,64,256]{2,1,0:T(8,128)S(1)}, bf16[64,256]{1,0:T(8,128)(2,1)S(1)}, bf16[32,8192]{1,0:T(8,128)(2,1)S(1)}, bf16[32,8192]{1,0:T(8,128)(2,1)S...) custom-call(bf16[16,8192]{1,0:T(8,128)(2,1)S(1)} %get-tuple-element., ...), custom_call_target="tpu_custom_call" | custom-call | bytes 120000 | tf_op jit(solution)/shard_map/pallas_call | solution.py:30
  66.6 1.6 %collective-permute-done.6.refs_2_ = bf16[16,8192]{1,0:T(8,128)(2,1)S(1)} collective-permute-done((bf16[16,8192]{1,0:T(8,128)(2,1)S(1)}, bf16[16,8192]{1,0:T(8,128)(2,1)S(1)}, u32[]{:S(2)}, u32[]{:S(2)}) %collective-permute-start.6) | collective-permute-done | bytes 262176 | tf_op jit(solution)/shard_map/ppermute | solution.py:278
  68.2 1.4 %collective-permute-start.11 = (bf16[32,8192]{1,0:T(8,128)(2,1)S(1)}, bf16[32,8192]{1,0:T(8,128)(2,1)S(1)}, u32[]{:S(2)}, u32[]{:S(2)}) collective-permute-start(bf16[32,8192]{1,0:T(8,128)(2,1)S(1)} %get-tuple-element.92.refs_0_), channel_id=1, source_target_pairs={{0,1},{1,0},{2,3},{3,2},{4,5},{5,4},{6,7},{7,6},{8,9},{9,8},{10,11... | collective-permute-start | bytes 1572872 | tf_op jit(solution)/shard_map/ppermute | solution.py:284
  69.6 2.1 %collective-permute-start.8 = (bf16[16,8192]{1,0:T(8,128)(2,1)S(1)}, bf16[16,8192]{1,0:T(8,128)(2,1)S(1)}, u32[]{:S(2)}, u32[]{:S(2)}) collective-permute-start(bf16[16,8192]{1,0:T(8,128)(2,1)S(1)} %get-tuple-element.89), channel_id=1, source_target_pairs={{0,8},{4,12},{8,0},{12,4},{1,9},{5,13},{9,1},{13,5},{2,10},{6,14},... | collective-permute-start | bytes 786440 | tf_op jit(solution)/shard_map/ppermute | solution.py:288
  71.7 1.5 %collective-permute-start.9 = (bf16[16,8192]{1,0:T(8,128)(2,1)S(1)}, bf16[16,8192]{1,0:T(8,128)(2,1)S(1)}, u32[]{:S(2)}, u32[]{:S(2)}) collective-permute-start(bf16[16,8192]{1,0:T(8,128)(2,1)S(1)} %get-tuple-element.90), channel_id=1, source_target_pairs={{0,12},{4,0},{8,4},{12,8},{1,13},{5,1},{9,5},{13,9},{2,14},{6,2},{... | collective-permute-start | bytes 786440 | tf_op jit(solution)/shard_map/ppermute | solution.py:288
  73.7 8.2 %shard_map.113 = (bf16[64,384]{1,0:T(8,128)(2,1)S(1)}, bf16[64,8576]{1,0:T(8,128)(2,1)S(1)}, f32[16,8192]{1,0:T(8,128)S(1)}, bf16[16,8192]{1,0:T(8,128)(2,1)S(1)...) custom-call(bf16[16,8192]{1,0:T(8,128)(2,1)S(1)} %get-tuple-element.93.refs_0_, ...), custom_call_target="tpu_custom_call" | custom-call | bytes 120000 | tf_op jit(solution)/shard_map/pallas_call | solution.py:30
  82.0 1.7 %collective-permute-done.9 = bf16[16,8192]{1,0:T(8,128)(2,1)S(1)} collective-permute-done((bf16[16,8192]{1,0:T(8,128)(2,1)S(1)}, bf16[16,8192]{1,0:T(8,128)(2,1)S(1)}, u32[]{:S(2)}, u32[]{:S(2)}) %collective-permute-start.9) | collective-permute-done | bytes 262176 | tf_op jit(solution)/shard_map/ppermute | solution.py:288
  83.7 1.5 %collective-permute-done.10 = bf16[16,8192]{1,0:T(8,128)(2,1)S(1)} collective-permute-done((bf16[16,8192]{1,0:T(8,128)(2,1)S(1)}, bf16[16,8192]{1,0:T(8,128)(2,1)S(1)}, u32[]{:S(2)}, u32[]{:S(2)}) %collective-permute-start.10) | collective-permute-done | bytes 262176 | tf_op jit(solution)/shard_map/ppermute | solution.py:288
  86.0 2.1 %collective-permute-start.14 = (bf16[16,8192]{1,0:T(8,128)(2,1)S(1)}, bf16[16,8192]{1,0:T(8,128)(2,1)S(1)}, u32[]{:S(2)}, u32[]{:S(2)}) collective-permute-start(bf16[16,8192]{1,0:T(8,128)(2,1)S(1)} %get-tuple-element.113), channel_id=1, source_target_pairs={{0,8},{4,12},{8,0},{12,4},{1,9},{5,13},{9,1},{13,5},{2,10},{6,14},... | collective-permute-start | bytes 786440 | tf_op jit(solution)/shard_map/ppermute | solution.py:288
  88.1 1.2 collective-permute-start.15
  90.2 1.5 %collective-permute-start.17 = (bf16[128,384]{1,0:T(8,128)(2,1)S(1)}, bf16[128,384]{1,0:T(8,128)(2,1)S(1)}, u32[]{:S(2)}, u32[]{:S(2)}) collective-permute-start(bf16[128,384]{1,0:T(8,128)(2,1)S(1)} %pad_maximum_fusion.1.refs_8_), channel_id=1, source_target_pairs={{0,1},{1,0},{2,3},{3,2},{4,5},{5,4},{6,7},{7,6},{8,9},{9,8},{10,11... | collective-permute-start | bytes 294920 | tf_op jit(solution)/shard_map/ppermute | solution.py:284
  91.9 5.7 %shard_map.114 = (bf16[72,4096]{1,0:T(8,128)(2,1)S(1)}, bf16[72,4096]{1,0:T(8,128)(2,1)S(1)}) custom-call(bf16[16,8192]{1,0:T(8,128)(2,1)S(1)} %get-tuple-element.93.refs_0_, bf16[16,8192]{1,0:T(8,128)(2,1)S(1)} %collective-permute-done.5.refs_1_, bf16[16,8192]{1,0:T(8,128)(2,1)S(1)} %collective-permute-done.6.refs_2_, ...), custom_call_target="tpu_custom_call" | custom-call | bytes 210000 | tf_op jit(solution)/shard_map/pallas_call | solution.py:30
  97.6 2.5 %collective-permute-done.15 = bf16[16,8192]{1,0:T(8,128)(2,1)S(1)} collective-permute-done((bf16[16,8192]{1,0:T(8,128)(2,1)S(1)}, bf16[16,8192]{1,0:T(8,128)(2,1)S(1)}, u32[]{:S(2)}, u32[]{:S(2)}) %collective-permute-start.15) | collective-permute-done | bytes 262176 | tf_op jit(solution)/shard_map/ppermute | solution.py:288
  100.1 1.5 %collective-permute-done.16 = bf16[16,8192]{1,0:T(8,128)(2,1)S(1)} collective-permute-done((bf16[16,8192]{1,0:T(8,128)(2,1)S(1)}, bf16[16,8192]{1,0:T(8,128)(2,1)S(1)}, u32[]{:S(2)}, u32[]{:S(2)}) %collective-permute-start.16) | collective-permute-done | bytes 262176 | tf_op jit(solution)/shard_map/ppermute | solution.py:288
  103.4 5.5 %all-to-all-start.1 = ((bf16[16,2,64,128]{3,2,1,0:T(8,128)(2,1)}), bf16[16,2,64,128]{3,2,1,0:T(8,128)(2,1)}, u32[]{:S(2)}, u32[]{:S(2)}) async-start(bf16[16,2,64,128]{3,2,1,0:T(8,128)(2,1)} %pad_maximum_fusion), calls=%async_computation.1 | async-start | bytes 1048576 | tf_op jit(solution)/shard_map/all_to_all | solution.py:396
  108.8 1.5 %collective-permute-start.22 = (bf16[72,4096]{1,0:T(8,128)(2,1)}, bf16[72,4096]{1,0:T(8,128)(2,1)S(1)}, u32[]{:S(2)}, u32[]{:S(2)}) collective-permute-start(bf16[72,4096]{1,0:T(8,128)(2,1)} %copy-done.17), channel_id=1, source_target_pairs={{0,1},{1,0},{2,3},{3,2},{4,5},{5,4},{6,7},{7,6},{8,9},{9,8},{10,11... | collective-permute-start | bytes 1769480 | tf_op jit(solution)/shard_map/ppermute | solution.py:284
  111.8 1.9 %collective-permute-done.20.refs_6_ = bf16[32,8192]{1,0:T(8,128)(2,1)S(1)} collective-permute-done((bf16[32,8192]{1,0:T(8,128)(2,1)S(1)}, bf16[32,8192]{1,0:T(8,128)(2,1)S(1)}, u32[]{:S(2)}, u32[]{:S(2)}) %collective-permute-start.20) | collective-permute-done | bytes 524320 | tf_op jit(solution)/shard_map/ppermute | solution.py:281
  115.0 6.9 %shard_map.115 = (f32[36,2,4096]{2,1,0:T(2,128)}, f32[36,2,4096]{2,1,0:T(2,128)}) custom-call(bf16[32,8192]{1,0:T(8,128)(2,1)S(1)} %get-tuple-element.92.refs_0_, bf16[32,8192]{1,0:T(8,128)(2,1)S(1)} %copy-done.6, bf16[32,8192]{1,0:T(8,128)(2,1)S(1)} %copy-done.8, bf16[32,8192]{1,0:T(8,128)(2,1)S(1)} %collective-permute-done.19.refs_3_, ...), custom_call_target="tpu_custom_call" | custom-call | bytes 210000 | tf_op jit(solution)/shard_map/pallas_call | solution.py:30
  122.0 7.4 %collective-permute-done.22.send_ref = bf16[72,4096]{1,0:T(8,128)(2,1)S(1)} collective-permute-done((bf16[72,4096]{1,0:T(8,128)(2,1)}, bf16[72,4096]{1,0:T(8,128)(2,1)S(1)}, u32[]{:S(2)}, u32[]{:S(2)}) %collective-permute-start.22) | collective-permute-done | bytes 589856 | tf_op jit(solution)/shard_map/ppermute | solution.py:284
  129.4 1.3 shard_map.116
  (104 shorter events, 20.9 us)
Async XLA Ops:
  0.6 13.2 %copy-start.20 = (s32[3,2]{0,1:T(2,128)S(1)}, s32[3,2]{0,1:T(2,128)}, u32[]{:S(2)}) copy-start(s32[3,2]{0,1:T(2,128)} %param.13) | copy-start | bytes 76
  0.6 13.3 %copy-start.19 = (s32[3,2,72]{2,1,0:T(2,128)S(1)}, s32[3,2,72]{2,1,0:T(2,128)}, u32[]{:S(2)}) copy-start(s32[3,2,72]{2,1,0:T(2,128)} %param.12) | copy-start | bytes 5188
  0.7 13.5 %copy-start.4 = (bf16[2,72,4096]{2,1,0:T(8,128)(2,1)S(1)}, bf16[2,72,4096]{2,1,0:T(8,128)(2,1)}, u32[]{:S(2)}) copy-start(bf16[2,72,4096]{2,1,0:T(8,128)(2,1)} %down_ref.1) | copy-start | bytes 3538948
  3.7 27.4 %all-to-all-start = ((bf16[16,2,64,128]{3,2,1,0:T(8,128)(2,1)}), bf16[16,2,64,128]{3,2,1,0:T(8,128)(2,1)}, u32[]{:S(2)}, u32[]{:S(2)}) async-start(bf16[16,2,64,128]{3,2,1,0:T(8,128)(2,1)} %broadcast_in_dim.22), calls=%async_computation | async-start | bytes 1048576 | tf_op jit(solution)/shard_map/all_to_all | solution.py:297
  34.0 19.9 %collective-permute-start.3 = (bf16[8192,256]{1,0:T(8,128)(2,1)}, bf16[8192,256]{1,0:T(8,128)(2,1)}, u32[]{:S(2)}, u32[]{:S(2)}) collective-permute-start(bf16[8192,256]{1,0:T(8,128)(2,1)} %copy-done), channel_id=1, source_target_pairs={{0,2},{2,0},{1,3},{3,1},{4,6},{6,4},{5,7},{7,5},{8,10},{10,8},{9,1... | collective-permute-start | bytes 12582920 | tf_op jit(solution)/shard_map/ppermute | solution.py:281
  34.1 19.8 %collective-permute-start.4 = (bf16[128,8192]{1,0:T(8,128)(2,1)S(1)}, bf16[128,8192]{1,0:T(8,128)(2,1)}, u32[]{:S(2)}, u32[]{:S(2)}) collective-permute-start(bf16[128,8192]{1,0:T(8,128)(2,1)S(1)} %shard_map.111.refs_6_), channel_id=1, source_target_pairs={{0,2},{2,0},{1,3},{3,1},{4,6},{6,4},{5,7},{7,5},{8,10},{10,8},{9,1... | collective-permute-start | bytes 6291464 | tf_op jit(solution)/shard_map/ppermute | solution.py:281
  34.6 14.5 %collective-permute-start.2 = (bf16[16,8192]{1,0:T(8,128)(2,1)S(1)}, bf16[16,8192]{1,0:T(8,128)(2,1)S(1)}, u32[]{:S(2)}, u32[]{:S(2)}) collective-permute-start(bf16[16,8192]{1,0:T(8,128)(2,1)S(1)} %get-tuple-element.72.refs_0_), channel_id=1, source_target_pairs={{0,12},{4,0},{8,4},{12,8},{1,13},{5,1},{9,5},{13,9},{2,14},{6,2},{... | collective-permute-start | bytes 786440 | tf_op jit(solution)/shard_map/ppermute | solution.py:278
  37.6 14.9 %collective-permute-start.1 = (bf16[16,8192]{1,0:T(8,128)(2,1)S(1)}, bf16[16,8192]{1,0:T(8,128)(2,1)S(1)}, u32[]{:S(2)}, u32[]{:S(2)}) collective-permute-start(bf16[16,8192]{1,0:T(8,128)(2,1)S(1)} %get-tuple-element.72.refs_0_), channel_id=1, source_target_pairs={{0,4},{4,8},{8,12},{12,0},{1,5},{5,9},{9,13},{13,1},{2,6},{6,10},{... | collective-permute-start | bytes 786440 | tf_op jit(solution)/shard_map/ppermute | solution.py:278
  37.6 15.6 %collective-permute-start = (bf16[16,8192]{1,0:T(8,128)(2,1)S(1)}, bf16[16,8192]{1,0:T(8,128)(2,1)S(1)}, u32[]{:S(2)}, u32[]{:S(2)}) collective-permute-start(bf16[16,8192]{1,0:T(8,128)(2,1)S(1)} %get-tuple-element.72.refs_0_), channel_id=1, source_target_pairs={{0,8},{4,12},{8,0},{12,4},{1,9},{5,13},{9,1},{13,5},{2,10},{6,14},... | collective-permute-start | bytes 786440 | tf_op jit(solution)/shard_map/ppermute | solution.py:278
  41.9 44.1 %copy-start.18 = (bf16[3,144,256]{2,1,0:T(8,128)(2,1)}, bf16[3,144,256]{2,1,0:T(8,128)(2,1)S(1)}, u32[]{:S(2)}) copy-start(bf16[3,144,256]{2,1,0:T(8,128)(2,1)S(1)} %fusion) | copy-start | bytes 663556
  53.9 12.7 %collective-permute-start.7 = (bf16[16,8192]{1,0:T(8,128)(2,1)S(1)}, bf16[16,8192]{1,0:T(8,128)(2,1)S(1)}, u32[]{:S(2)}, u32[]{:S(2)}) collective-permute-start(bf16[16,8192]{1,0:T(8,128)(2,1)S(1)} %get-tuple-element.93.refs_0_), channel_id=1, source_target_pairs={{0,12},{4,0},{8,4},{12,8},{1,13},{5,1},{9,5},{13,9},{2,14},{6,2},{... | collective-permute-start | bytes 786440 | tf_op jit(solution)/shard_map/ppermute | solution.py:278
  54.2 14.0 %collective-permute-start.6 = (bf16[16,8192]{1,0:T(8,128)(2,1)S(1)}, bf16[16,8192]{1,0:T(8,128)(2,1)S(1)}, u32[]{:S(2)}, u32[]{:S(2)}) collective-permute-start(bf16[16,8192]{1,0:T(8,128)(2,1)S(1)} %get-tuple-element.93.refs_0_), channel_id=1, source_target_pairs={{0,4},{4,8},{8,12},{12,0},{1,5},{5,9},{9,13},{13,1},{2,6},{6,10},{... | collective-permute-start | bytes 786440 | tf_op jit(solution)/shard_map/ppermute | solution.py:278
  55.9 12.3 %collective-permute-start.5 = (bf16[16,8192]{1,0:T(8,128)(2,1)S(1)}, bf16[16,8192]{1,0:T(8,128)(2,1)S(1)}, u32[]{:S(2)}, u32[]{:S(2)}) collective-permute-start(bf16[16,8192]{1,0:T(8,128)(2,1)S(1)} %get-tuple-element.93.refs_0_), channel_id=1, source_target_pairs={{0,8},{4,12},{8,0},{12,4},{1,9},{5,13},{9,1},{13,5},{2,10},{6,14},... | collective-permute-start | bytes 786440 | tf_op jit(solution)/shard_map/ppermute | solution.py:278
  66.5 18.8 %copy-start.5 = (bf16[32,8192]{1,0:T(8,128)(2,1)}, bf16[32,8192]{1,0:T(8,128)(2,1)S(1)}, u32[]{:S(2)}) copy-start(bf16[32,8192]{1,0:T(8,128)(2,1)S(1)} %get-tuple-element.116.refs_1_) | copy-start | bytes 1572868
  68.2 17.0 %collective-permute-start.12 = (bf16[32,8192]{1,0:T(8,128)(2,1)S(1)}, bf16[32,8192]{1,0:T(8,128)(2,1)S(1)}, u32[]{:S(2)}, u32[]{:S(2)}) collective-permute-start(bf16[32,8192]{1,0:T(8,128)(2,1)S(1)} %get-tuple-element.92.refs_0_), channel_id=1, source_target_pairs={{0,2},{2,0},{1,3},{3,1},{4,6},{6,4},{5,7},{7,5},{8,10},{10,8},{9,1... | collective-permute-start | bytes 1572872 | tf_op jit(solution)/shard_map/ppermute | solution.py:281
  68.2 17.0 %collective-permute-start.11 = (bf16[32,8192]{1,0:T(8,128)(2,1)S(1)}, bf16[32,8192]{1,0:T(8,128)(2,1)S(1)}, u32[]{:S(2)}, u32[]{:S(2)}) collective-permute-start(bf16[32,8192]{1,0:T(8,128)(2,1)S(1)} %get-tuple-element.92.refs_0_), channel_id=1, source_target_pairs={{0,1},{1,0},{2,3},{3,2},{4,5},{5,4},{6,7},{7,6},{8,9},{9,8},{10,11... | collective-permute-start | bytes 1572872 | tf_op jit(solution)/shard_map/ppermute | solution.py:284
  69.6 12.4 %collective-permute-start.8 = (bf16[16,8192]{1,0:T(8,128)(2,1)S(1)}, bf16[16,8192]{1,0:T(8,128)(2,1)S(1)}, u32[]{:S(2)}, u32[]{:S(2)}) collective-permute-start(bf16[16,8192]{1,0:T(8,128)(2,1)S(1)} %get-tuple-element.89), channel_id=1, source_target_pairs={{0,8},{4,12},{8,0},{12,4},{1,9},{5,13},{9,1},{13,5},{2,10},{6,14},... | collective-permute-start | bytes 786440 | tf_op jit(solution)/shard_map/ppermute | solution.py:288
  71.7 12.0 %collective-permute-start.9 = (bf16[16,8192]{1,0:T(8,128)(2,1)S(1)}, bf16[16,8192]{1,0:T(8,128)(2,1)S(1)}, u32[]{:S(2)}, u32[]{:S(2)}) collective-permute-start(bf16[16,8192]{1,0:T(8,128)(2,1)S(1)} %get-tuple-element.90), channel_id=1, source_target_pairs={{0,12},{4,0},{8,4},{12,8},{1,13},{5,1},{9,5},{13,9},{2,14},{6,2},{... | collective-permute-start | bytes 786440 | tf_op jit(solution)/shard_map/ppermute | solution.py:288
  73.2 12.0 %collective-permute-start.10 = (bf16[16,8192]{1,0:T(8,128)(2,1)S(1)}, bf16[16,8192]{1,0:T(8,128)(2,1)S(1)}, u32[]{:S(2)}, u32[]{:S(2)}) collective-permute-start(bf16[16,8192]{1,0:T(8,128)(2,1)S(1)} %get-tuple-element.91), channel_id=1, source_target_pairs={{0,4},{4,8},{8,12},{12,0},{1,5},{5,9},{9,13},{13,1},{2,6},{6,10},{... | collective-permute-start | bytes 786440 | tf_op jit(solution)/shard_map/ppermute | solution.py:288
  85.2 4.9 %collective-permute-start.13 = (bf16[64,8576]{1,0:T(8,128)(2,1)S(1)}, bf16[64,8576]{1,0:T(8,128)(2,1)S(1)}, u32[]{:S(2)}, u32[]{:S(2)}) collective-permute-start(bf16[64,8576]{1,0:T(8,128)(2,1)S(1)} %get-tuple-element.110), channel_id=1, source_target_pairs={{0,2},{2,0},{1,3},{3,1},{4,6},{6,4},{5,7},{7,5},{8,10},{10,8},{9,1... | collective-permute-start | bytes 3293192 | tf_op jit(solution)/shard_map/ppermute | solution.py:281
  85.3 16.3 %collective-permute-start.18 = (bf16[32,8192]{1,0:T(8,128)(2,1)S(1)}, bf16[32,8192]{1,0:T(8,128)(2,1)S(1)}, u32[]{:S(2)}, u32[]{:S(2)}) collective-permute-start(bf16[32,8192]{1,0:T(8,128)(2,1)S(1)} %get-tuple-element.116.refs_1_), channel_id=1, source_target_pairs={{0,1},{1,0},{2,3},{3,2},{4,5},{5,4},{6,7},{7,6},{8,9},{9,8},{10,11... | collective-permute-start | bytes 1572872 | tf_op jit(solution)/shard_map/ppermute | solution.py:284
  86.0 11.6 %collective-permute-start.14 = (bf16[16,8192]{1,0:T(8,128)(2,1)S(1)}, bf16[16,8192]{1,0:T(8,128)(2,1)S(1)}, u32[]{:S(2)}, u32[]{:S(2)}) collective-permute-start(bf16[16,8192]{1,0:T(8,128)(2,1)S(1)} %get-tuple-element.113), channel_id=1, source_target_pairs={{0,8},{4,12},{8,0},{12,4},{1,9},{5,13},{9,1},{13,5},{2,10},{6,14},... | collective-permute-start | bytes 786440 | tf_op jit(solution)/shard_map/ppermute | solution.py:288
  88.1 12.0 %collective-permute-start.15 = (bf16[16,8192]{1,0:T(8,128)(2,1)S(1)}, bf16[16,8192]{1,0:T(8,128)(2,1)S(1)}, u32[]{:S(2)}, u32[]{:S(2)}) collective-permute-start(bf16[16,8192]{1,0:T(8,128)(2,1)S(1)} %get-tuple-element.114), channel_id=1, source_target_pairs={{0,12},{4,0},{8,4},{12,8},{1,13},{5,1},{9,5},{13,9},{2,14},{6,2},{... | collective-permute-start | bytes 786440 | tf_op jit(solution)/shard_map/ppermute | solution.py:288
  89.3 12.3 %collective-permute-start.16 = (bf16[16,8192]{1,0:T(8,128)(2,1)S(1)}, bf16[16,8192]{1,0:T(8,128)(2,1)S(1)}, u32[]{:S(2)}, u32[]{:S(2)}) collective-permute-start(bf16[16,8192]{1,0:T(8,128)(2,1)S(1)} %get-tuple-element.115), channel_id=1, source_target_pairs={{0,4},{4,8},{8,12},{12,0},{1,5},{5,9},{9,13},{13,1},{2,6},{6,10},{... | collective-permute-start | bytes 786440 | tf_op jit(solution)/shard_map/ppermute | solution.py:288
  90.2 11.6 %collective-permute-start.17 = (bf16[128,384]{1,0:T(8,128)(2,1)S(1)}, bf16[128,384]{1,0:T(8,128)(2,1)S(1)}, u32[]{:S(2)}, u32[]{:S(2)}) collective-permute-start(bf16[128,384]{1,0:T(8,128)(2,1)S(1)} %pad_maximum_fusion.1.refs_8_), channel_id=1, source_target_pairs={{0,1},{1,0},{2,3},{3,2},{4,5},{5,4},{6,7},{7,6},{8,9},{9,8},{10,11... | collective-permute-start | bytes 294920 | tf_op jit(solution)/shard_map/ppermute | solution.py:284
  102.4 7.9 %copy-start.6 = (bf16[32,8192]{1,0:T(8,128)(2,1)S(1)}, bf16[32,8192]{1,0:T(8,128)(2,1)}, u32[]{:S(2)}) copy-start(bf16[32,8192]{1,0:T(8,128)(2,1)} %copy-done.5) | copy-start | bytes 1572868
  102.5 11.5 %copy-start.8 = (bf16[32,8192]{1,0:T(8,128)(2,1)S(1)}, bf16[32,8192]{1,0:T(8,128)(2,1)}, u32[]{:S(2)}) copy-start(bf16[32,8192]{1,0:T(8,128)(2,1)} %copy-done.7) | copy-start | bytes 1572868
  103.4 27.3 %all-to-all-start.1 = ((bf16[16,2,64,128]{3,2,1,0:T(8,128)(2,1)}), bf16[16,2,64,128]{3,2,1,0:T(8,128)(2,1)}, u32[]{:S(2)}, u32[]{:S(2)}) async-start(bf16[16,2,64,128]{3,2,1,0:T(8,128)(2,1)} %pad_maximum_fusion), calls=%async_computation.1 | async-start | bytes 1048576 | tf_op jit(solution)/shard_map/all_to_all | solution.py:396
  108.8 20.5 %collective-permute-start.22 = (bf16[72,4096]{1,0:T(8,128)(2,1)}, bf16[72,4096]{1,0:T(8,128)(2,1)S(1)}, u32[]{:S(2)}, u32[]{:S(2)}) collective-permute-start(bf16[72,4096]{1,0:T(8,128)(2,1)} %copy-done.17), channel_id=1, source_target_pairs={{0,1},{1,0},{2,3},{3,2},{4,5},{5,4},{6,7},{7,6},{8,9},{9,8},{10,11... | collective-permute-start | bytes 1769480 | tf_op jit(solution)/shard_map/ppermute | solution.py:284
  110.3 3.4 %collective-permute-start.19 = (bf16[32,8192]{1,0:T(8,128)(2,1)S(1)}, bf16[32,8192]{1,0:T(8,128)(2,1)S(1)}, u32[]{:S(2)}, u32[]{:S(2)}) collective-permute-start(bf16[32,8192]{1,0:T(8,128)(2,1)S(1)} %copy-done.6), channel_id=1, source_target_pairs={{0,2},{2,0},{1,3},{3,1},{4,6},{6,4},{5,7},{7,5},{8,10},{10,8},{9,1... | collective-permute-start | bytes 1572872 | tf_op jit(solution)/shard_map/ppermute | solution.py:281
  110.4 3.4 %collective-permute-start.20 = (bf16[32,8192]{1,0:T(8,128)(2,1)S(1)}, bf16[32,8192]{1,0:T(8,128)(2,1)S(1)}, u32[]{:S(2)}, u32[]{:S(2)}) collective-permute-start(bf16[32,8192]{1,0:T(8,128)(2,1)S(1)} %copy-done.10), channel_id=1, source_target_pairs={{0,2},{2,0},{1,3},{3,1},{4,6},{6,4},{5,7},{7,5},{8,10},{10,8},{9,1... | collective-permute-start | bytes 1572872 | tf_op jit(solution)/shard_map/ppermute | solution.py:281
  110.9 3.1 %collective-permute-start.21 = (bf16[32,8192]{1,0:T(8,128)(2,1)}, bf16[32,8192]{1,0:T(8,128)(2,1)S(1)}, u32[]{:S(2)}, u32[]{:S(2)}) collective-permute-start(bf16[32,8192]{1,0:T(8,128)(2,1)} %copy-done.11), channel_id=1, source_target_pairs={{0,2},{2,0},{1,3},{3,1},{4,6},{6,4},{5,7},{7,5},{8,10},{10,8},{9,1... | collective-permute-start | bytes 1572872 | tf_op jit(solution)/shard_map/ppermute | solution.py:281
  (14 other events, 51.2 us)

commit v3 on v2

--- a/solution.py
+++ b/solution.py
@@ -20,23 +20,25 @@
 FAR = 16
 SHIFTS = (2, 1, 3)
 VMEM_BYTES = 14 * 1024 * 1024
-COST_BYTES = 30_000
+SMALL_BYTES = 8 * 1024 * 1024
 BF16 = jnp.bfloat16
 F32 = jnp.float32
 NT = (((1,), (1,)), ((), ()))
 
 
-def call(kernel, outs, scratch, micros, *operands, space=pltpu.VMEM):
+def call(kernel, outs, scratch, *operands, inside=(), space=pltpu.VMEM, limit=VMEM_BYTES):
+    inside = dict(inside)
     return pl.pallas_call(
         kernel,
         out_shape=outs,
-        in_specs=[pl.BlockSpec(memory_space=pltpu.VMEM)] * len(operands),
+        in_specs=[
+            pl.BlockSpec(memory_space=inside.get(place, pltpu.VMEM))
+            for place in range(len(operands))
+        ],
         out_specs=[pl.BlockSpec(memory_space=space)] * len(outs),
         scratch_shapes=scratch,
-        compiler_params=pltpu.CompilerParams(vmem_limit_bytes=VMEM_BYTES),
-        cost_estimate=pl.CostEstimate(
-            flops=0, bytes_accessed=int(micros * COST_BYTES), transcendentals=0
-        ),
+        compiler_params=pltpu.CompilerParams(vmem_limit_bytes=limit),
+        cost_estimate=pl.CostEstimate(flops=0, bytes_accessed=100_000, transcendentals=0),
     )(*operands)
 
 
@@ -44,13 +46,78 @@
     return pl.ds(pl.multiple_of(step * width, width), width)
 
 
-def densify_wide_kernel(pick_ref, gate_ref, up_ref, wide_ref):
+def spread_kernel(act_ref, cot_ref, out_ref, strip_ref):
+    for which, row_ref in enumerate((act_ref, cot_ref)):
+        row = row_ref[...].astype(F32)
+        for part in range(SIDE):
+            strip_ref[part : part + 1, :] = row[:, part * LANES : (part + 1) * LANES]
+        turned_row = strip_ref[...].T
+        tile = jnp.concatenate([turned_row[:SIDE], turned_row[SIDE:]], axis=1).astype(BF16)
+        for place in range(FAR):
+            out_ref[place, which] = tile
+
+
+def gather_kernel(tiles_ref, act_ref, cot_ref, strip_ref):
+    for which, out_ref in enumerate((act_ref, cot_ref)):
+        for place in range(FAR):
+            strip_ref[which, place * SIDE : (place + 1) * SIDE, :] = tiles_ref[
+                place, which
+            ].astype(F32)
+        for inner in range(SIDE):
+            out_ref[:, inner * LANES : (inner + 1) * LANES] = strip_ref[
+                which, pl.ds(inner, FAR, SIDE), :
+            ].astype(BF16)
+
+
+def collect_kernel(*refs):
+    *parts, tiles_ref, strip_ref = refs
+    for which in range(2):
+        first_ref, *moved = parts[4 * which : 4 * which + 4]
+        for inner in range(SIDE):
+            cols = slice(inner * LANES, (inner + 1) * LANES)
+            total = first_ref[:, cols]
+            for ref in moved:
+                total = total + ref[:, cols].astype(F32)
+            strip_ref[which, pl.ds(inner, FAR, SIDE), :] = total
+        for place in range(FAR):
+            tiles_ref[place, which] = strip_ref[
+                which, place * SIDE : (place + 1) * SIDE, :
+            ].astype(BF16)
+
+
+def finish_kernel(total_ref, out_ref, grad_ref, strip_ref):
+    for which, row_ref in enumerate((out_ref, grad_ref)):
+        total = total_ref[0, which].astype(F32)
+        for place in range(1, FAR):
+            total = total + total_ref[place, which].astype(F32)
+        strip_ref[...] = jnp.concatenate([total[:, :SIDE], total[:, SIDE:]], axis=0).T
+        for part in range(SIDE):
+            row_ref[:, part * LANES : (part + 1) * LANES] = strip_ref[
+                part : part + 1, :
+            ].astype(BF16)
+
+
+def lane_of(block):
+    return (block & 1) * SIDE + (block >> 1)
+
+
+def one_hot(index_ref, count_ref, matrix, unit):
+    entries = index_ref[matrix, unit : unit + 1, :]
+    shape = (LANES, entries.shape[1])
+    rows = lax.broadcasted_iota(jnp.int32, shape, 0)
+    live = lax.broadcasted_iota(jnp.int32, shape, 1) < count_ref[matrix, unit]
+    return jnp.where((rows == lane_of(entries)) & live, 1.0, 0.0).astype(BF16)
+
+
+def densify_wide_kernel(index_ref, count_ref, gate_ref, up_ref, wide_ref):
+    picks = [[one_hot(index_ref, count_ref, matrix, unit) for unit in range(2)] for matrix in range(2)]
+
     def spread(step, carry):
         cols = span(step, 4 * SIDE)
         for matrix, blocks_ref in enumerate((gate_ref, up_ref)):
             first, second = (
                 jnp.dot(
-                    pick_ref[2 * matrix + unit],
+                    picks[matrix][unit],
                     blocks_ref[unit, :, cols],
                     preferred_element_type=F32,
                 ).astype(BF16)
@@ -66,12 +133,13 @@
     lax.fori_loop(0, 16, spread, 0, unroll=2)
 
 
-def densify_down_kernel(pick_ref, down_ref, dense_ref, strip_ref):
+def densify_down_kernel(index_ref, count_ref, down_ref, dense_ref, strip_ref):
     for unit in range(2):
-
-        def turn(step, carry, unit=unit):
+        pick = one_hot(index_ref, count_ref, 2, unit)
+
+        def turn(step, carry, unit=unit, pick=pick):
             dense = jnp.dot(
-                pick_ref[4 + unit],
+                pick,
                 down_ref[unit, :, span(step, 256)],
                 preferred_element_type=F32,
             )
@@ -288,46 +356,52 @@
             lax.ppermute(part, "y", ring(4, -shift)) for part, shift in zip(moved, SHIFTS)
         ]
 
-    def collect(first, moved):
-        return (first + sum(part.astype(F32) for part in moved)).astype(BF16)
-
     tie = lax.optimization_barrier
-    rows = jnp.stack([activations, out_cotangent], axis=1).reshape(1, 2, LANES, SIDE)
-    rows = jnp.broadcast_to(jnp.swapaxes(rows, 2, 3), (FAR, 2, SIDE, LANES))
-    rows = lax.all_to_all(rows, ("xh", "z"), 0, 0, tiled=True).reshape(FAR, 2, WIDTH)
-    act_first, cot_first = rows[:, 0], rows[:, 1]
-
-    live = jnp.arange(length)[None, None, :] < block_counts[:, :, None]
-    places = jnp.where(live, block_index, -1)
-    pick = (places[:, :, None, :] == jnp.arange(LANES)[None, None, :, None]).astype(BF16)
-    pick = pick.reshape(6, LANES, length)
+    numbers = (block_index, block_counts)
+    strips = pltpu.VMEM((2, SIDE * FAR, LANES), F32)
+
+    def exchange(tiles):
+        return lax.all_to_all(tiles, ("xh", "z"), 0, 0, tiled=True)
+
+    tiles = call(
+        spread_kernel,
+        [shaped((FAR, 2, SIDE, LANES))],
+        [pltpu.VMEM((SIDE, LANES), F32)],
+        activations,
+        out_cotangent,
+        limit=SMALL_BYTES,
+    )[0]
+    tiles = exchange(tiles)
+    down = call(
+        densify_down_kernel,
+        [shaped((UNITS, WIDTH))],
+        [pltpu.VMEM((2, SIDE * SIDE, LANES), F32)],
+        *numbers,
+        down_blocks,
+        inside={1: pltpu.SMEM},
+    )[0]
     wide = call(
         densify_wide_kernel,
         [shaped((WIDTH, 2 * UNITS))],
         [],
-        3,
-        pick[:4],
+        *numbers,
         gate_blocks,
         up_blocks,
+        inside={1: pltpu.SMEM},
     )[0]
-    down = call(
-        densify_down_kernel,
-        [shaped((UNITS, WIDTH))],
-        [pltpu.VMEM((2, SIDE * SIDE, LANES), F32)],
-        8,
-        pick,
-        down_blocks,
-    )[0]
-    act_first, cot_first, wide, down, places = tie((act_first, cot_first, wide, down, places))
-
+    tiles, wide, down, block_index = tie((tiles, wide, down, block_index))
+    act_first, cot_first = call(
+        gather_kernel, [shaped((ROWS, WIDTH))] * 2, [strips], tiles, limit=SMALL_BYTES
+    )
     acts = along(act_first)
     wides, downs = (wide, over(wide)), (down, over(down))
+    live = jnp.arange(length)[None, None, :] < block_counts[:, :, None]
+    places = jnp.where(live, lane_of(block_index), -1)
     halves = places.reshape(3, 2, 2, HALF)
     halves = jnp.where(lax.axis_index("rep") == 0, halves, halves[:, :, ::-1])
     halves = jnp.transpose(halves, (0, 2, 3, 1))
     goal = jnp.where(halves >= 0, halves + LANES * jnp.arange(2), -1)
     select = (goal.reshape(3, 2 * KEPT)[:, :, None] == jnp.arange(2 * LANES)).astype(BF16)
-    acts, wides, downs, cot_first, select = tie((acts, wides, downs, cot_first, select))
 
     cot_pieces = along(cot_first)
     first, moved = shaped((ROWS, WIDTH), F32), [shaped((ROWS, WIDTH))] * 3
@@ -343,7 +417,6 @@
             *moved,
         ],
         [],
-        4,
         *acts,
         *wides,
         *downs,
@@ -354,21 +427,17 @@
 
     out_moved = back(out_moved)
     far_low = swap(low)
-    over_low = over(low)
     near, away, grad_first, *grad_moved = call(
         backward_kernel,
         [shaped((TOKENS, TRIPLE)), shaped((TOKENS, WIDTH + TRIPLE)), first, *moved],
         [pltpu.VMEM((2, TOKENS, 2 * UNITS), BF16)],
-        4,
         *cot_pieces,
         *wides,
         *downs,
         both,
         hidden,
     )
-    out_moved, far_low, over_low, near, away, grad_moved, high = tie(
-        (out_moved, far_low, over_low, near, away, grad_moved, high)
-    )
+    out_moved, far_low, near, away, high = tie((out_moved, far_low, near, away, high))
 
     grad_moved = back(grad_moved)
     far_high = swap(high)
@@ -380,7 +449,6 @@
         down_grad_kernel,
         [kept, sent],
         [pltpu.VMEM((2, SIDE * SIDE, LANES), F32)],
-        7,
         *cot_pieces,
         near,
         away,
@@ -391,17 +459,24 @@
     )
 
     come_down = swap(send_down)
-    acts = [low, high, over_low, over(high), far_low, far_high, over(far_low), over(far_high)]
-    total = jnp.stack([collect(out_first, out_moved), collect(grad_first, grad_moved)], axis=1)
-    total = lax.all_to_all(
-        total.reshape(FAR, 2, SIDE, LANES), ("xh", "z"), 0, 0, tiled=True
+    acts = [low, high, over(low), over(high), far_low, far_high, over(far_low), over(far_high)]
+    tiles = exchange(
+        call(
+            collect_kernel,
+            [shaped((FAR, 2, SIDE, LANES))],
+            [strips],
+            out_first,
+            *out_moved,
+            grad_first,
+            *grad_moved,
+            limit=SMALL_BYTES,
+        )[0]
     )
     grad = shaped((HALF, 2, SIDE * SIDE), F32)
     gate_grad, up_grad = call(
         wide_grad_kernel,
         [grad, grad],
         [pltpu.VMEM((2, HALF, 2, SIDE * SIDE), F32), pltpu.SemaphoreType.DMA((2,))],
-        7,
         *acts,
         here,
         far,
@@ -412,7 +487,6 @@
         settle_kernel,
         [grad],
         [pltpu.VMEM((HALF, 2, SIDE * SIDE), F32), pltpu.SemaphoreType.DMA],
-        1.5,
         keep_down,
         come_down,
         space=pltpu.HBM,
@@ -420,9 +494,14 @@
     gate_grad, up_grad, down_grad = (
         jnp.swapaxes(grad, 0, 1) for grad in (gate_grad, up_grad, down_grad)
     )
-    total = jnp.sum(total.astype(F32), axis=0)
-    total = jnp.swapaxes(total, 1, 2).reshape(2, 1, WIDTH).astype(BF16)
-    return (total[0], total[1], gate_grad, up_grad, down_grad)
+    layer_out, input_grad = call(
+        finish_kernel,
+        [shaped((1, WIDTH))] * 2,
+        [pltpu.VMEM((SIDE, LANES), F32)],
+        tiles,
+        limit=SMALL_BYTES,
+    )
+    return (layer_out, input_grad, gate_grad, up_grad, down_grad)
 
 
 def solution(mesh):

time: 135 us -> 130 us (0.963)
  starting transfers between devices: 37.6 us -> 47.7 us
  waiting for transfers between devices: 33.3 us -> 25.1 us
  other arithmetic: 5.06 us -> 0.23 us
  local copies, waits for them, and re-layouts: 17.1 us -> 13.6 us
    ppermute x6, starting transfers between devices: 7.25 us -> 12.9 us  [along(): lax.ppermute(first, 'y', ring(4, shift))]
    ppermute x6, waiting for transfers between devices: 12.2 us -> 7.43 us  [along(): lax.ppermute(first, 'y', ring(4, shift))]
    unnamed x45 -> x59, local copies, waits for them, and re-layouts: 9.22 us -> 12.4 us
    all_to_all x2, waiting for transfers between devices: 4.17 us -> 1.83 us  [exchange(): return lax.all_to_all(tiles, ('xh', 'z'), 0, 0, tiled=True)]
    all_to_all x2, starting transfers between devices: 15.6 us -> 17.9 us  [exchange(): return lax.all_to_all(tiles, ('xh', 'z'), 0, 0, tiled=True)]
    unnamed x4 -> x0, other arithmetic: 2.06 us -> none
    squeeze x3 -> x0, local copies, waits for them, and re-layouts: 2.02 us -> none  [the longest x2 1.44 us: per_device(): return (total[0], total[1], gate_grad, up_grad, down_grad)]
    ppermute x6, starting transfers between devices: 8.25 us -> 10 us  [back(): lax.ppermute(part, 'y', ring(4, -shift))]
  transfers between devices with their start and end apart: 25 -> 25, of which waited for: 12 -> 13; matrix products, arithmetic and copies ran while one was open for 3% -> 1% of each run, Pallas kernels for 30% -> 29%
where the time goes in v3:
time: 130 us; the launch traced here: 128 us
  starting transfers between devices  47.7 us (37%)
  Pallas kernels  40.4 us (31%)
  waiting for transfers between devices  25.1 us (19%)
  local copies, waits for them, and re-layouts  13.6 us (10%)
    pallas_call x11, Pallas kernels, call(): pl.pallas_call(kernel, out_shape=outs, in_specs=[pl.BlockSpec(memory_spac...  40.4 us
    all_to_all x2, starting transfers between devices, exchange(): return lax.all_to_all(tiles, ('xh', 'z'), 0, 0, tiled=True)  17.9 us
    ppermute x6, starting transfers between devices, along(): lax.ppermute(first, 'y', ring(4, shift))  12.9 us
    unnamed x59, local copies, waits for them, and re-layouts  12.4 us
    ppermute x6, starting transfers between devices, back(): lax.ppermute(part, 'y', ring(4, -shift))  10 us
    ppermute x4, waiting for transfers between devices, swap(): return lax.ppermute(piece, 'rep', ring(2, 1))  7.96 us
    ppermute x6, waiting for transfers between devices, along(): lax.ppermute(first, 'y', ring(4, shift))  7.43 us
    ppermute x6, waiting for transfers between devices, back(): lax.ppermute(part, 'y', ring(4, -shift))  5.67 us
  transfers between devices with their start and end apart: 25, of which 13 were waited for; matrix products, arithmetic and copies ran while one was open for 1% of the time, Pallas kernels for 29%

profile of v3, /device:TPU:2, one launch (start us, length us, event | category | flops | bytes accessed | tf_op | source)
XLA Modules:
  0.0 128.1 jit_solution(12777153713750236256)
XLA Ops:
  3.2 10.1 %all-to-all-start = ((bf16[16,2,64,128]{3,2,1,0:T(8,128)(2,1)}), bf16[16,2,64,128]{3,2,1,0:T(8,128)(2,1)S(1)}, u32[]{:S(2)}, u32[]{:S(2)}) async-start(bf16[16,2,64,128]{3,2,1,0:T(8,128)(2,1)} %shard_map.110), calls=%async_computation | async-start | bytes 1048576 | tf_op jit(solution)/shard_map/all_to_all | solution.py:364
  13.4 1.3 copy-done.2
  14.7 8.4 %shard_map.112.refs_6_ = bf16[128,8192]{1,0:T(8,128)(2,1)S(1)} custom-call(s32[3,2,72]{2,1,0:T(2,128)S(1)} %copy-done.25, s32[3,2]{1,0:T(4,128)S(1)} %copy.16.count_ref, bf16[2,72,4096]{2,1,0:T(8,128)(2,1)S(1)} %copy-done.2), custom_call_target="tpu_custom_call" | custom-call | bytes 100000 | tf_op jit(solution)/shard_map/pallas_call | solution.py:31
  23.1 3.6 %shard_map.111.refs_4_ = bf16[8192,256]{1,0:T(8,128)(2,1)S(1)} custom-call(s32[3,2,72]{2,1,0:T(2,128)S(1)} %copy-done.25, s32[3,2]{1,0:T(4,128)S(1)} %copy.16.count_ref, bf16[2,72,4096]{2,1,0:T(8,128)(2,1)S(1)} %copy-done.3, bf16[2,72,4096]{2,1,0:T(8,128)(2,1)S(1)} %copy-done.4), custom_call_target="tpu_custom_call" | custom-call | bytes 100000 | tf_op jit(solution)/shard_map/pallas_call | solution.py:31
  26.7 2.0 %copy-done = bf16[8192,256]{1,0:T(8,128)(2,1)} copy-done((bf16[8192,256]{1,0:T(8,128)(2,1)}, bf16[8192,256]{1,0:T(8,128)(2,1)S(1)}, u32[]{:S(2)}) %copy-start) | copy-done | bytes 4194328
  28.7 1.8 %all-to-all-done.tiles_ref = bf16[16,2,64,128]{3,2,1,0:T(8,128)(2,1)S(1)} async-done(((bf16[16,2,64,128]{3,2,1,0:T(8,128)(2,1)}), bf16[16,2,64,128]{3,2,1,0:T(8,128)(2,1)S(1)}, u32[]{:S(2)}, u32[]{:S(2)}) %all-to-all-start) | async-done | bytes 524320 | tf_op jit(solution)/shard_map/all_to_all | solution.py:364
  31.7 3.3 %collective-permute-start = (bf16[16,8192]{1,0:T(8,128)(2,1)S(1)}, bf16[16,8192]{1,0:T(8,128)(2,1)S(1)}, u32[]{:S(2)}, u32[]{:S(2)}) collective-permute-start(bf16[16,8192]{1,0:T(8,128)(2,1)S(1)} %get-tuple-element.57.refs_0_), channel_id=1, source_target_pairs={{0,8},{4,12},{8,0},{12,4},{1,9},{5,13},{9,1},{13,5},{2,10},{6,14},... | collective-permute-start | bytes 786440 | tf_op jit(solution)/shard_map/ppermute | solution.py:346
  35.7 2.6 %collective-permute-start.2 = (bf16[16,8192]{1,0:T(8,128)(2,1)S(1)}, bf16[16,8192]{1,0:T(8,128)(2,1)S(1)}, u32[]{:S(2)}, u32[]{:S(2)}) collective-permute-start(bf16[16,8192]{1,0:T(8,128)(2,1)S(1)} %get-tuple-element.57.refs_0_), channel_id=1, source_target_pairs={{0,12},{4,0},{8,4},{12,8},{1,13},{5,1},{9,5},{13,9},{2,14},{6,2},{... | collective-permute-start | bytes 786440 | tf_op jit(solution)/shard_map/ppermute | solution.py:346
  38.2 4.3 %collective-permute-done.refs_1_ = bf16[16,8192]{1,0:T(8,128)(2,1)S(1)} collective-permute-done((bf16[16,8192]{1,0:T(8,128)(2,1)S(1)}, bf16[16,8192]{1,0:T(8,128)(2,1)S(1)}, u32[]{:S(2)}, u32[]{:S(2)}) %collective-permute-start) | collective-permute-done | bytes 262176 | tf_op jit(solution)/shard_map/ppermute | solution.py:346
  42.5 3.2 %collective-permute-start.5 = (bf16[16,8192]{1,0:T(8,128)(2,1)S(1)}, bf16[16,8192]{1,0:T(8,128)(2,1)S(1)}, u32[]{:S(2)}, u32[]{:S(2)}) collective-permute-start(bf16[16,8192]{1,0:T(8,128)(2,1)S(1)} %get-tuple-element.73.refs_0_), channel_id=1, source_target_pairs={{0,8},{4,12},{8,0},{12,4},{1,9},{5,13},{9,1},{13,5},{2,10},{6,14},... | collective-permute-start | bytes 786440 | tf_op jit(solution)/shard_map/ppermute | solution.py:346
  45.7 2.3 %collective-permute-done.1.refs_2_ = bf16[16,8192]{1,0:T(8,128)(2,1)S(1)} collective-permute-done((bf16[16,8192]{1,0:T(8,128)(2,1)S(1)}, bf16[16,8192]{1,0:T(8,128)(2,1)S(1)}, u32[]{:S(2)}, u32[]{:S(2)}) %collective-permute-start.1) | collective-permute-done | bytes 262176 | tf_op jit(solution)/shard_map/ppermute | solution.py:346
  48.1 1.8 %collective-permute-start.6 = (bf16[16,8192]{1,0:T(8,128)(2,1)S(1)}, bf16[16,8192]{1,0:T(8,128)(2,1)S(1)}, u32[]{:S(2)}, u32[]{:S(2)}) collective-permute-start(bf16[16,8192]{1,0:T(8,128)(2,1)S(1)} %get-tuple-element.73.refs_0_), channel_id=1, source_target_pairs={{0,4},{4,8},{8,12},{12,0},{1,5},{5,9},{9,13},{13,1},{2,6},{6,10},{... | collective-permute-start | bytes 786440 | tf_op jit(solution)/shard_map/ppermute | solution.py:346
  49.8 1.5 %collective-permute-start.7 = (bf16[16,8192]{1,0:T(8,128)(2,1)S(1)}, bf16[16,8192]{1,0:T(8,128)(2,1)S(1)}, u32[]{:S(2)}, u32[]{:S(2)}) collective-permute-start(bf16[16,8192]{1,0:T(8,128)(2,1)S(1)} %get-tuple-element.73.refs_0_), channel_id=1, source_target_pairs={{0,12},{4,0},{8,4},{12,8},{1,13},{5,1},{9,5},{13,9},{2,14},{6,2},{... | collective-permute-start | bytes 786440 | tf_op jit(solution)/shard_map/ppermute | solution.py:346
  51.3 2.2 %copy-done.1 = bf16[8192,256]{1,0:T(8,128)(2,1)S(1)} copy-done((bf16[8192,256]{1,0:T(8,128)(2,1)S(1)}, bf16[8192,256]{1,0:T(8,128)(2,1)}, u32[]{:S(2)}) %copy-start.1) | copy-done | bytes 4194328
  53.5 3.7 %shard_map.114 = (f32[2,64,256]{2,1,0:T(8,128)S(1)}, bf16[64,256]{1,0:T(8,128)(2,1)S(1)}, bf16[32,8192]{1,0:T(8,128)(2,1)S(1)}, bf16[32,8192]{1,0:T(8,128)(2,1)S...) custom-call(bf16[16,8192]{1,0:T(8,128)(2,1)S(1)} %get-tuple-element., ...), custom_call_target="tpu_custom_call" | custom-call | bytes 100000 | tf_op jit(solution)/shard_map/pallas_call | solution.py:31
  58.8 1.4 %collective-permute-start.11 = (bf16[32,8192]{1,0:T(8,128)(2,1)S(1)}, bf16[32,8192]{1,0:T(8,128)(2,1)S(1)}, u32[]{:S(2)}, u32[]{:S(2)}) collective-permute-start(bf16[32,8192]{1,0:T(8,128)(2,1)S(1)} %get-tuple-element.72.refs_0_), channel_id=1, source_target_pairs={{0,1},{1,0},{2,3},{3,2},{4,5},{5,4},{6,7},{7,6},{8,9},{9,8},{10,11... | collective-permute-start | bytes 1572872 | tf_op jit(solution)/shard_map/ppermute | solution.py:352
  60.2 1.4 %collective-permute-start.10 = (bf16[16,8192]{1,0:T(8,128)(2,1)S(1)}, bf16[16,8192]{1,0:T(8,128)(2,1)S(1)}, u32[]{:S(2)}, u32[]{:S(2)}) collective-permute-start(bf16[16,8192]{1,0:T(8,128)(2,1)S(1)} %get-tuple-element.71), channel_id=1, source_target_pairs={{0,4},{4,8},{8,12},{12,0},{1,5},{5,9},{9,13},{13,1},{2,6},{6,10},{... | collective-permute-start | bytes 786440 | tf_op jit(solution)/shard_map/ppermute | solution.py:356
  61.6 2.7 %collective-permute-start.8 = (bf16[16,8192]{1,0:T(8,128)(2,1)S(1)}, bf16[16,8192]{1,0:T(8,128)(2,1)S(1)}, u32[]{:S(2)}, u32[]{:S(2)}) collective-permute-start(bf16[16,8192]{1,0:T(8,128)(2,1)S(1)} %get-tuple-element.69), channel_id=1, source_target_pairs={{0,8},{4,12},{8,0},{12,4},{1,9},{5,13},{9,1},{13,5},{2,10},{6,14},... | collective-permute-start | bytes 786440 | tf_op jit(solution)/shard_map/ppermute | solution.py:356
  64.3 1.4 %collective-permute-start.9 = (bf16[16,8192]{1,0:T(8,128)(2,1)S(1)}, bf16[16,8192]{1,0:T(8,128)(2,1)S(1)}, u32[]{:S(2)}, u32[]{:S(2)}) collective-permute-start(bf16[16,8192]{1,0:T(8,128)(2,1)S(1)} %get-tuple-element.70), channel_id=1, source_target_pairs={{0,12},{4,0},{8,4},{12,8},{1,13},{5,1},{9,5},{13,9},{2,14},{6,2},{... | collective-permute-start | bytes 786440 | tf_op jit(solution)/shard_map/ppermute | solution.py:356
  65.7 6.5 %shard_map.115 = (bf16[64,384]{1,0:T(8,128)(2,1)S(1)}, bf16[64,8576]{1,0:T(8,128)(2,1)}, f32[16,8192]{1,0:T(8,128)S(1)}, bf16[16,8192]{1,0:T(8,128)(2,1)}, bf16[...) custom-call(bf16[16,8192]{1,0:T(8,128)(2,1)S(1)} %get-tuple-element.73.refs_0_, ...), custom_call_target="tpu_custom_call" | custom-call | bytes 100000 | tf_op jit(solution)/shard_map/pallas_call | solution.py:31
  73.7 1.6 %collective-permute-done.8.refs_1_ = bf16[16,8192]{1,0:T(8,128)(2,1)S(1)} collective-permute-done((bf16[16,8192]{1,0:T(8,128)(2,1)S(1)}, bf16[16,8192]{1,0:T(8,128)(2,1)S(1)}, u32[]{:S(2)}, u32[]{:S(2)}) %collective-permute-start.8) | collective-permute-done | bytes 262176 | tf_op jit(solution)/shard_map/ppermute | solution.py:356
  79.0 2.5 %collective-permute-start.13 = (bf16[16,8192]{1,0:T(8,128)(2,1)}, bf16[16,8192]{1,0:T(8,128)(2,1)S(1)}, u32[]{:S(2)}, u32[]{:S(2)}) collective-permute-start(bf16[16,8192]{1,0:T(8,128)(2,1)} %get-tuple-element.90), channel_id=1, source_target_pairs={{0,8},{4,12},{8,0},{12,4},{1,9},{5,13},{9,1},{13,5},{2,10},{6,14},... | collective-permute-start | bytes 786440 | tf_op jit(solution)/shard_map/ppermute | solution.py:356
  82.3 1.3 collective-permute-start.15
  83.6 1.5 %collective-permute-start.16 = (bf16[128,384]{1,0:T(8,128)(2,1)S(1)}, bf16[128,384]{1,0:T(8,128)(2,1)S(1)}, u32[]{:S(2)}, u32[]{:S(2)}) collective-permute-start(bf16[128,384]{1,0:T(8,128)(2,1)S(1)} %pad_maximum_fusion.refs_8_), channel_id=1, source_target_pairs={{0,1},{1,0},{2,3},{3,2},{4,5},{5,4},{6,7},{7,6},{8,9},{9,8},{10,11... | collective-permute-start | bytes 294920 | tf_op jit(solution)/shard_map/ppermute | solution.py:352
  85.2 5.7 %shard_map.116 = (bf16[72,4096]{1,0:T(8,128)(2,1)S(1)}, bf16[72,4096]{1,0:T(8,128)(2,1)S(1)}) custom-call(bf16[16,8192]{1,0:T(8,128)(2,1)S(1)} %get-tuple-element.73.refs_0_, bf16[16,8192]{1,0:T(8,128)(2,1)S(1)} %collective-permute-done.5.refs_1_, bf16[16,8192]{1,0:T(8,128)(2,1)S(1)} %collective-permute-done.6.refs_2_, ...), custom_call_target="tpu_custom_call" | custom-call | bytes 100000 | tf_op jit(solution)/shard_map/pallas_call | solution.py:31
  90.9 2.8 %collective-permute-done.14.refs_6_ = bf16[16,8192]{1,0:T(8,128)(2,1)S(1)} collective-permute-done((bf16[16,8192]{1,0:T(8,128)(2,1)}, bf16[16,8192]{1,0:T(8,128)(2,1)S(1)}, u32[]{:S(2)}, u32[]{:S(2)}) %collective-permute-start.14) | collective-permute-done | bytes 262176 | tf_op jit(solution)/shard_map/ppermute | solution.py:356
  95.8 1.8 %shard_map.117 = bf16[16,2,64,128]{3,2,1,0:T(8,128)(2,1)} custom-call(f32[16,8192]{1,0:T(8,128)S(1)} %copy-done.14, bf16[16,8192]{1,0:T(8,128)(2,1)S(1)} %copy-done.20, bf16[16,8192]{1,0:T(8,128)(2,1)S(1)} %copy-done.22, bf16[16,8192]{1,0:T(8,128)(2,1)S(1)} %copy-done.18, f32[16,8192]{1,0:T(8,128)S(1)} %copy-done.16, ...), custom_call_target="tpu_custom_call" | custom-call | bytes 100000 | tf_op jit(solution)/shard_map/pallas_call | solution.py:31
  97.6 7.8 %all-to-all-start.1 = ((bf16[16,2,64,128]{3,2,1,0:T(8,128)(2,1)}), bf16[16,2,64,128]{3,2,1,0:T(8,128)(2,1)S(1)}, u32[]{:S(2)}, u32[]{:S(2)}) async-start(bf16[16,2,64,128]{3,2,1,0:T(8,128)(2,1)} %shard_map.117), calls=%async_computation.1 | async-start | bytes 1048576 | tf_op jit(solution)/shard_map/all_to_all | solution.py:364
  105.4 1.5 %collective-permute-start.22 = (bf16[72,4096]{1,0:T(8,128)(2,1)}, bf16[72,4096]{1,0:T(8,128)(2,1)S(1)}, u32[]{:S(2)}, u32[]{:S(2)}) collective-permute-start(bf16[72,4096]{1,0:T(8,128)(2,1)} %copy-done.26), channel_id=1, source_target_pairs={{0,1},{1,0},{2,3},{3,2},{4,5},{5,4},{6,7},{7,6},{8,9},{9,8},{10,11... | collective-permute-start | bytes 1769480 | tf_op jit(solution)/shard_map/ppermute | solution.py:352
  111.0 6.9 %shard_map.119 = (f32[36,2,4096]{2,1,0:T(2,128)}, f32[36,2,4096]{2,1,0:T(2,128)}) custom-call(bf16[32,8192]{1,0:T(8,128)(2,1)S(1)} %copy-done.6, bf16[32,8192]{1,0:T(8,128)(2,1)S(1)} %copy-done.8, bf16[32,8192]{1,0:T(8,128)(2,1)S(1)} %collective-permute-done.18.refs_2_, bf16[32,8192]{1,0:T(8,128)(2,1)S(1)} %collective-permute-done.19.refs_3_, ...), custom_call_target="tpu_custom_call" | custom-call | bytes 100000 | tf_op jit(solution)/shard_map/pallas_call | solution.py:31
  118.0 7.9 %collective-permute-done.22.send_ref = bf16[72,4096]{1,0:T(8,128)(2,1)S(1)} collective-permute-done((bf16[72,4096]{1,0:T(8,128)(2,1)}, bf16[72,4096]{1,0:T(8,128)(2,1)S(1)}, u32[]{:S(2)}, u32[]{:S(2)}) %collective-permute-start.22) | collective-permute-done | bytes 589856 | tf_op jit(solution)/shard_map/ppermute | solution.py:352
  125.9 1.3 %shard_map.120 = f32[36,2,4096]{2,1,0:T(2,128)} custom-call(bf16[72,4096]{1,0:T(8,128)(2,1)S(1)} %get-tuple-element.105.keep_ref, bf16[72,4096]{1,0:T(8,128)(2,1)S(1)} %collective-permute-done.22.send_ref), custom_call_target="tpu_custom_call" | custom-call | bytes 100000 | tf_op jit(solution)/shard_map/pallas_call | solution.py:31
  (99 shorter events, 19.2 us)
Async XLA Ops:
  3.2 27.3 %all-to-all-start = ((bf16[16,2,64,128]{3,2,1,0:T(8,128)(2,1)}), bf16[16,2,64,128]{3,2,1,0:T(8,128)(2,1)S(1)}, u32[]{:S(2)}, u32[]{:S(2)}) async-start(bf16[16,2,64,128]{3,2,1,0:T(8,128)(2,1)} %shard_map.110), calls=%async_computation | async-start | bytes 1048576 | tf_op jit(solution)/shard_map/all_to_all | solution.py:364
  30.5 20.8 %collective-permute-start.3 = (bf16[8192,256]{1,0:T(8,128)(2,1)}, bf16[8192,256]{1,0:T(8,128)(2,1)S(1)}, u32[]{:S(2)}, u32[]{:S(2)}) collective-permute-start(bf16[8192,256]{1,0:T(8,128)(2,1)} %copy-done), channel_id=1, source_target_pairs={{0,2},{2,0},{1,3},{3,1},{4,6},{6,4},{5,7},{7,5},{8,10},{10,8},{9,1... | collective-permute-start | bytes 12582920 | tf_op jit(solution)/shard_map/ppermute | solution.py:349
  30.5 20.8 %collective-permute-start.4 = (bf16[128,8192]{1,0:T(8,128)(2,1)S(1)}, bf16[128,8192]{1,0:T(8,128)(2,1)S(1)}, u32[]{:S(2)}, u32[]{:S(2)}) collective-permute-start(bf16[128,8192]{1,0:T(8,128)(2,1)S(1)} %shard_map.112.refs_6_), channel_id=1, source_target_pairs={{0,2},{2,0},{1,3},{3,1},{4,6},{6,4},{5,7},{7,5},{8,10},{10,8},{9,1... | collective-permute-start | bytes 6291464 | tf_op jit(solution)/shard_map/ppermute | solution.py:349
  31.7 10.8 %collective-permute-start = (bf16[16,8192]{1,0:T(8,128)(2,1)S(1)}, bf16[16,8192]{1,0:T(8,128)(2,1)S(1)}, u32[]{:S(2)}, u32[]{:S(2)}) collective-permute-start(bf16[16,8192]{1,0:T(8,128)(2,1)S(1)} %get-tuple-element.57.refs_0_), channel_id=1, source_target_pairs={{0,8},{4,12},{8,0},{12,4},{1,9},{5,13},{9,1},{13,5},{2,10},{6,14},... | collective-permute-start | bytes 786440 | tf_op jit(solution)/shard_map/ppermute | solution.py:346
  35.0 13.1 %collective-permute-start.1 = (bf16[16,8192]{1,0:T(8,128)(2,1)S(1)}, bf16[16,8192]{1,0:T(8,128)(2,1)S(1)}, u32[]{:S(2)}, u32[]{:S(2)}) collective-permute-start(bf16[16,8192]{1,0:T(8,128)(2,1)S(1)} %get-tuple-element.57.refs_0_), channel_id=1, source_target_pairs={{0,4},{4,8},{8,12},{12,0},{1,5},{5,9},{9,13},{13,1},{2,6},{6,10},{... | collective-permute-start | bytes 786440 | tf_op jit(solution)/shard_map/ppermute | solution.py:346
  35.7 14.2 %collective-permute-start.2 = (bf16[16,8192]{1,0:T(8,128)(2,1)S(1)}, bf16[16,8192]{1,0:T(8,128)(2,1)S(1)}, u32[]{:S(2)}, u32[]{:S(2)}) collective-permute-start(bf16[16,8192]{1,0:T(8,128)(2,1)S(1)} %get-tuple-element.57.refs_0_), channel_id=1, source_target_pairs={{0,12},{4,0},{8,4},{12,8},{1,13},{5,1},{9,5},{13,9},{2,14},{6,2},{... | collective-permute-start | bytes 786440 | tf_op jit(solution)/shard_map/ppermute | solution.py:346
  42.5 15.4 %collective-permute-start.5 = (bf16[16,8192]{1,0:T(8,128)(2,1)S(1)}, bf16[16,8192]{1,0:T(8,128)(2,1)S(1)}, u32[]{:S(2)}, u32[]{:S(2)}) collective-permute-start(bf16[16,8192]{1,0:T(8,128)(2,1)S(1)} %get-tuple-element.73.refs_0_), channel_id=1, source_target_pairs={{0,8},{4,12},{8,0},{12,4},{1,9},{5,13},{9,1},{13,5},{2,10},{6,14},... | collective-permute-start | bytes 786440 | tf_op jit(solution)/shard_map/ppermute | solution.py:346
  48.1 10.4 %collective-permute-start.6 = (bf16[16,8192]{1,0:T(8,128)(2,1)S(1)}, bf16[16,8192]{1,0:T(8,128)(2,1)S(1)}, u32[]{:S(2)}, u32[]{:S(2)}) collective-permute-start(bf16[16,8192]{1,0:T(8,128)(2,1)S(1)} %get-tuple-element.73.refs_0_), channel_id=1, source_target_pairs={{0,4},{4,8},{8,12},{12,0},{1,5},{5,9},{9,13},{13,1},{2,6},{6,10},{... | collective-permute-start | bytes 786440 | tf_op jit(solution)/shard_map/ppermute | solution.py:346
  49.8 8.9 %collective-permute-start.7 = (bf16[16,8192]{1,0:T(8,128)(2,1)S(1)}, bf16[16,8192]{1,0:T(8,128)(2,1)S(1)}, u32[]{:S(2)}, u32[]{:S(2)}) collective-permute-start(bf16[16,8192]{1,0:T(8,128)(2,1)S(1)} %get-tuple-element.73.refs_0_), channel_id=1, source_target_pairs={{0,12},{4,0},{8,4},{12,8},{1,13},{5,1},{9,5},{13,9},{2,14},{6,2},{... | collective-permute-start | bytes 786440 | tf_op jit(solution)/shard_map/ppermute | solution.py:346
  58.0 14.2 %copy-start.5 = (bf16[32,8192]{1,0:T(8,128)(2,1)}, bf16[32,8192]{1,0:T(8,128)(2,1)S(1)}, u32[]{:S(2)}) copy-start(bf16[32,8192]{1,0:T(8,128)(2,1)S(1)} %get-tuple-element.72.refs_0_) | copy-start | bytes 1572868
  58.0 14.2 %copy-start.7 = (bf16[32,8192]{1,0:T(8,128)(2,1)}, bf16[32,8192]{1,0:T(8,128)(2,1)S(1)}, u32[]{:S(2)}) copy-start(bf16[32,8192]{1,0:T(8,128)(2,1)S(1)} %get-tuple-element.93.refs_1_) | copy-start | bytes 1572868
  58.8 18.0 %collective-permute-start.11 = (bf16[32,8192]{1,0:T(8,128)(2,1)S(1)}, bf16[32,8192]{1,0:T(8,128)(2,1)S(1)}, u32[]{:S(2)}, u32[]{:S(2)}) collective-permute-start(bf16[32,8192]{1,0:T(8,128)(2,1)S(1)} %get-tuple-element.72.refs_0_), channel_id=1, source_target_pairs={{0,1},{1,0},{2,3},{3,2},{4,5},{5,4},{6,7},{7,6},{8,9},{9,8},{10,11... | collective-permute-start | bytes 1572872 | tf_op jit(solution)/shard_map/ppermute | solution.py:352
  60.2 12.8 %collective-permute-start.10 = (bf16[16,8192]{1,0:T(8,128)(2,1)S(1)}, bf16[16,8192]{1,0:T(8,128)(2,1)S(1)}, u32[]{:S(2)}, u32[]{:S(2)}) collective-permute-start(bf16[16,8192]{1,0:T(8,128)(2,1)S(1)} %get-tuple-element.71), channel_id=1, source_target_pairs={{0,4},{4,8},{8,12},{12,0},{1,5},{5,9},{9,13},{13,1},{2,6},{6,10},{... | collective-permute-start | bytes 786440 | tf_op jit(solution)/shard_map/ppermute | solution.py:356
  61.6 13.7 %collective-permute-start.8 = (bf16[16,8192]{1,0:T(8,128)(2,1)S(1)}, bf16[16,8192]{1,0:T(8,128)(2,1)S(1)}, u32[]{:S(2)}, u32[]{:S(2)}) collective-permute-start(bf16[16,8192]{1,0:T(8,128)(2,1)S(1)} %get-tuple-element.69), channel_id=1, source_target_pairs={{0,8},{4,12},{8,0},{12,4},{1,9},{5,13},{9,1},{13,5},{2,10},{6,14},... | collective-permute-start | bytes 786440 | tf_op jit(solution)/shard_map/ppermute | solution.py:356
  64.3 11.7 %collective-permute-start.9 = (bf16[16,8192]{1,0:T(8,128)(2,1)S(1)}, bf16[16,8192]{1,0:T(8,128)(2,1)S(1)}, u32[]{:S(2)}, u32[]{:S(2)}) collective-permute-start(bf16[16,8192]{1,0:T(8,128)(2,1)S(1)} %get-tuple-element.70), channel_id=1, source_target_pairs={{0,12},{4,0},{8,4},{12,8},{1,13},{5,1},{9,5},{13,9},{2,14},{6,2},{... | collective-permute-start | bytes 786440 | tf_op jit(solution)/shard_map/ppermute | solution.py:356
  77.6 6.0 %collective-permute-start.12 = (bf16[64,8576]{1,0:T(8,128)(2,1)}, bf16[64,8576]{1,0:T(8,128)(2,1)S(1)}, u32[]{:S(2)}, u32[]{:S(2)}) collective-permute-start(bf16[64,8576]{1,0:T(8,128)(2,1)} %get-tuple-element.87), channel_id=1, source_target_pairs={{0,2},{2,0},{1,3},{3,1},{4,6},{6,4},{5,7},{7,5},{8,10},{10,8},{9,1... | collective-permute-start | bytes 3293192 | tf_op jit(solution)/shard_map/ppermute | solution.py:349
  78.0 16.9 %collective-permute-start.17 = (bf16[32,8192]{1,0:T(8,128)(2,1)}, bf16[32,8192]{1,0:T(8,128)(2,1)S(1)}, u32[]{:S(2)}, u32[]{:S(2)}) collective-permute-start(bf16[32,8192]{1,0:T(8,128)(2,1)} %copy-done.7), channel_id=1, source_target_pairs={{0,1},{1,0},{2,3},{3,2},{4,5},{5,4},{6,7},{7,6},{8,9},{9,8},{10,11... | collective-permute-start | bytes 1572872 | tf_op jit(solution)/shard_map/ppermute | solution.py:352
  79.0 11.8 %collective-permute-start.13 = (bf16[16,8192]{1,0:T(8,128)(2,1)}, bf16[16,8192]{1,0:T(8,128)(2,1)S(1)}, u32[]{:S(2)}, u32[]{:S(2)}) collective-permute-start(bf16[16,8192]{1,0:T(8,128)(2,1)} %get-tuple-element.90), channel_id=1, source_target_pairs={{0,8},{4,12},{8,0},{12,4},{1,9},{5,13},{9,1},{13,5},{2,10},{6,14},... | collective-permute-start | bytes 786440 | tf_op jit(solution)/shard_map/ppermute | solution.py:356
  81.5 12.2 %collective-permute-start.14 = (bf16[16,8192]{1,0:T(8,128)(2,1)}, bf16[16,8192]{1,0:T(8,128)(2,1)S(1)}, u32[]{:S(2)}, u32[]{:S(2)}) collective-permute-start(bf16[16,8192]{1,0:T(8,128)(2,1)} %get-tuple-element.91), channel_id=1, source_target_pairs={{0,12},{4,0},{8,4},{12,8},{1,13},{5,1},{9,5},{13,9},{2,14},{6,2},{... | collective-permute-start | bytes 786440 | tf_op jit(solution)/shard_map/ppermute | solution.py:356
  82.3 12.6 %collective-permute-start.15 = (bf16[16,8192]{1,0:T(8,128)(2,1)}, bf16[16,8192]{1,0:T(8,128)(2,1)S(1)}, u32[]{:S(2)}, u32[]{:S(2)}) collective-permute-start(bf16[16,8192]{1,0:T(8,128)(2,1)} %get-tuple-element.92), channel_id=1, source_target_pairs={{0,4},{4,8},{8,12},{12,0},{1,5},{5,9},{9,13},{13,1},{2,6},{6,10},{... | collective-permute-start | bytes 786440 | tf_op jit(solution)/shard_map/ppermute | solution.py:356
  83.6 12.1 %copy-start.14 = (f32[16,8192]{1,0:T(8,128)S(1)}, f32[16,8192]{1,0:T(8,128)}, u32[]{:S(2)}) copy-start(f32[16,8192]{1,0:T(8,128)} %copy-done.13) | copy-start | bytes 1572868
  83.6 12.1 %copy-start.16 = (f32[16,8192]{1,0:T(8,128)S(1)}, f32[16,8192]{1,0:T(8,128)}, u32[]{:S(2)}) copy-start(f32[16,8192]{1,0:T(8,128)} %copy-done.15) | copy-start | bytes 1572868
  83.6 12.1 %copy-start.18 = (bf16[16,8192]{1,0:T(8,128)(2,1)S(1)}, bf16[16,8192]{1,0:T(8,128)(2,1)}, u32[]{:S(2)}) copy-start(bf16[16,8192]{1,0:T(8,128)(2,1)} %copy-done.17) | copy-start | bytes 786436
  83.6 12.1 %copy-start.20 = (bf16[16,8192]{1,0:T(8,128)(2,1)S(1)}, bf16[16,8192]{1,0:T(8,128)(2,1)}, u32[]{:S(2)}) copy-start(bf16[16,8192]{1,0:T(8,128)(2,1)} %copy-done.19) | copy-start | bytes 786436
  83.6 12.1 %copy-start.22 = (bf16[16,8192]{1,0:T(8,128)(2,1)S(1)}, bf16[16,8192]{1,0:T(8,128)(2,1)}, u32[]{:S(2)}) copy-start(bf16[16,8192]{1,0:T(8,128)(2,1)} %copy-done.21) | copy-start | bytes 786436
  83.6 11.3 %collective-permute-start.16 = (bf16[128,384]{1,0:T(8,128)(2,1)S(1)}, bf16[128,384]{1,0:T(8,128)(2,1)S(1)}, u32[]{:S(2)}, u32[]{:S(2)}) collective-permute-start(bf16[128,384]{1,0:T(8,128)(2,1)S(1)} %pad_maximum_fusion.refs_8_), channel_id=1, source_target_pairs={{0,1},{1,0},{2,3},{3,2},{4,5},{5,4},{6,7},{7,6},{8,9},{9,8},{10,11... | collective-permute-start | bytes 294920 | tf_op jit(solution)/shard_map/ppermute | solution.py:352
  97.6 29.6 %all-to-all-start.1 = ((bf16[16,2,64,128]{3,2,1,0:T(8,128)(2,1)}), bf16[16,2,64,128]{3,2,1,0:T(8,128)(2,1)S(1)}, u32[]{:S(2)}, u32[]{:S(2)}) async-start(bf16[16,2,64,128]{3,2,1,0:T(8,128)(2,1)} %shard_map.117), calls=%async_computation.1 | async-start | bytes 1048576 | tf_op jit(solution)/shard_map/all_to_all | solution.py:364
  105.4 20.5 %collective-permute-start.22 = (bf16[72,4096]{1,0:T(8,128)(2,1)}, bf16[72,4096]{1,0:T(8,128)(2,1)S(1)}, u32[]{:S(2)}, u32[]{:S(2)}) collective-permute-start(bf16[72,4096]{1,0:T(8,128)(2,1)} %copy-done.26), channel_id=1, source_target_pairs={{0,1},{1,0},{2,3},{3,2},{4,5},{5,4},{6,7},{7,6},{8,9},{9,8},{10,11... | collective-permute-start | bytes 1769480 | tf_op jit(solution)/shard_map/ppermute | solution.py:352
  106.9 1.9 %collective-permute-start.18 = (bf16[32,8192]{1,0:T(8,128)(2,1)S(1)}, bf16[32,8192]{1,0:T(8,128)(2,1)S(1)}, u32[]{:S(2)}, u32[]{:S(2)}) collective-permute-start(bf16[32,8192]{1,0:T(8,128)(2,1)S(1)} %copy-done.6), channel_id=1, source_target_pairs={{0,2},{2,0},{1,3},{3,1},{4,6},{6,4},{5,7},{7,5},{8,10},{10,8},{9,1... | collective-permute-start | bytes 1572872 | tf_op jit(solution)/shard_map/ppermute | solution.py:349
  106.9 2.7 %collective-permute-start.19 = (bf16[32,8192]{1,0:T(8,128)(2,1)S(1)}, bf16[32,8192]{1,0:T(8,128)(2,1)S(1)}, u32[]{:S(2)}, u32[]{:S(2)}) collective-permute-start(bf16[32,8192]{1,0:T(8,128)(2,1)S(1)} %copy-done.8), channel_id=1, source_target_pairs={{0,2},{2,0},{1,3},{3,1},{4,6},{6,4},{5,7},{7,5},{8,10},{10,8},{9,1... | collective-permute-start | bytes 1572872 | tf_op jit(solution)/shard_map/ppermute | solution.py:349
  107.4 2.9 %collective-permute-start.20 = (bf16[32,8192]{1,0:T(8,128)(2,1)S(1)}, bf16[32,8192]{1,0:T(8,128)(2,1)S(1)}, u32[]{:S(2)}, u32[]{:S(2)}) collective-permute-start(bf16[32,8192]{1,0:T(8,128)(2,1)S(1)} %copy-done.10), channel_id=1, source_target_pairs={{0,2},{2,0},{1,3},{3,1},{4,6},{6,4},{5,7},{7,5},{8,10},{10,8},{9,1... | collective-permute-start | bytes 1572872 | tf_op jit(solution)/shard_map/ppermute | solution.py:349
  107.5 3.5 %collective-permute-start.21 = (bf16[32,8192]{1,0:T(8,128)(2,1)S(1)}, bf16[32,8192]{1,0:T(8,128)(2,1)S(1)}, u32[]{:S(2)}, u32[]{:S(2)}) collective-permute-start(bf16[32,8192]{1,0:T(8,128)(2,1)S(1)} %copy-done.12), channel_id=1, source_target_pairs={{0,2},{2,0},{1,3},{3,1},{4,6},{6,4},{5,7},{7,5},{8,10},{10,8},{9,1... | collective-permute-start | bytes 1572872 | tf_op jit(solution)/shard_map/ppermute | solution.py:349
  (22 other events, 108.3 us)

commit v4 on v3

--- a/solution.py
+++ b/solution.py
@@ -69,20 +69,26 @@
             ].astype(BF16)
 
 
-def collect_kernel(*refs):
-    *parts, tiles_ref, strip_ref = refs
-    for which in range(2):
-        first_ref, *moved = parts[4 * which : 4 * which + 4]
-        for inner in range(SIDE):
-            cols = slice(inner * LANES, (inner + 1) * LANES)
-            total = first_ref[:, cols]
-            for ref in moved:
-                total = total + ref[:, cols].astype(F32)
-            strip_ref[which, pl.ds(inner, FAR, SIDE), :] = total
-        for place in range(FAR):
-            tiles_ref[place, which] = strip_ref[
-                which, place * SIDE : (place + 1) * SIDE, :
-            ].astype(BF16)
+def summed(first_ref, moved, strip_ref, tiles_ref):
+    for inner in range(SIDE):
+        cols = slice(inner * LANES, (inner + 1) * LANES)
+        total = first_ref[:, cols]
+        for ref in moved:
+            total = total + ref[:, cols].astype(F32)
+        strip_ref[pl.ds(inner, FAR, SIDE), :] = total
+    for place in range(FAR):
+        tiles_ref[place] = strip_ref[place * SIDE : (place + 1) * SIDE, :].astype(BF16)
+
+
+def collect_kernel(first_ref, *refs):
+    *moved, tiles_ref, strip_ref = refs
+    summed(first_ref, moved, strip_ref, tiles_ref)
+
+
+def join_kernel(out_ref, first_ref, *refs):
+    *moved, tiles_ref, strip_ref = refs
+    tiles_ref[:, 0] = out_ref[...]
+    summed(first_ref, moved, strip_ref, tiles_ref.at[:, 1])
 
 
 def finish_kernel(total_ref, out_ref, grad_ref, strip_ref):
@@ -359,6 +365,7 @@
     tie = lax.optimization_barrier
     numbers = (block_index, block_counts)
     strips = pltpu.VMEM((2, SIDE * FAR, LANES), F32)
+    strip = pltpu.VMEM((SIDE * FAR, LANES), F32)
 
     def exchange(tiles):
         return lax.all_to_all(tiles, ("xh", "z"), 0, 0, tiled=True)
@@ -369,7 +376,7 @@
         [pltpu.VMEM((SIDE, LANES), F32)],
         activations,
         out_cotangent,
-        limit=SMALL_BYTES,
+        limit=62 * 1024 * 1024,
     )[0]
     tiles = exchange(tiles)
     down = call(
@@ -437,7 +444,15 @@
         both,
         hidden,
     )
-    out_moved, far_low, near, away, high = tie((out_moved, far_low, near, away, high))
+    out_tiles = call(
+        collect_kernel,
+        [shaped((FAR, SIDE, LANES))],
+        [strip],
+        out_first,
+        *out_moved,
+        limit=SMALL_BYTES,
+    )[0]
+    out_tiles, far_low, near, away, high = tie((out_tiles, far_low, near, away, high))
 
     grad_moved = back(grad_moved)
     far_high = swap(high)
@@ -462,11 +477,10 @@
     acts = [low, high, over(low), over(high), far_low, far_high, over(far_low), over(far_high)]
     tiles = exchange(
         call(
-            collect_kernel,
+            join_kernel,
             [shaped((FAR, 2, SIDE, LANES))],
-            [strips],
-            out_first,
-            *out_moved,
+            [strip],
+            out_tiles,
             grad_first,
             *grad_moved,
             limit=SMALL_BYTES,
@@ -483,6 +497,14 @@
         select[:2, :KEPT],
         space=pltpu.HBM,
     )
+    layer_out, input_grad = call(
+        finish_kernel,
+        [shaped((1, WIDTH))] * 2,
+        [pltpu.VMEM((SIDE, LANES), F32)],
+        tiles,
+        limit=SMALL_BYTES,
+    )
+    layer_out, input_grad, come_down = tie((layer_out, input_grad, come_down))
     down_grad = call(
         settle_kernel,
         [grad],
@@ -493,13 +515,6 @@
     )[0]
     gate_grad, up_grad, down_grad = (
         jnp.swapaxes(grad, 0, 1) for grad in (gate_grad, up_grad, down_grad)
-    )
-    layer_out, input_grad = call(
-        finish_kernel,
-        [shaped((1, WIDTH))] * 2,
-        [pltpu.VMEM((SIDE, LANES), F32)],
-        tiles,
-        limit=SMALL_BYTES,
     )
     return (layer_out, input_grad, gate_grad, up_grad, down_grad)
 

time: 130 us -> 126 us (0.969)
  local copies, waits for them, and re-layouts: 13.6 us -> 9.33 us
  Pallas kernels: 40.4 us -> 42.7 us
  waiting for transfers between devices: 25.1 us -> 23.5 us
    ppermute x4, waiting for transfers between devices: 7.96 us -> 2.51 us  [swap(): return lax.ppermute(piece, 'rep', ring(2, 1))]
    unnamed x59 -> x47, local copies, waits for them, and re-layouts: 12.4 us -> 8.06 us
    all_to_all x2, waiting for transfers between devices: 1.83 us -> 4.48 us  [exchange(): return lax.all_to_all(tiles, ('xh', 'z'), 0, 0, tiled=True)]
    pallas_call x11 -> x12, Pallas kernels: 40.4 us -> 42.7 us  [call(): pl.pallas_call(kernel, out_shape=outs, in_specs=[pl.BlockSpec(memory_spac...]
  transfers between devices with their start and end apart: 25 -> 25, of which waited for: 13 -> 16; matrix products, arithmetic and copies ran while one was open for 1% -> 1% of each run, Pallas kernels for 29% -> 31%
where the time goes in v4:
time: 126 us; the launch traced here: 125 us
  starting transfers between devices  47.9 us (38%)
  Pallas kernels  42.7 us (34%)
  waiting for transfers between devices  23.5 us (19%)
  local copies, waits for them, and re-layouts  9.33 us (7%)
    pallas_call x12, Pallas kernels, call(): pl.pallas_call(kernel, out_shape=outs, in_specs=[pl.BlockSpec(memory_spac...  42.7 us
    all_to_all x2, starting transfers between devices, exchange(): return lax.all_to_all(tiles, ('xh', 'z'), 0, 0, tiled=True)  18 us
    ppermute x6, starting transfers between devices, along(): lax.ppermute(first, 'y', ring(4, shift))  12.9 us
    ppermute x6, starting transfers between devices, back(): lax.ppermute(part, 'y', ring(4, -shift))  10.2 us
    unnamed x47, local copies, waits for them, and re-layouts  8.06 us
    ppermute x6, waiting for transfers between devices, along(): lax.ppermute(first, 'y', ring(4, shift))  7.48 us
    ppermute x6, waiting for transfers between devices, back(): lax.ppermute(part, 'y', ring(4, -shift))  6.75 us
    ppermute x4, starting transfers between devices, swap(): return lax.ppermute(piece, 'rep', ring(2, 1))  5.16 us
  transfers between devices with their start and end apart: 25, of which 16 were waited for; matrix products, arithmetic and copies ran while one was open for 1% of the time, Pallas kernels for 31%

profile of v4, /device:TPU:2, one launch (start us, length us, event | category | flops | bytes accessed | tf_op | source)
XLA Modules:
  0.0 124.7 jit_solution(844461424478057104)
XLA Ops:
  0.7 1.8 %shard_map.110 = bf16[16,2,64,128]{3,2,1,0:T(8,128)(2,1)} custom-call(bf16[1,8192]{1,0:T(2,128)(2,1)} %act_ref.1, bf16[1,8192]{1,0:T(2,128)(2,1)} %cot_ref.1), custom_call_target="tpu_custom_call" | custom-call | bytes 100000 | tf_op jit(solution)/shard_map/pallas_call | solution.py:31
  2.5 10.1 %all-to-all-start = ((bf16[16,2,64,128]{3,2,1,0:T(8,128)(2,1)}), bf16[16,2,64,128]{3,2,1,0:T(8,128)(2,1)S(1)}, u32[]{:S(2)}, u32[]{:S(2)}) async-start(bf16[16,2,64,128]{3,2,1,0:T(8,128)(2,1)} %shard_map.110), calls=%async_computation | async-start | bytes 1048576 | tf_op jit(solution)/shard_map/all_to_all | solution.py:371
  12.7 1.3 %copy-done.2 = bf16[2,72,4096]{2,1,0:T(8,128)(2,1)S(1)} copy-done((bf16[2,72,4096]{2,1,0:T(8,128)(2,1)S(1)}, bf16[2,72,4096]{2,1,0:T(8,128)(2,1)}, u32[]{:S(2)}) %copy-start.2) | copy-done | bytes 1179672
  14.0 8.4 %shard_map.112.refs_6_ = bf16[128,8192]{1,0:T(8,128)(2,1)S(1)} custom-call(s32[3,2,72]{2,1,0:T(2,128)S(1)} %copy-done.17, s32[3,2]{1,0:T(4,128)S(1)} %copy.16.count_ref, bf16[2,72,4096]{2,1,0:T(8,128)(2,1)S(1)} %copy-done.2), custom_call_target="tpu_custom_call" | custom-call | bytes 100000 | tf_op jit(solution)/shard_map/pallas_call | solution.py:31
  22.4 3.6 %shard_map.111.refs_4_ = bf16[8192,256]{1,0:T(8,128)(2,1)S(1)} custom-call(s32[3,2,72]{2,1,0:T(2,128)S(1)} %copy-done.17, s32[3,2]{1,0:T(4,128)S(1)} %copy.16.count_ref, bf16[2,72,4096]{2,1,0:T(8,128)(2,1)S(1)} %copy-done.3, bf16[2,72,4096]{2,1,0:T(8,128)(2,1)S(1)} %copy-done.4), custom_call_target="tpu_custom_call" | custom-call | bytes 100000 | tf_op jit(solution)/shard_map/pallas_call | solution.py:31
  26.0 2.0 %copy-done = bf16[8192,256]{1,0:T(8,128)(2,1)} copy-done((bf16[8192,256]{1,0:T(8,128)(2,1)}, bf16[8192,256]{1,0:T(8,128)(2,1)S(1)}, u32[]{:S(2)}) %copy-start) | copy-done | bytes 4194328
  28.0 1.8 %all-to-all-done.tiles_ref = bf16[16,2,64,128]{3,2,1,0:T(8,128)(2,1)S(1)} async-done(((bf16[16,2,64,128]{3,2,1,0:T(8,128)(2,1)}), bf16[16,2,64,128]{3,2,1,0:T(8,128)(2,1)S(1)}, u32[]{:S(2)}, u32[]{:S(2)}) %all-to-all-start) | async-done | bytes 524320 | tf_op jit(solution)/shard_map/all_to_all | solution.py:371
  31.0 3.3 %collective-permute-start = (bf16[16,8192]{1,0:T(8,128)(2,1)S(1)}, bf16[16,8192]{1,0:T(8,128)(2,1)S(1)}, u32[]{:S(2)}, u32[]{:S(2)}) collective-permute-start(bf16[16,8192]{1,0:T(8,128)(2,1)S(1)} %get-tuple-element.58.refs_0_), channel_id=1, source_target_pairs={{0,8},{4,12},{8,0},{12,4},{1,9},{5,13},{9,1},{13,5},{2,10},{6,14},... | collective-permute-start | bytes 786440 | tf_op jit(solution)/shard_map/ppermute | solution.py:352
  35.0 2.6 %collective-permute-start.2 = (bf16[16,8192]{1,0:T(8,128)(2,1)S(1)}, bf16[16,8192]{1,0:T(8,128)(2,1)S(1)}, u32[]{:S(2)}, u32[]{:S(2)}) collective-permute-start(bf16[16,8192]{1,0:T(8,128)(2,1)S(1)} %get-tuple-element.58.refs_0_), channel_id=1, source_target_pairs={{0,12},{4,0},{8,4},{12,8},{1,13},{5,1},{9,5},{13,9},{2,14},{6,2},{... | collective-permute-start | bytes 786440 | tf_op jit(solution)/shard_map/ppermute | solution.py:352
  37.5 4.3 %collective-permute-done.refs_1_ = bf16[16,8192]{1,0:T(8,128)(2,1)S(1)} collective-permute-done((bf16[16,8192]{1,0:T(8,128)(2,1)S(1)}, bf16[16,8192]{1,0:T(8,128)(2,1)S(1)}, u32[]{:S(2)}, u32[]{:S(2)}) %collective-permute-start) | collective-permute-done | bytes 262176 | tf_op jit(solution)/shard_map/ppermute | solution.py:352
  41.8 3.2 %collective-permute-start.5 = (bf16[16,8192]{1,0:T(8,128)(2,1)S(1)}, bf16[16,8192]{1,0:T(8,128)(2,1)S(1)}, u32[]{:S(2)}, u32[]{:S(2)}) collective-permute-start(bf16[16,8192]{1,0:T(8,128)(2,1)S(1)} %get-tuple-element.74.refs_0_), channel_id=1, source_target_pairs={{0,8},{4,12},{8,0},{12,4},{1,9},{5,13},{9,1},{13,5},{2,10},{6,14},... | collective-permute-start | bytes 786440 | tf_op jit(solution)/shard_map/ppermute | solution.py:352
  45.0 2.3 %collective-permute-done.1.refs_2_ = bf16[16,8192]{1,0:T(8,128)(2,1)S(1)} collective-permute-done((bf16[16,8192]{1,0:T(8,128)(2,1)S(1)}, bf16[16,8192]{1,0:T(8,128)(2,1)S(1)}, u32[]{:S(2)}, u32[]{:S(2)}) %collective-permute-start.1) | collective-permute-done | bytes 262176 | tf_op jit(solution)/shard_map/ppermute | solution.py:352
  47.3 1.8 %collective-permute-start.6 = (bf16[16,8192]{1,0:T(8,128)(2,1)S(1)}, bf16[16,8192]{1,0:T(8,128)(2,1)S(1)}, u32[]{:S(2)}, u32[]{:S(2)}) collective-permute-start(bf16[16,8192]{1,0:T(8,128)(2,1)S(1)} %get-tuple-element.74.refs_0_), channel_id=1, source_target_pairs={{0,4},{4,8},{8,12},{12,0},{1,5},{5,9},{9,13},{13,1},{2,6},{6,10},{... | collective-permute-start | bytes 786440 | tf_op jit(solution)/shard_map/ppermute | solution.py:352
  49.1 1.5 %collective-permute-start.7 = (bf16[16,8192]{1,0:T(8,128)(2,1)S(1)}, bf16[16,8192]{1,0:T(8,128)(2,1)S(1)}, u32[]{:S(2)}, u32[]{:S(2)}) collective-permute-start(bf16[16,8192]{1,0:T(8,128)(2,1)S(1)} %get-tuple-element.74.refs_0_), channel_id=1, source_target_pairs={{0,12},{4,0},{8,4},{12,8},{1,13},{5,1},{9,5},{13,9},{2,14},{6,2},{... | collective-permute-start | bytes 786440 | tf_op jit(solution)/shard_map/ppermute | solution.py:352
  50.6 2.2 %copy-done.1 = bf16[8192,256]{1,0:T(8,128)(2,1)S(1)} copy-done((bf16[8192,256]{1,0:T(8,128)(2,1)S(1)}, bf16[8192,256]{1,0:T(8,128)(2,1)}, u32[]{:S(2)}) %copy-start.1) | copy-done | bytes 4194328
  52.8 4.4 %shard_map.114 = (f32[2,64,256]{2,1,0:T(8,128)S(1)}, bf16[64,256]{1,0:T(8,128)(2,1)S(1)}, bf16[32,8192]{1,0:T(8,128)(2,1)S(1)}, bf16[32,8192]{1,0:T(8,128)(2,1)}...) custom-call(bf16[16,8192]{1,0:T(8,128)(2,1)S(1)} %get-tuple-element., ...), custom_call_target="tpu_custom_call" | custom-call | bytes 100000 | tf_op jit(solution)/shard_map/pallas_call | solution.py:31
  58.0 1.4 %collective-permute-start.11 = (bf16[32,8192]{1,0:T(8,128)(2,1)S(1)}, bf16[32,8192]{1,0:T(8,128)(2,1)S(1)}, u32[]{:S(2)}, u32[]{:S(2)}) collective-permute-start(bf16[32,8192]{1,0:T(8,128)(2,1)S(1)} %get-tuple-element.73.refs_0_), channel_id=1, source_target_pairs={{0,1},{1,0},{2,3},{3,2},{4,5},{5,4},{6,7},{7,6},{8,9},{9,8},{10,11... | collective-permute-start | bytes 1572872 | tf_op jit(solution)/shard_map/ppermute | solution.py:358
  59.5 2.9 %collective-permute-start.8 = (bf16[16,8192]{1,0:T(8,128)(2,1)S(1)}, bf16[16,8192]{1,0:T(8,128)(2,1)S(1)}, u32[]{:S(2)}, u32[]{:S(2)}) collective-permute-start(bf16[16,8192]{1,0:T(8,128)(2,1)S(1)} %get-tuple-element.70), channel_id=1, source_target_pairs={{0,8},{4,12},{8,0},{12,4},{1,9},{5,13},{9,1},{13,5},{2,10},{6,14},... | collective-permute-start | bytes 786440 | tf_op jit(solution)/shard_map/ppermute | solution.py:362
  62.3 1.2 collective-permute-start.9
  64.4 6.2 %shard_map.116 = (bf16[64,384]{1,0:T(8,128)(2,1)S(1)}, bf16[64,8576]{1,0:T(8,128)(2,1)}, f32[16,8192]{1,0:T(8,128)S(1)}, bf16[16,8192]{1,0:T(8,128)(2,1)S(1)}, b...) custom-call(bf16[16,8192]{1,0:T(8,128)(2,1)S(1)} %get-tuple-element.74.refs_0_, ...), custom_call_target="tpu_custom_call" | custom-call | bytes 100000 | tf_op jit(solution)/shard_map/pallas_call | solution.py:31
  70.6 3.4 %collective-permute-done.9.refs_1_ = bf16[16,8192]{1,0:T(8,128)(2,1)S(1)} collective-permute-done((bf16[16,8192]{1,0:T(8,128)(2,1)S(1)}, bf16[16,8192]{1,0:T(8,128)(2,1)S(1)}, u32[]{:S(2)}, u32[]{:S(2)}) %collective-permute-start.9) | collective-permute-done | bytes 262176 | tf_op jit(solution)/shard_map/ppermute | solution.py:362
  76.8 3.3 %collective-permute-start.13 = (bf16[16,8192]{1,0:T(8,128)(2,1)}, bf16[16,8192]{1,0:T(8,128)(2,1)S(1)}, u32[]{:S(2)}, u32[]{:S(2)}) collective-permute-start(bf16[16,8192]{1,0:T(8,128)(2,1)} %copy-done.20), channel_id=1, source_target_pairs={{0,8},{4,12},{8,0},{12,4},{1,9},{5,13},{9,1},{13,5},{2,10},{6,14},... | collective-permute-start | bytes 786440 | tf_op jit(solution)/shard_map/ppermute | solution.py:362
  82.2 1.5 %collective-permute-start.16 = (bf16[128,384]{1,0:T(8,128)(2,1)S(1)}, bf16[128,384]{1,0:T(8,128)(2,1)S(1)}, u32[]{:S(2)}, u32[]{:S(2)}) collective-permute-start(bf16[128,384]{1,0:T(8,128)(2,1)S(1)} %pad_maximum_fusion.refs_8_), channel_id=1, source_target_pairs={{0,1},{1,0},{2,3},{3,2},{4,5},{5,4},{6,7},{7,6},{8,9},{9,8},{10,11... | collective-permute-start | bytes 294920 | tf_op jit(solution)/shard_map/ppermute | solution.py:358
  83.7 5.7 %shard_map.117 = (bf16[72,4096]{1,0:T(8,128)(2,1)S(1)}, bf16[72,4096]{1,0:T(8,128)(2,1)S(1)}) custom-call(bf16[16,8192]{1,0:T(8,128)(2,1)S(1)} %get-tuple-element.74.refs_0_, bf16[16,8192]{1,0:T(8,128)(2,1)S(1)} %collective-permute-done.5.refs_1_, bf16[16,8192]{1,0:T(8,128)(2,1)S(1)} %collective-permute-done.6.refs_2_, ...), custom_call_target="tpu_custom_call" | custom-call | bytes 100000 | tf_op jit(solution)/shard_map/pallas_call | solution.py:31
  89.4 3.1 %collective-permute-done.14.refs_1_ = bf16[16,8192]{1,0:T(8,128)(2,1)S(1)} collective-permute-done((bf16[16,8192]{1,0:T(8,128)(2,1)}, bf16[16,8192]{1,0:T(8,128)(2,1)S(1)}, u32[]{:S(2)}, u32[]{:S(2)}) %collective-permute-start.14) | collective-permute-done | bytes 262176 | tf_op jit(solution)/shard_map/ppermute | solution.py:362
  93.5 1.3 %shard_map.118 = bf16[16,2,64,128]{3,2,1,0:T(8,128)(2,1)} custom-call(bf16[16,64,128]{2,1,0:T(8,128)(2,1)S(1)} %shard_map.115.out_ref, f32[16,8192]{1,0:T(8,128)S(1)} %copy-done.12, bf16[16,8192]{1,0:T(8,128)(2,1)S(1)} %collective-permute-done.13.refs_0_, bf16[16,8192]{1,0:T(8,128)(2,1)S(1)} %collective-permute-done.14.refs_1_, ...), custom_call_target="tpu_custom_call" | custom-call | bytes 100000 | tf_op jit(solution)/shard_map/pallas_call | solution.py:31
  94.8 7.9 %all-to-all-start.1 = ((bf16[16,2,64,128]{3,2,1,0:T(8,128)(2,1)}), bf16[16,2,64,128]{3,2,1,0:T(8,128)(2,1)S(1)}, u32[]{:S(2)}, u32[]{:S(2)}) async-start(bf16[16,2,64,128]{3,2,1,0:T(8,128)(2,1)} %shard_map.118), calls=%async_computation.1 | async-start | bytes 1048576 | tf_op jit(solution)/shard_map/all_to_all | solution.py:371
  102.7 1.5 %collective-permute-start.18 = (bf16[72,4096]{1,0:T(8,128)(2,1)}, bf16[72,4096]{1,0:T(8,128)(2,1)S(1)}, u32[]{:S(2)}, u32[]{:S(2)}) collective-permute-start(bf16[72,4096]{1,0:T(8,128)(2,1)} %copy-done.18), channel_id=1, source_target_pairs={{0,1},{1,0},{2,3},{3,2},{4,5},{5,4},{6,7},{7,6},{8,9},{9,8},{10,11... | collective-permute-start | bytes 1769480 | tf_op jit(solution)/shard_map/ppermute | solution.py:358
  109.3 8.0 %shard_map.120 = (f32[36,2,4096]{2,1,0:T(2,128)}, f32[36,2,4096]{2,1,0:T(2,128)}) custom-call(bf16[32,8192]{1,0:T(8,128)(2,1)S(1)} %copy-done.6, bf16[32,8192]{1,0:T(8,128)(2,1)} %get-tuple-element.92.refs_1_, bf16[32,8192]{1,0:T(8,128)(2,1)S(1)} %collective-permute-done.19.refs_2_, bf16[32,8192]{1,0:T(8,128)(2,1)S(1)} %collective-permute-done.20.refs_3_, ...), custom_call_target="tpu_custom_call" | custom-call | bytes 100000 | tf_op jit(solution)/shard_map/pallas_call | solution.py:31
  117.3 2.6 %all-to-all-done.1.total_ref = bf16[16,2,64,128]{3,2,1,0:T(8,128)(2,1)S(1)} async-done(((bf16[16,2,64,128]{3,2,1,0:T(8,128)(2,1)}), bf16[16,2,64,128]{3,2,1,0:T(8,128)(2,1)S(1)}, u32[]{:S(2)}, u32[]{:S(2)}) %all-to-all-start.1) | async-done | bytes 524320 | tf_op jit(solution)/shard_map/all_to_all | solution.py:371
  120.8 2.4 %collective-permute-done.18.send_ref = bf16[72,4096]{1,0:T(8,128)(2,1)S(1)} collective-permute-done((bf16[72,4096]{1,0:T(8,128)(2,1)}, bf16[72,4096]{1,0:T(8,128)(2,1)S(1)}, u32[]{:S(2)}, u32[]{:S(2)}) %collective-permute-start.18) | collective-permute-done | bytes 589856 | tf_op jit(solution)/shard_map/ppermute | solution.py:358
  123.2 1.3 %shard_map.121 = f32[36,2,4096]{2,1,0:T(2,128)} custom-call(bf16[72,4096]{1,0:T(8,128)(2,1)S(1)} %get-tuple-element.107.keep_ref, bf16[72,4096]{1,0:T(8,128)(2,1)S(1)} %collective-permute-done.18.send_ref), custom_call_target="tpu_custom_call" | custom-call | bytes 100000 | tf_op jit(solution)/shard_map/pallas_call | solution.py:31
  (88 shorter events, 15.3 us)
Async XLA Ops:
  0.6 12.0 %copy-start.22 = (s32[3,2]{0,1:T(2,128)S(1)}, s32[3,2]{0,1:T(2,128)}, u32[]{:S(2)}) copy-start(s32[3,2]{0,1:T(2,128)} %param.13) | copy-start | bytes 76
  0.6 12.1 %copy-start.17 = (s32[3,2,72]{2,1,0:T(2,128)S(1)}, s32[3,2,72]{2,1,0:T(2,128)}, u32[]{:S(2)}) copy-start(s32[3,2,72]{2,1,0:T(2,128)} %index_ref.3) | copy-start | bytes 5188
  2.5 27.3 %all-to-all-start = ((bf16[16,2,64,128]{3,2,1,0:T(8,128)(2,1)}), bf16[16,2,64,128]{3,2,1,0:T(8,128)(2,1)S(1)}, u32[]{:S(2)}, u32[]{:S(2)}) async-start(bf16[16,2,64,128]{3,2,1,0:T(8,128)(2,1)} %shard_map.110), calls=%async_computation | async-start | bytes 1048576 | tf_op jit(solution)/shard_map/all_to_all | solution.py:371
  29.8 20.8 %collective-permute-start.3 = (bf16[8192,256]{1,0:T(8,128)(2,1)}, bf16[8192,256]{1,0:T(8,128)(2,1)S(1)}, u32[]{:S(2)}, u32[]{:S(2)}) collective-permute-start(bf16[8192,256]{1,0:T(8,128)(2,1)} %copy-done), channel_id=1, source_target_pairs={{0,2},{2,0},{1,3},{3,1},{4,6},{6,4},{5,7},{7,5},{8,10},{10,8},{9,1... | collective-permute-start | bytes 12582920 | tf_op jit(solution)/shard_map/ppermute | solution.py:355
  29.8 20.8 %collective-permute-start.4 = (bf16[128,8192]{1,0:T(8,128)(2,1)S(1)}, bf16[128,8192]{1,0:T(8,128)(2,1)S(1)}, u32[]{:S(2)}, u32[]{:S(2)}) collective-permute-start(bf16[128,8192]{1,0:T(8,128)(2,1)S(1)} %shard_map.112.refs_6_), channel_id=1, source_target_pairs={{0,2},{2,0},{1,3},{3,1},{4,6},{6,4},{5,7},{7,5},{8,10},{10,8},{9,1... | collective-permute-start | bytes 6291464 | tf_op jit(solution)/shard_map/ppermute | solution.py:355
  31.0 10.8 %collective-permute-start = (bf16[16,8192]{1,0:T(8,128)(2,1)S(1)}, bf16[16,8192]{1,0:T(8,128)(2,1)S(1)}, u32[]{:S(2)}, u32[]{:S(2)}) collective-permute-start(bf16[16,8192]{1,0:T(8,128)(2,1)S(1)} %get-tuple-element.58.refs_0_), channel_id=1, source_target_pairs={{0,8},{4,12},{8,0},{12,4},{1,9},{5,13},{9,1},{13,5},{2,10},{6,14},... | collective-permute-start | bytes 786440 | tf_op jit(solution)/shard_map/ppermute | solution.py:352
  34.3 13.1 %collective-permute-start.1 = (bf16[16,8192]{1,0:T(8,128)(2,1)S(1)}, bf16[16,8192]{1,0:T(8,128)(2,1)S(1)}, u32[]{:S(2)}, u32[]{:S(2)}) collective-permute-start(bf16[16,8192]{1,0:T(8,128)(2,1)S(1)} %get-tuple-element.58.refs_0_), channel_id=1, source_target_pairs={{0,4},{4,8},{8,12},{12,0},{1,5},{5,9},{9,13},{13,1},{2,6},{6,10},{... | collective-permute-start | bytes 786440 | tf_op jit(solution)/shard_map/ppermute | solution.py:352
  35.0 14.2 %collective-permute-start.2 = (bf16[16,8192]{1,0:T(8,128)(2,1)S(1)}, bf16[16,8192]{1,0:T(8,128)(2,1)S(1)}, u32[]{:S(2)}, u32[]{:S(2)}) collective-permute-start(bf16[16,8192]{1,0:T(8,128)(2,1)S(1)} %get-tuple-element.58.refs_0_), channel_id=1, source_target_pairs={{0,12},{4,0},{8,4},{12,8},{1,13},{5,1},{9,5},{13,9},{2,14},{6,2},{... | collective-permute-start | bytes 786440 | tf_op jit(solution)/shard_map/ppermute | solution.py:352
  41.8 15.4 %collective-permute-start.5 = (bf16[16,8192]{1,0:T(8,128)(2,1)S(1)}, bf16[16,8192]{1,0:T(8,128)(2,1)S(1)}, u32[]{:S(2)}, u32[]{:S(2)}) collective-permute-start(bf16[16,8192]{1,0:T(8,128)(2,1)S(1)} %get-tuple-element.74.refs_0_), channel_id=1, source_target_pairs={{0,8},{4,12},{8,0},{12,4},{1,9},{5,13},{9,1},{13,5},{2,10},{6,14},... | collective-permute-start | bytes 786440 | tf_op jit(solution)/shard_map/ppermute | solution.py:352
  47.3 10.4 %collective-permute-start.6 = (bf16[16,8192]{1,0:T(8,128)(2,1)S(1)}, bf16[16,8192]{1,0:T(8,128)(2,1)S(1)}, u32[]{:S(2)}, u32[]{:S(2)}) collective-permute-start(bf16[16,8192]{1,0:T(8,128)(2,1)S(1)} %get-tuple-element.74.refs_0_), channel_id=1, source_target_pairs={{0,4},{4,8},{8,12},{12,0},{1,5},{5,9},{9,13},{13,1},{2,6},{6,10},{... | collective-permute-start | bytes 786440 | tf_op jit(solution)/shard_map/ppermute | solution.py:352
  49.1 8.9 %collective-permute-start.7 = (bf16[16,8192]{1,0:T(8,128)(2,1)S(1)}, bf16[16,8192]{1,0:T(8,128)(2,1)S(1)}, u32[]{:S(2)}, u32[]{:S(2)}) collective-permute-start(bf16[16,8192]{1,0:T(8,128)(2,1)S(1)} %get-tuple-element.74.refs_0_), channel_id=1, source_target_pairs={{0,12},{4,0},{8,4},{12,8},{1,13},{5,1},{9,5},{13,9},{2,14},{6,2},{... | collective-permute-start | bytes 786440 | tf_op jit(solution)/shard_map/ppermute | solution.py:352
  57.2 13.4 %copy-start.5 = (bf16[32,8192]{1,0:T(8,128)(2,1)}, bf16[32,8192]{1,0:T(8,128)(2,1)S(1)}, u32[]{:S(2)}) copy-start(bf16[32,8192]{1,0:T(8,128)(2,1)S(1)} %get-tuple-element.73.refs_0_) | copy-start | bytes 1572868
  58.0 16.6 %collective-permute-start.11 = (bf16[32,8192]{1,0:T(8,128)(2,1)S(1)}, bf16[32,8192]{1,0:T(8,128)(2,1)S(1)}, u32[]{:S(2)}, u32[]{:S(2)}) collective-permute-start(bf16[32,8192]{1,0:T(8,128)(2,1)S(1)} %get-tuple-element.73.refs_0_), channel_id=1, source_target_pairs={{0,1},{1,0},{2,3},{3,2},{4,5},{5,4},{6,7},{7,6},{8,9},{9,8},{10,11... | collective-permute-start | bytes 1572872 | tf_op jit(solution)/shard_map/ppermute | solution.py:358
  59.5 11.1 %collective-permute-start.8 = (bf16[16,8192]{1,0:T(8,128)(2,1)S(1)}, bf16[16,8192]{1,0:T(8,128)(2,1)S(1)}, u32[]{:S(2)}, u32[]{:S(2)}) collective-permute-start(bf16[16,8192]{1,0:T(8,128)(2,1)S(1)} %get-tuple-element.70), channel_id=1, source_target_pairs={{0,8},{4,12},{8,0},{12,4},{1,9},{5,13},{9,1},{13,5},{2,10},{6,14},... | collective-permute-start | bytes 786440 | tf_op jit(solution)/shard_map/ppermute | solution.py:362
  62.3 11.7 %collective-permute-start.9 = (bf16[16,8192]{1,0:T(8,128)(2,1)S(1)}, bf16[16,8192]{1,0:T(8,128)(2,1)S(1)}, u32[]{:S(2)}, u32[]{:S(2)}) collective-permute-start(bf16[16,8192]{1,0:T(8,128)(2,1)S(1)} %get-tuple-element.71), channel_id=1, source_target_pairs={{0,12},{4,0},{8,4},{12,8},{1,13},{5,1},{9,5},{13,9},{2,14},{6,2},{... | collective-permute-start | bytes 786440 | tf_op jit(solution)/shard_map/ppermute | solution.py:362
  63.6 10.6 %collective-permute-start.10 = (bf16[16,8192]{1,0:T(8,128)(2,1)S(1)}, bf16[16,8192]{1,0:T(8,128)(2,1)S(1)}, u32[]{:S(2)}, u32[]{:S(2)}) collective-permute-start(bf16[16,8192]{1,0:T(8,128)(2,1)S(1)} %get-tuple-element.72), channel_id=1, source_target_pairs={{0,4},{4,8},{8,12},{12,0},{1,5},{5,9},{9,13},{13,1},{2,6},{6,10},{... | collective-permute-start | bytes 786440 | tf_op jit(solution)/shard_map/ppermute | solution.py:362
  75.4 6.7 %collective-permute-start.12 = (bf16[64,8576]{1,0:T(8,128)(2,1)}, bf16[64,8576]{1,0:T(8,128)(2,1)S(1)}, u32[]{:S(2)}, u32[]{:S(2)}) collective-permute-start(bf16[64,8576]{1,0:T(8,128)(2,1)} %get-tuple-element.86), channel_id=1, source_target_pairs={{0,2},{2,0},{1,3},{3,1},{4,6},{6,4},{5,7},{7,5},{8,10},{10,8},{9,1... | collective-permute-start | bytes 3293192 | tf_op jit(solution)/shard_map/ppermute | solution.py:355
  76.0 16.7 %collective-permute-start.17 = (bf16[32,8192]{1,0:T(8,128)(2,1)}, bf16[32,8192]{1,0:T(8,128)(2,1)S(1)}, u32[]{:S(2)}, u32[]{:S(2)}) collective-permute-start(bf16[32,8192]{1,0:T(8,128)(2,1)} %get-tuple-element.92.refs_1_), channel_id=1, source_target_pairs={{0,1},{1,0},{2,3},{3,2},{4,5},{5,4},{6,7},{7,6},{8,9},{9,8},{10,11... | collective-permute-start | bytes 1572872 | tf_op jit(solution)/shard_map/ppermute | solution.py:358
  76.8 12.6 %collective-permute-start.13 = (bf16[16,8192]{1,0:T(8,128)(2,1)}, bf16[16,8192]{1,0:T(8,128)(2,1)S(1)}, u32[]{:S(2)}, u32[]{:S(2)}) collective-permute-start(bf16[16,8192]{1,0:T(8,128)(2,1)} %copy-done.20), channel_id=1, source_target_pairs={{0,8},{4,12},{8,0},{12,4},{1,9},{5,13},{9,1},{13,5},{2,10},{6,14},... | collective-permute-start | bytes 786440 | tf_op jit(solution)/shard_map/ppermute | solution.py:362
  80.1 12.4 %collective-permute-start.14 = (bf16[16,8192]{1,0:T(8,128)(2,1)}, bf16[16,8192]{1,0:T(8,128)(2,1)S(1)}, u32[]{:S(2)}, u32[]{:S(2)}) collective-permute-start(bf16[16,8192]{1,0:T(8,128)(2,1)} %copy-done.19), channel_id=1, source_target_pairs={{0,12},{4,0},{8,4},{12,8},{1,13},{5,1},{9,5},{13,9},{2,14},{6,2},{... | collective-permute-start | bytes 786440 | tf_op jit(solution)/shard_map/ppermute | solution.py:362
  81.3 11.3 %collective-permute-start.15 = (bf16[16,8192]{1,0:T(8,128)(2,1)S(1)}, bf16[16,8192]{1,0:T(8,128)(2,1)S(1)}, u32[]{:S(2)}, u32[]{:S(2)}) collective-permute-start(bf16[16,8192]{1,0:T(8,128)(2,1)S(1)} %get-tuple-element.91), channel_id=1, source_target_pairs={{0,4},{4,8},{8,12},{12,0},{1,5},{5,9},{9,13},{13,1},{2,6},{6,10},{... | collective-permute-start | bytes 786440 | tf_op jit(solution)/shard_map/ppermute | solution.py:362
  82.2 11.3 %copy-start.12 = (f32[16,8192]{1,0:T(8,128)S(1)}, f32[16,8192]{1,0:T(8,128)}, u32[]{:S(2)}) copy-start(f32[16,8192]{1,0:T(8,128)} %copy-done.11) | copy-start | bytes 1572868
  82.2 10.5 %collective-permute-start.16 = (bf16[128,384]{1,0:T(8,128)(2,1)S(1)}, bf16[128,384]{1,0:T(8,128)(2,1)S(1)}, u32[]{:S(2)}, u32[]{:S(2)}) collective-permute-start(bf16[128,384]{1,0:T(8,128)(2,1)S(1)} %pad_maximum_fusion.refs_8_), channel_id=1, source_target_pairs={{0,1},{1,0},{2,3},{3,2},{4,5},{5,4},{6,7},{7,6},{8,9},{9,8},{10,11... | collective-permute-start | bytes 294920 | tf_op jit(solution)/shard_map/ppermute | solution.py:358
  93.5 11.3 %copy-start.8 = (bf16[32,8192]{1,0:T(8,128)(2,1)S(1)}, bf16[32,8192]{1,0:T(8,128)(2,1)}, u32[]{:S(2)}) copy-start(bf16[32,8192]{1,0:T(8,128)(2,1)} %copy-done.7) | copy-start | bytes 1572868
  93.5 11.3 %copy-start.10 = (bf16[32,8192]{1,0:T(8,128)(2,1)S(1)}, bf16[32,8192]{1,0:T(8,128)(2,1)}, u32[]{:S(2)}) copy-start(bf16[32,8192]{1,0:T(8,128)(2,1)} %copy-done.9) | copy-start | bytes 1572868
  94.8 13.6 %copy-start.14 = (bf16[128,384]{1,0:T(8,128)(2,1)S(1)}, bf16[128,384]{1,0:T(8,128)(2,1)}, u32[]{:S(2)}) copy-start(bf16[128,384]{1,0:T(8,128)(2,1)} %copy-done.13) | copy-start | bytes 294916
  94.8 25.1 %all-to-all-start.1 = ((bf16[16,2,64,128]{3,2,1,0:T(8,128)(2,1)}), bf16[16,2,64,128]{3,2,1,0:T(8,128)(2,1)S(1)}, u32[]{:S(2)}, u32[]{:S(2)}) async-start(bf16[16,2,64,128]{3,2,1,0:T(8,128)(2,1)} %shard_map.118), calls=%async_computation.1 | async-start | bytes 1048576 | tf_op jit(solution)/shard_map/all_to_all | solution.py:371
  102.7 20.5 %collective-permute-start.18 = (bf16[72,4096]{1,0:T(8,128)(2,1)}, bf16[72,4096]{1,0:T(8,128)(2,1)S(1)}, u32[]{:S(2)}, u32[]{:S(2)}) collective-permute-start(bf16[72,4096]{1,0:T(8,128)(2,1)} %copy-done.18), channel_id=1, source_target_pairs={{0,1},{1,0},{2,3},{3,2},{4,5},{5,4},{6,7},{7,6},{8,9},{9,8},{10,11... | collective-permute-start | bytes 1769480 | tf_op jit(solution)/shard_map/ppermute | solution.py:358
  104.2 2.6 %collective-permute-start.19 = (bf16[32,8192]{1,0:T(8,128)(2,1)S(1)}, bf16[32,8192]{1,0:T(8,128)(2,1)S(1)}, u32[]{:S(2)}, u32[]{:S(2)}) collective-permute-start(bf16[32,8192]{1,0:T(8,128)(2,1)S(1)} %copy-done.6), channel_id=1, source_target_pairs={{0,2},{2,0},{1,3},{3,1},{4,6},{6,4},{5,7},{7,5},{8,10},{10,8},{9,1... | collective-permute-start | bytes 1572872 | tf_op jit(solution)/shard_map/ppermute | solution.py:355
  104.2 3.2 %collective-permute-start.20 = (bf16[32,8192]{1,0:T(8,128)(2,1)}, bf16[32,8192]{1,0:T(8,128)(2,1)S(1)}, u32[]{:S(2)}, u32[]{:S(2)}) collective-permute-start(bf16[32,8192]{1,0:T(8,128)(2,1)} %get-tuple-element.92.refs_1_), channel_id=1, source_target_pairs={{0,2},{2,0},{1,3},{3,1},{4,6},{6,4},{5,7},{7,5},{8,10},{10,8},{9,1... | collective-permute-start | bytes 1572872 | tf_op jit(solution)/shard_map/ppermute | solution.py:355
  104.7 2.9 %collective-permute-start.21 = (bf16[32,8192]{1,0:T(8,128)(2,1)S(1)}, bf16[32,8192]{1,0:T(8,128)(2,1)S(1)}, u32[]{:S(2)}, u32[]{:S(2)}) collective-permute-start(bf16[32,8192]{1,0:T(8,128)(2,1)S(1)} %copy-done.8), channel_id=1, source_target_pairs={{0,2},{2,0},{1,3},{3,1},{4,6},{6,4},{5,7},{7,5},{8,10},{10,8},{9,1... | collective-permute-start | bytes 1572872 | tf_op jit(solution)/shard_map/ppermute | solution.py:355
  104.7 3.6 %collective-permute-start.22 = (bf16[32,8192]{1,0:T(8,128)(2,1)S(1)}, bf16[32,8192]{1,0:T(8,128)(2,1)S(1)}, u32[]{:S(2)}, u32[]{:S(2)}) collective-permute-start(bf16[32,8192]{1,0:T(8,128)(2,1)S(1)} %copy-done.10), channel_id=1, source_target_pairs={{0,2},{2,0},{1,3},{3,1},{4,6},{6,4},{5,7},{7,5},{8,10},{10,8},{9,1... | collective-permute-start | bytes 1572872 | tf_op jit(solution)/shard_map/ppermute | solution.py:355
  (16 other events, 69.1 us)

commit v5 on v4

--- a/solution.py
+++ b/solution.py
@@ -18,7 +18,7 @@
 ROWS = 16
 TOKENS = 4 * ROWS
 FAR = 16
-SHIFTS = (2, 1, 3)
+SHIFTS = (1, 3, 2)
 VMEM_BYTES = 14 * 1024 * 1024
 SMALL_BYTES = 8 * 1024 * 1024
 BF16 = jnp.bfloat16

time: 126 us -> 125 us (level)
  starting transfers between devices: 47.9 us -> 43.8 us
  waiting for transfers between devices: 23.5 us -> 26.6 us
    ppermute x6, waiting for transfers between devices: 6.75 us -> 9.51 us  [back(): lax.ppermute(part, 'y', ring(4, -shift))]
    ppermute x6, starting transfers between devices: 10.2 us -> 7.66 us  [back(): lax.ppermute(part, 'y', ring(4, -shift))]
    all_to_all x2, waiting for transfers between devices: 4.48 us -> 2.1 us  [exchange(): return lax.all_to_all(tiles, ('xh', 'z'), 0, 0, tiled=True)]
    ppermute x6, waiting for transfers between devices: 7.48 us -> 9.66 us  [along(): lax.ppermute(first, 'y', ring(4, shift))]
    ppermute x6, starting transfers between devices: 12.9 us -> 11.4 us  [along(): lax.ppermute(first, 'y', ring(4, shift))]
  transfers between devices with their start and end apart: 25 -> 25, of which waited for: 16 -> 14; matrix products, arithmetic and copies ran while one was open for 1% -> 1% of each run, Pallas kernels for 31% -> 31%
where the time goes in v5:
time: 125 us; the launch traced here: 124 us
  starting transfers between devices  43.8 us (35%)
  Pallas kernels  42.7 us (34%)
  waiting for transfers between devices  26.6 us (21%)
  local copies, waits for them, and re-layouts  9.36 us (7%)
    pallas_call x12, Pallas kernels, call(): pl.pallas_call(kernel, out_shape=outs, in_specs=[pl.BlockSpec(memory_spac...  42.7 us
    all_to_all x2, starting transfers between devices, exchange(): return lax.all_to_all(tiles, ('xh', 'z'), 0, 0, tiled=True)  18.1 us
    ppermute x6, starting transfers between devices, along(): lax.ppermute(first, 'y', ring(4, shift))  11.4 us
    ppermute x6, waiting for transfers between devices, along(): lax.ppermute(first, 'y', ring(4, shift))  9.66 us
    ppermute x6, waiting for transfers between devices, back(): lax.ppermute(part, 'y', ring(4, -shift))  9.51 us
    unnamed x47, local copies, waits for them, and re-layouts  8.1 us
    ppermute x6, starting transfers between devices, back(): lax.ppermute(part, 'y', ring(4, -shift))  7.66 us
    ppermute x4, starting transfers between devices, swap(): return lax.ppermute(piece, 'rep', ring(2, 1))  5.1 us
  transfers between devices with their start and end apart: 25, of which 14 were waited for; matrix products, arithmetic and copies ran while one was open for 1% of the time, Pallas kernels for 31%

profile of v5, /device:TPU:2, one launch (start us, length us, event | category | flops | bytes accessed | tf_op | source)
XLA Modules:
  0.0 123.7 jit_solution(8386128762865700590)
XLA Ops:
  0.7 1.8 %shard_map.110 = bf16[16,2,64,128]{3,2,1,0:T(8,128)(2,1)} custom-call(bf16[1,8192]{1,0:T(2,128)(2,1)} %act_ref.1, bf16[1,8192]{1,0:T(2,128)(2,1)} %cot_ref.1), custom_call_target="tpu_custom_call" | custom-call | bytes 100000 | tf_op jit(solution)/shard_map/pallas_call | solution.py:31
  2.5 10.1 %all-to-all-start = ((bf16[16,2,64,128]{3,2,1,0:T(8,128)(2,1)}), bf16[16,2,64,128]{3,2,1,0:T(8,128)(2,1)S(1)}, u32[]{:S(2)}, u32[]{:S(2)}) async-start(bf16[16,2,64,128]{3,2,1,0:T(8,128)(2,1)} %shard_map.110), calls=%async_computation | async-start | bytes 1048576 | tf_op jit(solution)/shard_map/all_to_all | solution.py:371
  14.0 8.4 %shard_map.112.refs_6_ = bf16[128,8192]{1,0:T(8,128)(2,1)S(1)} custom-call(s32[3,2,72]{2,1,0:T(2,128)S(1)} %copy-done.17, s32[3,2]{1,0:T(4,128)S(1)} %copy.16.count_ref, bf16[2,72,4096]{2,1,0:T(8,128)(2,1)S(1)} %copy-done.2), custom_call_target="tpu_custom_call" | custom-call | bytes 100000 | tf_op jit(solution)/shard_map/pallas_call | solution.py:31
  22.4 3.6 %shard_map.111.refs_4_ = bf16[8192,256]{1,0:T(8,128)(2,1)S(1)} custom-call(s32[3,2,72]{2,1,0:T(2,128)S(1)} %copy-done.17, s32[3,2]{1,0:T(4,128)S(1)} %copy.16.count_ref, bf16[2,72,4096]{2,1,0:T(8,128)(2,1)S(1)} %copy-done.3, bf16[2,72,4096]{2,1,0:T(8,128)(2,1)S(1)} %copy-done.4), custom_call_target="tpu_custom_call" | custom-call | bytes 100000 | tf_op jit(solution)/shard_map/pallas_call | solution.py:31
  26.0 2.0 %copy-done = bf16[8192,256]{1,0:T(8,128)(2,1)} copy-done((bf16[8192,256]{1,0:T(8,128)(2,1)}, bf16[8192,256]{1,0:T(8,128)(2,1)S(1)}, u32[]{:S(2)}) %copy-start) | copy-done | bytes 4194328
  28.0 1.8 %all-to-all-done.tiles_ref = bf16[16,2,64,128]{3,2,1,0:T(8,128)(2,1)S(1)} async-done(((bf16[16,2,64,128]{3,2,1,0:T(8,128)(2,1)}), bf16[16,2,64,128]{3,2,1,0:T(8,128)(2,1)S(1)}, u32[]{:S(2)}, u32[]{:S(2)}) %all-to-all-start) | async-done | bytes 524320 | tf_op jit(solution)/shard_map/all_to_all | solution.py:371
  31.0 1.7 %collective-permute-start = (bf16[16,8192]{1,0:T(8,128)(2,1)S(1)}, bf16[16,8192]{1,0:T(8,128)(2,1)S(1)}, u32[]{:S(2)}, u32[]{:S(2)}) collective-permute-start(bf16[16,8192]{1,0:T(8,128)(2,1)S(1)} %get-tuple-element.58.refs_0_), channel_id=1, source_target_pairs={{0,4},{4,8},{8,12},{12,0},{1,5},{5,9},{9,13},{13,1},{2,6},{6,10},{... | collective-permute-start | bytes 786440 | tf_op jit(solution)/shard_map/ppermute | solution.py:352
  32.7 1.7 %collective-permute-start.1 = (bf16[16,8192]{1,0:T(8,128)(2,1)S(1)}, bf16[16,8192]{1,0:T(8,128)(2,1)S(1)}, u32[]{:S(2)}, u32[]{:S(2)}) collective-permute-start(bf16[16,8192]{1,0:T(8,128)(2,1)S(1)} %get-tuple-element.58.refs_0_), channel_id=1, source_target_pairs={{0,12},{4,0},{8,4},{12,8},{1,13},{5,1},{9,5},{13,9},{2,14},{6,2},{... | collective-permute-start | bytes 786440 | tf_op jit(solution)/shard_map/ppermute | solution.py:352
  34.3 2.0 %collective-permute-start.2 = (bf16[16,8192]{1,0:T(8,128)(2,1)S(1)}, bf16[16,8192]{1,0:T(8,128)(2,1)S(1)}, u32[]{:S(2)}, u32[]{:S(2)}) collective-permute-start(bf16[16,8192]{1,0:T(8,128)(2,1)S(1)} %get-tuple-element.58.refs_0_), channel_id=1, source_target_pairs={{0,8},{4,12},{8,0},{12,4},{1,9},{5,13},{9,1},{13,5},{2,10},{6,14},... | collective-permute-start | bytes 786440 | tf_op jit(solution)/shard_map/ppermute | solution.py:352
  36.3 4.3 %collective-permute-done.refs_1_ = bf16[16,8192]{1,0:T(8,128)(2,1)S(1)} collective-permute-done((bf16[16,8192]{1,0:T(8,128)(2,1)S(1)}, bf16[16,8192]{1,0:T(8,128)(2,1)S(1)}, u32[]{:S(2)}, u32[]{:S(2)}) %collective-permute-start) | collective-permute-done | bytes 262176 | tf_op jit(solution)/shard_map/ppermute | solution.py:352
  41.8 2.6 %collective-permute-done.1.refs_2_ = bf16[16,8192]{1,0:T(8,128)(2,1)S(1)} collective-permute-done((bf16[16,8192]{1,0:T(8,128)(2,1)S(1)}, bf16[16,8192]{1,0:T(8,128)(2,1)S(1)}, u32[]{:S(2)}, u32[]{:S(2)}) %collective-permute-start.1) | collective-permute-done | bytes 262176 | tf_op jit(solution)/shard_map/ppermute | solution.py:352
  44.4 4.2 %collective-permute-start.6 = (bf16[16,8192]{1,0:T(8,128)(2,1)S(1)}, bf16[16,8192]{1,0:T(8,128)(2,1)S(1)}, u32[]{:S(2)}, u32[]{:S(2)}) collective-permute-start(bf16[16,8192]{1,0:T(8,128)(2,1)S(1)} %get-tuple-element.74.refs_0_), channel_id=1, source_target_pairs={{0,12},{4,0},{8,4},{12,8},{1,13},{5,1},{9,5},{13,9},{2,14},{6,2},{... | collective-permute-start | bytes 786440 | tf_op jit(solution)/shard_map/ppermute | solution.py:352
  49.2 2.2 %copy-done.1 = bf16[8192,256]{1,0:T(8,128)(2,1)S(1)} copy-done((bf16[8192,256]{1,0:T(8,128)(2,1)S(1)}, bf16[8192,256]{1,0:T(8,128)(2,1)}, u32[]{:S(2)}) %copy-start.1) | copy-done | bytes 4194328
  51.4 4.4 %shard_map.114 = (f32[2,64,256]{2,1,0:T(8,128)S(1)}, bf16[64,256]{1,0:T(8,128)(2,1)S(1)}, bf16[32,8192]{1,0:T(8,128)(2,1)S(1)}, bf16[32,8192]{1,0:T(8,128)(2,1)}...) custom-call(bf16[16,8192]{1,0:T(8,128)(2,1)S(1)} %get-tuple-element., ...), custom_call_target="tpu_custom_call" | custom-call | bytes 100000 | tf_op jit(solution)/shard_map/pallas_call | solution.py:31
  55.8 1.6 %collective-permute-done.6.refs_2_ = bf16[16,8192]{1,0:T(8,128)(2,1)S(1)} collective-permute-done((bf16[16,8192]{1,0:T(8,128)(2,1)S(1)}, bf16[16,8192]{1,0:T(8,128)(2,1)S(1)}, u32[]{:S(2)}, u32[]{:S(2)}) %collective-permute-start.6) | collective-permute-done | bytes 262176 | tf_op jit(solution)/shard_map/ppermute | solution.py:352
  58.6 1.4 %collective-permute-start.11 = (bf16[32,8192]{1,0:T(8,128)(2,1)S(1)}, bf16[32,8192]{1,0:T(8,128)(2,1)S(1)}, u32[]{:S(2)}, u32[]{:S(2)}) collective-permute-start(bf16[32,8192]{1,0:T(8,128)(2,1)S(1)} %get-tuple-element.73.refs_0_), channel_id=1, source_target_pairs={{0,1},{1,0},{2,3},{3,2},{4,5},{5,4},{6,7},{7,6},{8,9},{9,8},{10,11... | collective-permute-start | bytes 1572872 | tf_op jit(solution)/shard_map/ppermute | solution.py:358
  60.1 2.5 %collective-permute-start.8 = (bf16[16,8192]{1,0:T(8,128)(2,1)S(1)}, bf16[16,8192]{1,0:T(8,128)(2,1)S(1)}, u32[]{:S(2)}, u32[]{:S(2)}) collective-permute-start(bf16[16,8192]{1,0:T(8,128)(2,1)S(1)} %get-tuple-element.70), channel_id=1, source_target_pairs={{0,12},{4,0},{8,4},{12,8},{1,13},{5,1},{9,5},{13,9},{2,14},{6,2},{... | collective-permute-start | bytes 786440 | tf_op jit(solution)/shard_map/ppermute | solution.py:362
  62.6 1.5 %collective-permute-start.10 = (bf16[16,8192]{1,0:T(8,128)(2,1)S(1)}, bf16[16,8192]{1,0:T(8,128)(2,1)S(1)}, u32[]{:S(2)}, u32[]{:S(2)}) collective-permute-start(bf16[16,8192]{1,0:T(8,128)(2,1)S(1)} %get-tuple-element.72), channel_id=1, source_target_pairs={{0,8},{4,12},{8,0},{12,4},{1,9},{5,13},{9,1},{13,5},{2,10},{6,14},... | collective-permute-start | bytes 786440 | tf_op jit(solution)/shard_map/ppermute | solution.py:362
  64.0 6.2 %shard_map.116 = (bf16[64,384]{1,0:T(8,128)(2,1)S(1)}, bf16[64,8576]{1,0:T(8,128)(2,1)}, f32[16,8192]{1,0:T(8,128)S(1)}, bf16[16,8192]{1,0:T(8,128)(2,1)S(1)}, b...) custom-call(bf16[16,8192]{1,0:T(8,128)(2,1)S(1)} %get-tuple-element.74.refs_0_, ...), custom_call_target="tpu_custom_call" | custom-call | bytes 100000 | tf_op jit(solution)/shard_map/pallas_call | solution.py:31
  70.3 1.6 %collective-permute-done.8.refs_0_ = bf16[16,8192]{1,0:T(8,128)(2,1)S(1)} collective-permute-done((bf16[16,8192]{1,0:T(8,128)(2,1)S(1)}, bf16[16,8192]{1,0:T(8,128)(2,1)S(1)}, u32[]{:S(2)}, u32[]{:S(2)}) %collective-permute-start.8) | collective-permute-done | bytes 262176 | tf_op jit(solution)/shard_map/ppermute | solution.py:362
  71.8 2.2 %collective-permute-done.9.refs_1_ = bf16[16,8192]{1,0:T(8,128)(2,1)S(1)} collective-permute-done((bf16[16,8192]{1,0:T(8,128)(2,1)S(1)}, bf16[16,8192]{1,0:T(8,128)(2,1)S(1)}, u32[]{:S(2)}, u32[]{:S(2)}) %collective-permute-start.9) | collective-permute-done | bytes 262176 | tf_op jit(solution)/shard_map/ppermute | solution.py:362
  76.6 1.6 %collective-permute-start.13 = (bf16[16,8192]{1,0:T(8,128)(2,1)}, bf16[16,8192]{1,0:T(8,128)(2,1)S(1)}, u32[]{:S(2)}, u32[]{:S(2)}) collective-permute-start(bf16[16,8192]{1,0:T(8,128)(2,1)} %copy-done.20), channel_id=1, source_target_pairs={{0,12},{4,0},{8,4},{12,8},{1,13},{5,1},{9,5},{13,9},{2,14},{6,2},{... | collective-permute-start | bytes 786440 | tf_op jit(solution)/shard_map/ppermute | solution.py:362
  78.7 1.6 %collective-permute-start.15 = (bf16[16,8192]{1,0:T(8,128)(2,1)S(1)}, bf16[16,8192]{1,0:T(8,128)(2,1)S(1)}, u32[]{:S(2)}, u32[]{:S(2)}) collective-permute-start(bf16[16,8192]{1,0:T(8,128)(2,1)S(1)} %get-tuple-element.91), channel_id=1, source_target_pairs={{0,8},{4,12},{8,0},{12,4},{1,9},{5,13},{9,1},{13,5},{2,10},{6,14},... | collective-permute-start | bytes 786440 | tf_op jit(solution)/shard_map/ppermute | solution.py:362
  80.4 1.5 %collective-permute-start.16 = (bf16[128,384]{1,0:T(8,128)(2,1)S(1)}, bf16[128,384]{1,0:T(8,128)(2,1)S(1)}, u32[]{:S(2)}, u32[]{:S(2)}) collective-permute-start(bf16[128,384]{1,0:T(8,128)(2,1)S(1)} %pad_maximum_fusion.refs_8_), channel_id=1, source_target_pairs={{0,1},{1,0},{2,3},{3,2},{4,5},{5,4},{6,7},{7,6},{8,9},{9,8},{10,11... | collective-permute-start | bytes 294920 | tf_op jit(solution)/shard_map/ppermute | solution.py:358
  81.9 5.7 %shard_map.117 = (bf16[72,4096]{1,0:T(8,128)(2,1)S(1)}, bf16[72,4096]{1,0:T(8,128)(2,1)S(1)}) custom-call(bf16[16,8192]{1,0:T(8,128)(2,1)S(1)} %get-tuple-element.74.refs_0_, bf16[16,8192]{1,0:T(8,128)(2,1)S(1)} %collective-permute-done.5.refs_1_, bf16[16,8192]{1,0:T(8,128)(2,1)S(1)} %collective-permute-done.6.refs_2_, ...), custom_call_target="tpu_custom_call" | custom-call | bytes 100000 | tf_op jit(solution)/shard_map/pallas_call | solution.py:31
  87.6 5.8 %collective-permute-done.14.refs_1_ = bf16[16,8192]{1,0:T(8,128)(2,1)S(1)} collective-permute-done((bf16[16,8192]{1,0:T(8,128)(2,1)}, bf16[16,8192]{1,0:T(8,128)(2,1)S(1)}, u32[]{:S(2)}, u32[]{:S(2)}) %collective-permute-start.14) | collective-permute-done | bytes 262176 | tf_op jit(solution)/shard_map/ppermute | solution.py:362
  94.2 1.3 %shard_map.118 = bf16[16,2,64,128]{3,2,1,0:T(8,128)(2,1)} custom-call(bf16[16,64,128]{2,1,0:T(8,128)(2,1)S(1)} %shard_map.115.out_ref, f32[16,8192]{1,0:T(8,128)S(1)} %copy-done.12, bf16[16,8192]{1,0:T(8,128)(2,1)S(1)} %collective-permute-done.13.refs_0_, bf16[16,8192]{1,0:T(8,128)(2,1)S(1)} %collective-permute-done.14.refs_1_, ...), custom_call_target="tpu_custom_call" | custom-call | bytes 100000 | tf_op jit(solution)/shard_map/pallas_call | solution.py:31
  95.6 8.0 %all-to-all-start.1 = ((bf16[16,2,64,128]{3,2,1,0:T(8,128)(2,1)}), bf16[16,2,64,128]{3,2,1,0:T(8,128)(2,1)S(1)}, u32[]{:S(2)}, u32[]{:S(2)}) async-start(bf16[16,2,64,128]{3,2,1,0:T(8,128)(2,1)} %shard_map.118), calls=%async_computation.1 | async-start | bytes 1048576 | tf_op jit(solution)/shard_map/all_to_all | solution.py:371
  103.5 1.5 %collective-permute-start.18 = (bf16[72,4096]{1,0:T(8,128)(2,1)}, bf16[72,4096]{1,0:T(8,128)(2,1)S(1)}, u32[]{:S(2)}, u32[]{:S(2)}) collective-permute-start(bf16[72,4096]{1,0:T(8,128)(2,1)} %copy-done.18), channel_id=1, source_target_pairs={{0,1},{1,0},{2,3},{3,2},{4,5},{5,4},{6,7},{7,6},{8,9},{9,8},{10,11... | collective-permute-start | bytes 1769480 | tf_op jit(solution)/shard_map/ppermute | solution.py:358
  110.1 8.0 %shard_map.120 = (f32[36,2,4096]{2,1,0:T(2,128)}, f32[36,2,4096]{2,1,0:T(2,128)}) custom-call(bf16[32,8192]{1,0:T(8,128)(2,1)S(1)} %copy-done.6, bf16[32,8192]{1,0:T(8,128)(2,1)} %get-tuple-element.92.refs_1_, bf16[32,8192]{1,0:T(8,128)(2,1)S(1)} %collective-permute-done.19.refs_2_, bf16[32,8192]{1,0:T(8,128)(2,1)S(1)} %collective-permute-done.20.refs_3_, ...), custom_call_target="tpu_custom_call" | custom-call | bytes 100000 | tf_op jit(solution)/shard_map/pallas_call | solution.py:31
  119.2 3.1 %collective-permute-done.18.send_ref = bf16[72,4096]{1,0:T(8,128)(2,1)S(1)} collective-permute-done((bf16[72,4096]{1,0:T(8,128)(2,1)}, bf16[72,4096]{1,0:T(8,128)(2,1)S(1)}, u32[]{:S(2)}, u32[]{:S(2)}) %collective-permute-start.18) | collective-permute-done | bytes 589856 | tf_op jit(solution)/shard_map/ppermute | solution.py:358
  122.3 1.3 %shard_map.121 = f32[36,2,4096]{2,1,0:T(2,128)} custom-call(bf16[72,4096]{1,0:T(8,128)(2,1)S(1)} %get-tuple-element.107.keep_ref, bf16[72,4096]{1,0:T(8,128)(2,1)S(1)} %collective-permute-done.18.send_ref), custom_call_target="tpu_custom_call" | custom-call | bytes 100000 | tf_op jit(solution)/shard_map/pallas_call | solution.py:31
  (88 shorter events, 15.7 us)
Async XLA Ops:
  0.6 12.0 %copy-start.22 = (s32[3,2]{0,1:T(2,128)S(1)}, s32[3,2]{0,1:T(2,128)}, u32[]{:S(2)}) copy-start(s32[3,2]{0,1:T(2,128)} %param.13) | copy-start | bytes 76
  0.6 12.1 %copy-start.17 = (s32[3,2,72]{2,1,0:T(2,128)S(1)}, s32[3,2,72]{2,1,0:T(2,128)}, u32[]{:S(2)}) copy-start(s32[3,2,72]{2,1,0:T(2,128)} %index_ref.3) | copy-start | bytes 5188
  2.5 27.3 %all-to-all-start = ((bf16[16,2,64,128]{3,2,1,0:T(8,128)(2,1)}), bf16[16,2,64,128]{3,2,1,0:T(8,128)(2,1)S(1)}, u32[]{:S(2)}, u32[]{:S(2)}) async-start(bf16[16,2,64,128]{3,2,1,0:T(8,128)(2,1)} %shard_map.110), calls=%async_computation | async-start | bytes 1048576 | tf_op jit(solution)/shard_map/all_to_all | solution.py:371
  29.8 19.4 %collective-permute-start.3 = (bf16[8192,256]{1,0:T(8,128)(2,1)}, bf16[8192,256]{1,0:T(8,128)(2,1)S(1)}, u32[]{:S(2)}, u32[]{:S(2)}) collective-permute-start(bf16[8192,256]{1,0:T(8,128)(2,1)} %copy-done), channel_id=1, source_target_pairs={{0,2},{2,0},{1,3},{3,1},{4,6},{6,4},{5,7},{7,5},{8,10},{10,8},{9,1... | collective-permute-start | bytes 12582920 | tf_op jit(solution)/shard_map/ppermute | solution.py:355
  29.8 19.4 %collective-permute-start.4 = (bf16[128,8192]{1,0:T(8,128)(2,1)S(1)}, bf16[128,8192]{1,0:T(8,128)(2,1)S(1)}, u32[]{:S(2)}, u32[]{:S(2)}) collective-permute-start(bf16[128,8192]{1,0:T(8,128)(2,1)S(1)} %shard_map.112.refs_6_), channel_id=1, source_target_pairs={{0,2},{2,0},{1,3},{3,1},{4,6},{6,4},{5,7},{7,5},{8,10},{10,8},{9,1... | collective-permute-start | bytes 6291464 | tf_op jit(solution)/shard_map/ppermute | solution.py:355
  31.0 9.6 %collective-permute-start = (bf16[16,8192]{1,0:T(8,128)(2,1)S(1)}, bf16[16,8192]{1,0:T(8,128)(2,1)S(1)}, u32[]{:S(2)}, u32[]{:S(2)}) collective-permute-start(bf16[16,8192]{1,0:T(8,128)(2,1)S(1)} %get-tuple-element.58.refs_0_), channel_id=1, source_target_pairs={{0,4},{4,8},{8,12},{12,0},{1,5},{5,9},{9,13},{13,1},{2,6},{6,10},{... | collective-permute-start | bytes 786440 | tf_op jit(solution)/shard_map/ppermute | solution.py:352
  32.7 11.8 %collective-permute-start.1 = (bf16[16,8192]{1,0:T(8,128)(2,1)S(1)}, bf16[16,8192]{1,0:T(8,128)(2,1)S(1)}, u32[]{:S(2)}, u32[]{:S(2)}) collective-permute-start(bf16[16,8192]{1,0:T(8,128)(2,1)S(1)} %get-tuple-element.58.refs_0_), channel_id=1, source_target_pairs={{0,12},{4,0},{8,4},{12,8},{1,13},{5,1},{9,5},{13,9},{2,14},{6,2},{... | collective-permute-start | bytes 786440 | tf_op jit(solution)/shard_map/ppermute | solution.py:352
  34.3 14.3 %collective-permute-start.2 = (bf16[16,8192]{1,0:T(8,128)(2,1)S(1)}, bf16[16,8192]{1,0:T(8,128)(2,1)S(1)}, u32[]{:S(2)}, u32[]{:S(2)}) collective-permute-start(bf16[16,8192]{1,0:T(8,128)(2,1)S(1)} %get-tuple-element.58.refs_0_), channel_id=1, source_target_pairs={{0,8},{4,12},{8,0},{12,4},{1,9},{5,13},{9,1},{13,5},{2,10},{6,14},... | collective-permute-start | bytes 786440 | tf_op jit(solution)/shard_map/ppermute | solution.py:352
  40.6 15.3 %collective-permute-start.5 = (bf16[16,8192]{1,0:T(8,128)(2,1)S(1)}, bf16[16,8192]{1,0:T(8,128)(2,1)S(1)}, u32[]{:S(2)}, u32[]{:S(2)}) collective-permute-start(bf16[16,8192]{1,0:T(8,128)(2,1)S(1)} %get-tuple-element.74.refs_0_), channel_id=1, source_target_pairs={{0,4},{4,8},{8,12},{12,0},{1,5},{5,9},{9,13},{13,1},{2,6},{6,10},{... | collective-permute-start | bytes 786440 | tf_op jit(solution)/shard_map/ppermute | solution.py:352
  44.4 13.1 %collective-permute-start.6 = (bf16[16,8192]{1,0:T(8,128)(2,1)S(1)}, bf16[16,8192]{1,0:T(8,128)(2,1)S(1)}, u32[]{:S(2)}, u32[]{:S(2)}) collective-permute-start(bf16[16,8192]{1,0:T(8,128)(2,1)S(1)} %get-tuple-element.74.refs_0_), channel_id=1, source_target_pairs={{0,12},{4,0},{8,4},{12,8},{1,13},{5,1},{9,5},{13,9},{2,14},{6,2},{... | collective-permute-start | bytes 786440 | tf_op jit(solution)/shard_map/ppermute | solution.py:352
  48.6 10.0 %collective-permute-start.7 = (bf16[16,8192]{1,0:T(8,128)(2,1)S(1)}, bf16[16,8192]{1,0:T(8,128)(2,1)S(1)}, u32[]{:S(2)}, u32[]{:S(2)}) collective-permute-start(bf16[16,8192]{1,0:T(8,128)(2,1)S(1)} %get-tuple-element.74.refs_0_), channel_id=1, source_target_pairs={{0,8},{4,12},{8,0},{12,4},{1,9},{5,13},{9,1},{13,5},{2,10},{6,14},... | collective-permute-start | bytes 786440 | tf_op jit(solution)/shard_map/ppermute | solution.py:352
  55.8 14.4 %copy-start.5 = (bf16[32,8192]{1,0:T(8,128)(2,1)}, bf16[32,8192]{1,0:T(8,128)(2,1)S(1)}, u32[]{:S(2)}) copy-start(bf16[32,8192]{1,0:T(8,128)(2,1)S(1)} %get-tuple-element.73.refs_0_) | copy-start | bytes 1572868
  58.6 15.8 %collective-permute-start.11 = (bf16[32,8192]{1,0:T(8,128)(2,1)S(1)}, bf16[32,8192]{1,0:T(8,128)(2,1)S(1)}, u32[]{:S(2)}, u32[]{:S(2)}) collective-permute-start(bf16[32,8192]{1,0:T(8,128)(2,1)S(1)} %get-tuple-element.73.refs_0_), channel_id=1, source_target_pairs={{0,1},{1,0},{2,3},{3,2},{4,5},{5,4},{6,7},{7,6},{8,9},{9,8},{10,11... | collective-permute-start | bytes 1572872 | tf_op jit(solution)/shard_map/ppermute | solution.py:358
  60.1 11.8 %collective-permute-start.8 = (bf16[16,8192]{1,0:T(8,128)(2,1)S(1)}, bf16[16,8192]{1,0:T(8,128)(2,1)S(1)}, u32[]{:S(2)}, u32[]{:S(2)}) collective-permute-start(bf16[16,8192]{1,0:T(8,128)(2,1)S(1)} %get-tuple-element.70), channel_id=1, source_target_pairs={{0,12},{4,0},{8,4},{12,8},{1,13},{5,1},{9,5},{13,9},{2,14},{6,2},{... | collective-permute-start | bytes 786440 | tf_op jit(solution)/shard_map/ppermute | solution.py:362
  62.6 11.4 %collective-permute-start.9 = (bf16[16,8192]{1,0:T(8,128)(2,1)S(1)}, bf16[16,8192]{1,0:T(8,128)(2,1)S(1)}, u32[]{:S(2)}, u32[]{:S(2)}) collective-permute-start(bf16[16,8192]{1,0:T(8,128)(2,1)S(1)} %get-tuple-element.71), channel_id=1, source_target_pairs={{0,4},{4,8},{8,12},{12,0},{1,5},{5,9},{9,13},{13,1},{2,6},{6,10},{... | collective-permute-start | bytes 786440 | tf_op jit(solution)/shard_map/ppermute | solution.py:362
  62.6 11.4 %collective-permute-start.10 = (bf16[16,8192]{1,0:T(8,128)(2,1)S(1)}, bf16[16,8192]{1,0:T(8,128)(2,1)S(1)}, u32[]{:S(2)}, u32[]{:S(2)}) collective-permute-start(bf16[16,8192]{1,0:T(8,128)(2,1)S(1)} %get-tuple-element.72), channel_id=1, source_target_pairs={{0,8},{4,12},{8,0},{12,4},{1,9},{5,13},{9,1},{13,5},{2,10},{6,14},... | collective-permute-start | bytes 786440 | tf_op jit(solution)/shard_map/ppermute | solution.py:362
  75.3 5.0 %collective-permute-start.12 = (bf16[64,8576]{1,0:T(8,128)(2,1)}, bf16[64,8576]{1,0:T(8,128)(2,1)S(1)}, u32[]{:S(2)}, u32[]{:S(2)}) collective-permute-start(bf16[64,8576]{1,0:T(8,128)(2,1)} %get-tuple-element.86), channel_id=1, source_target_pairs={{0,2},{2,0},{1,3},{3,1},{4,6},{6,4},{5,7},{7,5},{8,10},{10,8},{9,1... | collective-permute-start | bytes 3293192 | tf_op jit(solution)/shard_map/ppermute | solution.py:355
  75.8 17.6 %collective-permute-start.17 = (bf16[32,8192]{1,0:T(8,128)(2,1)}, bf16[32,8192]{1,0:T(8,128)(2,1)S(1)}, u32[]{:S(2)}, u32[]{:S(2)}) collective-permute-start(bf16[32,8192]{1,0:T(8,128)(2,1)} %get-tuple-element.92.refs_1_), channel_id=1, source_target_pairs={{0,1},{1,0},{2,3},{3,2},{4,5},{5,4},{6,7},{7,6},{8,9},{9,8},{10,11... | collective-permute-start | bytes 1572872 | tf_op jit(solution)/shard_map/ppermute | solution.py:358
  76.6 11.0 %collective-permute-start.13 = (bf16[16,8192]{1,0:T(8,128)(2,1)}, bf16[16,8192]{1,0:T(8,128)(2,1)S(1)}, u32[]{:S(2)}, u32[]{:S(2)}) collective-permute-start(bf16[16,8192]{1,0:T(8,128)(2,1)} %copy-done.20), channel_id=1, source_target_pairs={{0,12},{4,0},{8,4},{12,8},{1,13},{5,1},{9,5},{13,9},{2,14},{6,2},{... | collective-permute-start | bytes 786440 | tf_op jit(solution)/shard_map/ppermute | solution.py:362
  78.2 15.2 %collective-permute-start.14 = (bf16[16,8192]{1,0:T(8,128)(2,1)}, bf16[16,8192]{1,0:T(8,128)(2,1)S(1)}, u32[]{:S(2)}, u32[]{:S(2)}) collective-permute-start(bf16[16,8192]{1,0:T(8,128)(2,1)} %copy-done.19), channel_id=1, source_target_pairs={{0,4},{4,8},{8,12},{12,0},{1,5},{5,9},{9,13},{13,1},{2,6},{6,10},{... | collective-permute-start | bytes 786440 | tf_op jit(solution)/shard_map/ppermute | solution.py:362
  78.7 14.7 %collective-permute-start.15 = (bf16[16,8192]{1,0:T(8,128)(2,1)S(1)}, bf16[16,8192]{1,0:T(8,128)(2,1)S(1)}, u32[]{:S(2)}, u32[]{:S(2)}) collective-permute-start(bf16[16,8192]{1,0:T(8,128)(2,1)S(1)} %get-tuple-element.91), channel_id=1, source_target_pairs={{0,8},{4,12},{8,0},{12,4},{1,9},{5,13},{9,1},{13,5},{2,10},{6,14},... | collective-permute-start | bytes 786440 | tf_op jit(solution)/shard_map/ppermute | solution.py:362
  80.3 13.9 %copy-start.12 = (f32[16,8192]{1,0:T(8,128)S(1)}, f32[16,8192]{1,0:T(8,128)}, u32[]{:S(2)}) copy-start(f32[16,8192]{1,0:T(8,128)} %copy-done.11) | copy-start | bytes 1572868
  80.4 13.0 %collective-permute-start.16 = (bf16[128,384]{1,0:T(8,128)(2,1)S(1)}, bf16[128,384]{1,0:T(8,128)(2,1)S(1)}, u32[]{:S(2)}, u32[]{:S(2)}) collective-permute-start(bf16[128,384]{1,0:T(8,128)(2,1)S(1)} %pad_maximum_fusion.refs_8_), channel_id=1, source_target_pairs={{0,1},{1,0},{2,3},{3,2},{4,5},{5,4},{6,7},{7,6},{8,9},{9,8},{10,11... | collective-permute-start | bytes 294920 | tf_op jit(solution)/shard_map/ppermute | solution.py:358
  94.2 11.3 %copy-start.8 = (bf16[32,8192]{1,0:T(8,128)(2,1)S(1)}, bf16[32,8192]{1,0:T(8,128)(2,1)}, u32[]{:S(2)}) copy-start(bf16[32,8192]{1,0:T(8,128)(2,1)} %copy-done.7) | copy-start | bytes 1572868
  94.2 11.3 %copy-start.10 = (bf16[32,8192]{1,0:T(8,128)(2,1)S(1)}, bf16[32,8192]{1,0:T(8,128)(2,1)}, u32[]{:S(2)}) copy-start(bf16[32,8192]{1,0:T(8,128)(2,1)} %copy-done.9) | copy-start | bytes 1572868
  95.6 13.6 %copy-start.14 = (bf16[128,384]{1,0:T(8,128)(2,1)S(1)}, bf16[128,384]{1,0:T(8,128)(2,1)}, u32[]{:S(2)}) copy-start(bf16[128,384]{1,0:T(8,128)(2,1)} %copy-done.13) | copy-start | bytes 294916
  95.6 22.8 %all-to-all-start.1 = ((bf16[16,2,64,128]{3,2,1,0:T(8,128)(2,1)}), bf16[16,2,64,128]{3,2,1,0:T(8,128)(2,1)S(1)}, u32[]{:S(2)}, u32[]{:S(2)}) async-start(bf16[16,2,64,128]{3,2,1,0:T(8,128)(2,1)} %shard_map.118), calls=%async_computation.1 | async-start | bytes 1048576 | tf_op jit(solution)/shard_map/all_to_all | solution.py:371
  103.5 18.7 %collective-permute-start.18 = (bf16[72,4096]{1,0:T(8,128)(2,1)}, bf16[72,4096]{1,0:T(8,128)(2,1)S(1)}, u32[]{:S(2)}, u32[]{:S(2)}) collective-permute-start(bf16[72,4096]{1,0:T(8,128)(2,1)} %copy-done.18), channel_id=1, source_target_pairs={{0,1},{1,0},{2,3},{3,2},{4,5},{5,4},{6,7},{7,6},{8,9},{9,8},{10,11... | collective-permute-start | bytes 1769480 | tf_op jit(solution)/shard_map/ppermute | solution.py:358
  105.0 2.6 %collective-permute-start.19 = (bf16[32,8192]{1,0:T(8,128)(2,1)S(1)}, bf16[32,8192]{1,0:T(8,128)(2,1)S(1)}, u32[]{:S(2)}, u32[]{:S(2)}) collective-permute-start(bf16[32,8192]{1,0:T(8,128)(2,1)S(1)} %copy-done.6), channel_id=1, source_target_pairs={{0,2},{2,0},{1,3},{3,1},{4,6},{6,4},{5,7},{7,5},{8,10},{10,8},{9,1... | collective-permute-start | bytes 1572872 | tf_op jit(solution)/shard_map/ppermute | solution.py:355
  105.0 3.2 %collective-permute-start.20 = (bf16[32,8192]{1,0:T(8,128)(2,1)}, bf16[32,8192]{1,0:T(8,128)(2,1)S(1)}, u32[]{:S(2)}, u32[]{:S(2)}) collective-permute-start(bf16[32,8192]{1,0:T(8,128)(2,1)} %get-tuple-element.92.refs_1_), channel_id=1, source_target_pairs={{0,2},{2,0},{1,3},{3,1},{4,6},{6,4},{5,7},{7,5},{8,10},{10,8},{9,1... | collective-permute-start | bytes 1572872 | tf_op jit(solution)/shard_map/ppermute | solution.py:355
  105.5 2.9 %collective-permute-start.21 = (bf16[32,8192]{1,0:T(8,128)(2,1)S(1)}, bf16[32,8192]{1,0:T(8,128)(2,1)S(1)}, u32[]{:S(2)}, u32[]{:S(2)}) collective-permute-start(bf16[32,8192]{1,0:T(8,128)(2,1)S(1)} %copy-done.8), channel_id=1, source_target_pairs={{0,2},{2,0},{1,3},{3,1},{4,6},{6,4},{5,7},{7,5},{8,10},{10,8},{9,1... | collective-permute-start | bytes 1572872 | tf_op jit(solution)/shard_map/ppermute | solution.py:355
  105.5 3.6 %collective-permute-start.22 = (bf16[32,8192]{1,0:T(8,128)(2,1)S(1)}, bf16[32,8192]{1,0:T(8,128)(2,1)S(1)}, u32[]{:S(2)}, u32[]{:S(2)}) collective-permute-start(bf16[32,8192]{1,0:T(8,128)(2,1)S(1)} %copy-done.10), channel_id=1, source_target_pairs={{0,2},{2,0},{1,3},{3,1},{4,6},{6,4},{5,7},{7,5},{8,10},{10,8},{9,1... | collective-permute-start | bytes 1572872 | tf_op jit(solution)/shard_map/ppermute | solution.py:355
  (16 other events, 70.5 us)
